TPU v7x, 128 devices: a whole 4x4x4 slice. The times are simulated.
128 devices in a mesh: row: 64 (over z, y, x_hi, core), col: 2 (over x_lo).
Axes of the slice: x: 4 (x_hi: 2, x_lo: 2; x = x_hi * 2 + x_lo), y: 4, z: 4, core: 2. Of those that a mesh axis runs over, the one named last changes fastest.
Arguments:
- current: bfloat16 [2, 256, 512, 256], P(None, None, 'row', 'col'), may hold values from -6 to 6
- previous: bfloat16 [2, 256, 512, 256], P(None, None, 'row', 'col'), may hold values from -6 to 6
- shift: int32 [2, 2], replicated, may hold values from -4 to 4, as said below
- weight: bfloat16 [128, 81], replicated, may hold values from -0.625 to 0.625
- cotangent: bfloat16 [2, 128, 512, 256], P(None, None, 'row', 'col'), may hold values from -6 to 6
Outputs:
- grad_current: bfloat16 [2, 256, 512, 256], P(None, None, 'row', 'col')
- grad_previous: bfloat16 [2, 256, 512, 256], P(None, None, 'row', 'col')
- grad_weight: float32 [128, 81], replicated
Inputs may be any that keep to these rules, and one draw needn't show every extreme that they name: `shift`: in every draw the row offset of the first pair and the column offset of the last pair are 4 and -4 in some order.
All inputs are finite; a program needn't handle non-finite values.
Results may differ from a plain program's by a relative error of at most 0.005.
Values may be sent and summed in bfloat16 or wider, within the bound.
A program may use at most 320 MiB of HBM per device.

v0:
```python
import math

import jax
import jax.numpy as jnp
from jax import lax
from jax.sharding import PartitionSpec as P


def with_halo(x, sides, width):
    for axis, dim in sides:
        size, length = (lax.axis_size(axis), x.shape[dim])
        up = [(i, (i + 1) % size) for i in range(size - 1)]
        down = [(j, i) for i, j in up]
        last = lax.slice_in_dim(x, length - width, length, axis=dim)
        initial = lax.slice_in_dim(x, 0, width, axis=dim)
        before = lax.ppermute(last, axis, up)
        after = lax.ppermute(initial, axis, down)
        x = jnp.concatenate([before, x, after], axis=dim)
    return x


def spread_terms(cur_ext, grad_ext, start_row, start_col, rows, cols):
    channels = cur_ext.shape[0]
    zero = jnp.int32(0)
    win_cur = lax.dynamic_slice(
        cur_ext, (zero, start_row, start_col), (channels, rows + 8, cols + 8)
    )
    win_grad = lax.dynamic_slice(
        grad_ext, (zero, start_row, start_col), (grad_ext.shape[0], rows + 8, cols + 8)
    )
    cur_stack = jnp.stack([win_cur[:, :, 8 - b : 8 - b + cols] for b in range(9)])
    total = jnp.zeros((channels, rows, cols), jnp.float32)
    for first in range(9):
        grad_part = jnp.stack(
            [
                win_grad[9 * first + b, 8 - first : 8 - first + rows, 8 - b : 8 - b + cols]
                for b in range(9)
            ]
        )
        total = total + jnp.einsum(
            "vyx,vcyx->cyx",
            grad_part,
            cur_stack[:, :, 8 - first : 8 - first + rows],
            preferred_element_type=jnp.float32,
        )
    return total


def local(current, previous, shift, weight, cotangent):
    pairs, channels, rows, cols = current.shape
    scale = 1.0 / math.sqrt(channels)
    zero = jnp.int32(0)
    prev_ext = with_halo(previous, (("row", 2), ("col", 3)), 8)
    weight_acc = jnp.zeros((weight.shape[0], weight.shape[1]), jnp.float32)
    grads_cur = []
    grads_prev = []
    for pair in range(pairs):
        row_off = shift[pair, 0]
        col_off = shift[pair, 1]
        window = lax.dynamic_slice(
            prev_ext[pair], (zero, 4 + row_off, 4 + col_off), (channels, rows + 8, cols + 8)
        )
        prev_stack = jnp.stack([window[:, :, b : b + cols] for b in range(9)])
        cur_pair = current[pair]
        volume = (
            jnp.concatenate(
                [
                    jnp.einsum(
                        "cyx,vcyx->vyx",
                        cur_pair,
                        prev_stack[:, :, a : a + rows],
                        preferred_element_type=jnp.float32,
                    )
                    for a in range(9)
                ],
                axis=0,
            )
            * scale
        )
        activated = jax.nn.silu(volume).astype(jnp.bfloat16)
        cot_pair = cotangent[pair]
        weight_term = jnp.einsum(
            "oyx,dyx->od", cot_pair, activated, preferred_element_type=jnp.float32
        )
        weight_acc = weight_acc + lax.psum(weight_term, ("row", "col"))
        pre = jnp.einsum("od,oyx->dyx", weight, cot_pair, preferred_element_type=jnp.float32)
        sig = jax.nn.sigmoid(volume)
        grad_volume = (pre * sig * (1.0 + volume * (1.0 - sig)) * scale).astype(jnp.bfloat16)
        grad_cur = jnp.zeros((channels, rows, cols), jnp.float32)
        for first in range(9):
            grad_cur = grad_cur + jnp.einsum(
                "vyx,vcyx->cyx",
                grad_volume[9 * first : 9 * first + 9],
                prev_stack[:, :, first : first + rows],
                preferred_element_type=jnp.float32,
            )
        grads_cur.append(grad_cur.astype(jnp.bfloat16))
        joined = jnp.concatenate([cur_pair, grad_volume], axis=0)
        joined_ext = with_halo(joined, (("row", 1), ("col", 2)), 8)
        grad_prev = spread_terms(
            joined_ext[:channels], joined_ext[channels:], 4 - row_off, 4 - col_off, rows, cols
        )
        grads_prev.append(grad_prev.astype(jnp.bfloat16))
    cells = pairs * rows * lax.axis_size("row") * cols * lax.axis_size("col")
    grad_weight = weight_acc * (1.0 / math.sqrt(cells))
    return (jnp.stack(grads_cur), jnp.stack(grads_prev), grad_weight)


def solution(mesh):
    in_specs = (
        P(None, None, "row", "col"),
        P(None, None, "row", "col"),
        P(),
        P(),
        P(None, None, "row", "col"),
    )
    out_specs = (P(None, None, "row", "col"), P(None, None, "row", "col"), P())
    return jax.shard_map(local, mesh=mesh, in_specs=in_specs, out_specs=out_specs, check_vma=False)
```

profile of v0, /device:TPU:1, one launch (start us, length us, event | category | flops | bytes accessed | tf_op | source)
XLA Modules:
  0.0 501.2 jit_solution(17866688412914634469)
XLA Ops:
  5.7 4.6 collective-permute-start
  38.4 4.1 collective-permute-done.3
  48.6 11.7 %multiply_reduce_fusion.27 = (f32[8,128,9]{1,0,2:T(8,128)S(1)}, f32[8,128,9]{1,0,2:T(8,128)S(1)}, f32[8,128,9]{1,0,2:T(8,128)S(1)}, f32[8,128,9]{1,0,2:T(8,128)S...) fusion(f32[8,128,256]{2,1,0:T(8,128)S(1)} %copy-done.16, ...), kind=kLoop, calls=%fused_computation.27 | loop fusion | flops 63618048 | bytes 43847680
  71.8 5.0 collective-permute-start.8
  79.6 11.7 %multiply_reduce_fusion.45 = (f32[8,128,9]{1,0,2:T(8,128)S(1)}, f32[8,128,9]{1,0,2:T(8,128)S(1)}, f32[8,128,9]{1,0,2:T(8,128)S(1)}, f32[8,128,9]{1,0,2:T(8,128)S...) fusion(f32[8,128,256]{2,1,0:T(8,128)S(1)} %copy-done.15, ...), kind=kLoop, calls=%fused_computation.45 | loop fusion | flops 63618048 | bytes 43847680
  96.5 5.1 %collective-permute-start.4 = (bf16[337,8,128]{2,1,0:T(8,128)(2,1)}, bf16[337,8,128]{2,1,0:T(8,128)(2,1)S(1)}, u32[]{:S(2)}, u32[]{:S(2)}) collective-permute-start(bf16[337,8,128]{2,1,0:T(8,128)(2,1)} %pad_maximum_fusion.7), channel_id=1, source_target_pairs={{0,2},{2,4},{4,6},{6,8},{8,10},{10,12},{12,14},{14,16},{16,18},{18... | collective-permute-start | bytes 2070536 | tf_op jit(solution)/shard_map/ppermute | solution.py:16
  109.5 24.3 %multiply_reduce_fusion.25 = (f32[8,128,256]{2,1,0:T(8,128)}, f32[8,128,256]{2,1,0:T(8,128)}, f32[8,128,256]{2,1,0:T(8,128)}, f32[8,128,256]{2,1,0:T(8,128)}, f3...) fusion(f32[8,128,9]{1,0,2:T(8,128)} %copy.464, ...), kind=kLoop, calls=%fused_computation.25 | loop fusion | flops 61341696 | bytes 52236288
  158.1 76.4 %psum.16 = f32[128,81]{0,1:T(8,128)S(1)} all-reduce(f32[128,81]{0,1:T(8,128)S(1)} %fusion.7), channel_id=1, replica_groups=mesh['row'=64,'col'=2] {'row','col'}, use_global_device_ids=true, to_apply=%region_0.1 | all-reduce | flops 10368 | bytes 82944 | tf_op jit(solution)/shard_map/psum | solution.py:85
  238.0 4.9 fusion.55
  242.9 23.5 %multiply_reduce_fusion.43 = (f32[8,128,256]{2,1,0:T(8,128)}, f32[8,128,256]{2,1,0:T(8,128)}, f32[8,128,256]{2,1,0:T(8,128)}, f32[8,128,256]{2,1,0:T(8,128)}, f3...) fusion(f32[8,128,9]{1,0,2:T(8,128)S(1)} %copy.454, ...), kind=kLoop, calls=%fused_computation.43 | loop fusion | flops 61341696 | bytes 52236288
  290.1 4.1 fusion.54
  300.9 4.1 copy.32
  305.0 4.1 copy.33
  310.4 5.5 %collective-permute-start.10 = (bf16[337,24,8]{0,2,1:T(8,128)(2,1)}, bf16[337,24,8]{0,2,1:T(8,128)(2,1)}, u32[]{:S(2)}, u32[]{:S(2)}) collective-permute-start(bf16[337,24,8]{0,2,1:T(8,128)(2,1)} %copy.32), channel_id=1, source_target_pairs={{0,1},{2,3},{4,5},{6,7},{8,9},{10,11},{12,13},{14,15},{16,17},{18,... | collective-permute-start | bytes 388232 | tf_op jit(solution)/shard_map/ppermute | solution.py:16
  319.4 4.1 copy.27
  328.0 5.3 %collective-permute-start.6 = (bf16[337,24,8]{0,2,1:T(8,128)(2,1)}, bf16[337,24,8]{0,2,1:T(8,128)(2,1)}, u32[]{:S(2)}, u32[]{:S(2)}) collective-permute-start(bf16[337,24,8]{0,2,1:T(8,128)(2,1)} %copy.27), channel_id=1, source_target_pairs={{0,1},{2,3},{4,5},{6,7},{8,9},{10,11},{12,13},{14,15},{16,17},{18,... | collective-permute-start | bytes 388232 | tf_op jit(solution)/shard_map/ppermute | solution.py:16
  337.3 4.5 copy.35
  341.8 7.3 %pad_maximum_fusion.1 = bf16[337,24,144]{2,1,0:T(8,128)(2,1)S(1)} fusion(bf16[337,24,8]{2,1,0:T(8,128)(2,1)} %copy.35, bf16[337,8,128]{2,1,0:T(8,128)(2,1)} %collective-permute-done.9, bf16[81,8,128]{2,1,0:T(8,128)(2,1)} %copy-done.17, bf16[256,8,128]{2,1,0:T(8,128)(2,1)S(1)} %get-tuple-element.68, bf16[337,8,128]{2,1,0:T(8,128)(2,1)} %collective-permute-done.8, ...), kind=kLoop, calls=%fused_computation.73 | loop fusion | flops 13976064 | bytes 4658688 | tf_op jit(solution)/shard_map/concatenate | solution.py:18
  381.4 4.6 copy.29
  388.1 4.6 copy.30
  392.7 7.5 %pad_maximum_fusion = bf16[337,24,144]{2,1,0:T(8,128)(2,1)S(1)} fusion(bf16[337,24,8]{2,1,0:T(8,128)(2,1)} %copy.30, bf16[337,8,128]{2,1,0:T(8,128)(2,1)} %copy-done.11, bf16[81,8,128]{2,1,0:T(8,128)(2,1)S(1)} %copy.26, bf16[256,8,128]{2,1,0:T(8,128)(2,1)} %copy-done.8, bf16[337,8,128]{2,1,0:T(8,128)(2,1)} %copy-done.13, bf16[337,24,8]{2,1,0:T(8,128)(2,1)} %copy.29), kind=kLoop, calls=%fused_computation.72 | loop fusion | flops 13976064 | bytes 4658688 | tf_op jit(solution)/shard_map/concatenate | solution.py:18
  427.5 32.1 %multiply_reduce_fusion.7 = (f32[8,128,256]{1,0,2:T(8,128)S(1)}, f32[8,128,256]{1,0,2:T(8,128)S(1)}, f32[8,128,256]{1,0,2:T(8,128)S(1)}, f32[8,128,256]{1,0,2:T(...) fusion(bf16[9,256,16,128]{3,2,1,0:T(8,128)(2,1)} %fusion.8, ...), kind=kLoop, calls=%fused_computation.7 | loop fusion | flops 61341696 | bytes 52236288 | tf_op jit(solution)/shard_map/vyx,vcyx->cyx/dot_general | solution.py:40
  459.6 4.2 fusion.57
  463.9 32.5 %multiply_reduce_fusion.16 = (f32[8,128,256]{1,0,2:T(8,128)S(1)}, f32[8,128,256]{1,0,2:T(8,128)S(1)}, f32[8,128,256]{1,0,2:T(8,128)S(1)}, f32[8,128,256]{1,0,2:T...) fusion(bf16[9,256,16,128]{3,2,1,0:T(8,128)(2,1)} %fusion.17, ...), kind=kLoop, calls=%fused_computation.16 | loop fusion | flops 61341696 | bytes 52236288 | tf_op jit(solution)/shard_map/vyx,vcyx->cyx/dot_general | solution.py:40
  (270 shorter events, 192.9 us)
Async XLA Ops:
  0.6 66.0 %copy-start = (bf16[128,81]{0,1:T(8,128)(2,1)S(1)}, bf16[128,81]{0,1:T(8,128)(2,1)}, u32[]{:S(2)}) copy-start(bf16[128,81]{0,1:T(8,128)(2,1)} %param.8) | copy-start | bytes 62212
  0.6 35.0 %copy-start.21 = (bf16[2,128,8,128]{3,2,1,0:T(8,128)(2,1)S(1)}, bf16[2,128,8,128]{3,2,1,0:T(8,128)(2,1)}, u32[]{:S(2)}) copy-start(bf16[2,128,8,128]{3,2,1,0:T(8,128)(2,1)} %param.9) | copy-start | bytes 1572868
  2.4 27.9 %collective-permute-start.1 = (bf16[2,256,8,128]{1,3,2,0:T(8,128)(2,1)S(1)}, bf16[2,256,8,128]{1,3,2,0:T(8,128)(2,1)}, u32[]{:S(2)}, u32[]{:S(2)}) collective-permute-start(bf16[2,256,8,128]{1,3,2,0:T(8,128)(2,1)S(1)} %copy.21), channel_id=1, source_target_pairs={{2,0},{4,2},{6,4},{8,6},{10,8},{12,10},{14,12},{16,14},{18,16},{20... | collective-permute-start | bytes 3145736 | tf_op jit(solution)/shard_map/ppermute | solution.py:17
  5.7 24.6 %collective-permute-start = (bf16[2,256,8,128]{1,3,2,0:T(8,128)(2,1)S(1)}, bf16[2,256,8,128]{1,3,2,0:T(8,128)(2,1)}, u32[]{:S(2)}, u32[]{:S(2)}) collective-permute-start(bf16[2,256,8,128]{1,3,2,0:T(8,128)(2,1)S(1)} %copy.21), channel_id=1, source_target_pairs={{0,2},{2,4},{4,6},{6,8},{8,10},{10,12},{12,14},{14,16},{16,18},{18... | collective-permute-start | bytes 3145736 | tf_op jit(solution)/shard_map/ppermute | solution.py:16
  24.8 291.1 %copy-start.8 = (bf16[256,8,128]{2,1,0:T(8,128)(2,1)}, bf16[256,8,128]{2,1,0:T(8,128)(2,1)S(1)}, u32[]{:S(2)}) copy-start(bf16[256,8,128]{2,1,0:T(8,128)(2,1)S(1)} %get-tuple-element.65) | copy-start | bytes 1572868
  24.8 317.0 %copy-start.10 = (bf16[256,8,128]{2,1,0:T(8,128)(2,1)}, bf16[256,8,128]{2,1,0:T(8,128)(2,1)S(1)}, u32[]{:S(2)}) copy-start(bf16[256,8,128]{2,1,0:T(8,128)(2,1)S(1)} %get-tuple-element.68) | copy-start | bytes 1572868
  31.2 7.2 %collective-permute-start.2 = (bf16[2,256,24,8]{1,3,2,0:T(8,128)(2,1)S(1)}, bf16[2,256,24,8]{1,3,2,0:T(8,128)(2,1)S(1)}, u32[]{:S(2)}, u32[]{:S(2)}) collective-permute-start(bf16[2,256,24,8]{1,3,2,0:T(8,128)(2,1)S(1)} %get-tuple-element.59), channel_id=1, source_target_pairs={{0,1},{2,3},{4,5},{6,7},{8,9},{10,11},{12,13},{14,15},{16,17},{18,... | collective-permute-start | bytes 589832 | tf_op jit(solution)/shard_map/ppermute | solution.py:16
  34.3 8.2 %collective-permute-start.3 = (bf16[2,256,24,8]{1,3,2,0:T(8,128)(2,1)S(1)}, bf16[2,256,24,8]{1,3,2,0:T(8,128)(2,1)S(1)}, u32[]{:S(2)}, u32[]{:S(2)}) collective-permute-start(bf16[2,256,24,8]{1,3,2,0:T(8,128)(2,1)S(1)} %get-tuple-element.60), channel_id=1, source_target_pairs={{1,0},{3,2},{5,4},{7,6},{9,8},{11,10},{13,12},{15,14},{17,16},{19,... | collective-permute-start | bytes 589832 | tf_op jit(solution)/shard_map/ppermute | solution.py:17
  35.7 56.8 %copy-start.27 = (bf16[1,128,8,128]{3,2,1,0:T(8,128)(2,1)}, bf16[1,128,8,128]{3,2,1,0:T(8,128)(2,1)S(1)}, u32[]{:S(2)}) copy-start(bf16[1,128,8,128]{3,2,1,0:T(8,128)(2,1)S(1)} %get-tuple-element.229) | copy-start | bytes 786436
  67.8 228.5 %copy-start.17 = (bf16[81,8,128]{2,1,0:T(8,128)(2,1)}, bf16[81,8,128]{2,1,0:T(8,128)(2,1)S(1)}, u32[]{:S(2)}) copy-start(bf16[81,8,128]{2,1,0:T(8,128)(2,1)S(1)} %copy.31) | copy-start | bytes 497668
  69.6 226.7 %collective-permute-start.9 = (bf16[337,8,128]{2,1,0:T(8,128)(2,1)}, bf16[337,8,128]{2,1,0:T(8,128)(2,1)}, u32[]{:S(2)}, u32[]{:S(2)}) collective-permute-start(bf16[337,8,128]{2,1,0:T(8,128)(2,1)} %pad_maximum_fusion.8), channel_id=1, source_target_pairs={{2,0},{4,2},{6,4},{8,6},{10,8},{12,10},{14,12},{16,14},{18,16},{20... | collective-permute-start | bytes 2070536 | tf_op jit(solution)/shard_map/ppermute | solution.py:17
  71.8 224.4 %collective-permute-start.8 = (bf16[337,8,128]{2,1,0:T(8,128)(2,1)}, bf16[337,8,128]{2,1,0:T(8,128)(2,1)}, u32[]{:S(2)}, u32[]{:S(2)}) collective-permute-start(bf16[337,8,128]{2,1,0:T(8,128)(2,1)} %pad_maximum_fusion.8), channel_id=1, source_target_pairs={{0,2},{2,4},{4,6},{6,8},{8,10},{10,12},{12,14},{14,16},{16,18},{18... | collective-permute-start | bytes 2070536 | tf_op jit(solution)/shard_map/ppermute | solution.py:16
  94.5 221.3 %collective-permute-start.5 = (bf16[337,8,128]{2,1,0:T(8,128)(2,1)}, bf16[337,8,128]{2,1,0:T(8,128)(2,1)S(1)}, u32[]{:S(2)}, u32[]{:S(2)}) collective-permute-start(bf16[337,8,128]{2,1,0:T(8,128)(2,1)} %pad_maximum_fusion.7), channel_id=1, source_target_pairs={{2,0},{4,2},{6,4},{8,6},{10,8},{12,10},{14,12},{16,14},{18,16},{20... | collective-permute-start | bytes 2070536 | tf_op jit(solution)/shard_map/ppermute | solution.py:17
  96.5 219.5 %collective-permute-start.4 = (bf16[337,8,128]{2,1,0:T(8,128)(2,1)}, bf16[337,8,128]{2,1,0:T(8,128)(2,1)S(1)}, u32[]{:S(2)}, u32[]{:S(2)}) collective-permute-start(bf16[337,8,128]{2,1,0:T(8,128)(2,1)} %pad_maximum_fusion.7), channel_id=1, source_target_pairs={{0,2},{2,4},{4,6},{6,8},{8,10},{10,12},{12,14},{14,16},{16,18},{18... | collective-permute-start | bytes 2070536 | tf_op jit(solution)/shard_map/ppermute | solution.py:16
  136.4 101.5 %copy-start.26 = (f32[8,128,9]{1,2,0:T(8,128)S(1)}, f32[8,128,9]{1,2,0:T(8,128)}, u32[]{:S(2)}) copy-start(f32[8,128,9]{1,2,0:T(8,128)} %get-tuple-element.235) | copy-start | bytes 110596
  136.4 101.5 %copy-start.25 = (f32[8,128,9]{1,2,0:T(8,128)S(1)}, f32[8,128,9]{1,2,0:T(8,128)}, u32[]{:S(2)}) copy-start(f32[8,128,9]{1,2,0:T(8,128)} %get-tuple-element.236) | copy-start | bytes 110596
  136.4 101.6 %copy-start.24 = (f32[8,128,9]{1,2,0:T(8,128)S(1)}, f32[8,128,9]{1,2,0:T(8,128)}, u32[]{:S(2)}) copy-start(f32[8,128,9]{1,2,0:T(8,128)} %get-tuple-element.237) | copy-start | bytes 110596
  136.4 101.6 %copy-start.23 = (f32[8,128,9]{1,2,0:T(8,128)S(1)}, f32[8,128,9]{1,2,0:T(8,128)}, u32[]{:S(2)}) copy-start(f32[8,128,9]{1,2,0:T(8,128)} %get-tuple-element.238) | copy-start | bytes 110596
  136.4 101.6 %copy-start.22 = (f32[8,128,9]{1,2,0:T(8,128)S(1)}, f32[8,128,9]{1,2,0:T(8,128)}, u32[]{:S(2)}) copy-start(f32[8,128,9]{1,2,0:T(8,128)} %get-tuple-element.239) | copy-start | bytes 110596
  309.1 28.1 %collective-permute-start.11 = (bf16[337,24,8]{0,2,1:T(8,128)(2,1)}, bf16[337,24,8]{0,2,1:T(8,128)(2,1)}, u32[]{:S(2)}, u32[]{:S(2)}) collective-permute-start(bf16[337,24,8]{0,2,1:T(8,128)(2,1)} %copy.33), channel_id=1, source_target_pairs={{1,0},{3,2},{5,4},{7,6},{9,8},{11,10},{13,12},{15,14},{17,16},{19,... | collective-permute-start | bytes 388232 | tf_op jit(solution)/shard_map/ppermute | solution.py:17
  310.4 22.9 %collective-permute-start.10 = (bf16[337,24,8]{0,2,1:T(8,128)(2,1)}, bf16[337,24,8]{0,2,1:T(8,128)(2,1)}, u32[]{:S(2)}, u32[]{:S(2)}) collective-permute-start(bf16[337,24,8]{0,2,1:T(8,128)(2,1)} %copy.32), channel_id=1, source_target_pairs={{0,1},{2,3},{4,5},{6,7},{8,9},{10,11},{12,13},{14,15},{16,17},{18,... | collective-permute-start | bytes 388232 | tf_op jit(solution)/shard_map/ppermute | solution.py:16
  326.7 61.4 %collective-permute-start.7 = (bf16[337,24,8]{0,2,1:T(8,128)(2,1)}, bf16[337,24,8]{0,2,1:T(8,128)(2,1)}, u32[]{:S(2)}, u32[]{:S(2)}) collective-permute-start(bf16[337,24,8]{0,2,1:T(8,128)(2,1)} %copy.28), channel_id=1, source_target_pairs={{1,0},{3,2},{5,4},{7,6},{9,8},{11,10},{13,12},{15,14},{17,16},{19,... | collective-permute-start | bytes 388232 | tf_op jit(solution)/shard_map/ppermute | solution.py:17
  328.0 53.4 %collective-permute-start.6 = (bf16[337,24,8]{0,2,1:T(8,128)(2,1)}, bf16[337,24,8]{0,2,1:T(8,128)(2,1)}, u32[]{:S(2)}, u32[]{:S(2)}) collective-permute-start(bf16[337,24,8]{0,2,1:T(8,128)(2,1)} %copy.27), channel_id=1, source_target_pairs={{0,1},{2,3},{4,5},{6,7},{8,9},{10,11},{12,13},{14,15},{16,17},{18,... | collective-permute-start | bytes 388232 | tf_op jit(solution)/shard_map/ppermute | solution.py:16
  463.8 37.0 %copy-start.1 = (bf16[128,81]{0,1:T(8,128)(2,1)S(1)}, bf16[128,81]{0,1:T(8,128)(2,1)}, u32[]{:S(2)}) copy-start(bf16[128,81]{0,1:T(8,128)(2,1)} %param.8) | copy-start | bytes 62212
  (32 other events, 324.4 us)
where the time goes:
time: 511 us; the launch traced here: 501 us
  other arithmetic  197 us (39%)
  local copies, waits for them, and re-layouts  165 us (32%)
  blocking collectives  76.4 us (15%)
  starting transfers between devices  40 us (8%)
  between operations  12.4 us (2%)
  waiting for transfers between devices  6.87 us (1%)
    unnamed x24, other arithmetic  82.2 us
    psum x1, blocking collectives, local(): weight_acc = weight_acc + lax.psum(weight_term, ('row', 'col'))  76.4 us
    unnamed x157, local copies, waits for them, and re-layouts  65 us
    dot_general x2, other arithmetic, spread_terms(): jnp.einsum('vyx,vcyx->cyx', grad_part, cur_stack[:, :, 8 - first:8 - firs...  64.5 us
    dot_general x18, local copies, waits for them, and re-layouts, local(): jnp.einsum('vyx,vcyx->cyx', grad_volume[9 * first:9 * first + 9], prev_st...  46 us
    ppermute x6, starting transfers between devices, with_halo(): before = lax.ppermute(last, axis, up)  28.6 us
    another operation x6, other arithmetic, local(): return (jnp.stack(grads_cur), jnp.stack(grads_prev), grad_weight)  19.8 us
    concatenate x5, other arithmetic, with_halo(): x = jnp.concatenate([before, x, after], axis=dim)  18.6 us
  transfers between devices with their start and end apart: 12, of which 2 were waited for; matrix products, arithmetic and copies ran while one was open for 44% of the time, Pallas kernels for 0%

commit v1 on v0

v1 whole, which is shorter than its diff:
```python
import math

import jax
import jax.numpy as jnp
import numpy as np
from jax import lax
from jax.experimental import pallas as pl
from jax.experimental.pallas import tpu as pltpu
from jax.sharding import PartitionSpec as P

BF = jnp.bfloat16
F32 = jnp.float32
MESH = pl.DeviceIdType.MESH
NT = (((1,), (1,)), ((), ()))
TN = (((0,), (0,)), ((), ()))
NN = (((1,), (0,)), ((), ()))
WIDE = 144


def dot(a, b, dims=NN):
    return lax.dot_general(a, b, dims, preferred_element_type=F32)


def iota(shape, axis):
    return lax.broadcasted_iota(jnp.int32, shape, axis)


def skew(x, shift):
    return pltpu.roll(x, shift % 256, 1, stride=1, stride_axis=0)


def flip8(x):
    idx = 7 - iota((8, 128), 0)
    parts = [
        jnp.take_along_axis(x[:, at : at + 128], idx, axis=0) for at in range(0, x.shape[1], 128)
    ]
    return parts[0] if len(parts) == 1 else jnp.concatenate(parts, axis=1)


def activation(vol_dot):
    half = vol_dot * (1.0 / 32.0)
    q = 1.0 + jnp.tanh(half)
    act = half * q
    return act, q + act * (2.0 - q)


def cell_part(p, bb, dy, win_ref, cur_ref, cot_ref, wk, out_ref, acc_ref):
    at = pl.multiple_of(bb * 16, 16)
    cur = cur_ref[p, :, pl.ds(at, 16), :].reshape(128, 256)
    cot = cot_ref[p, :, pl.ds(at, 16), :].reshape(128, 128)
    win = win_ref[pl.ds(4 + dy, 16), pl.ds(at, 32), :]
    win_e = win[:, 0:16].reshape(256, 256)
    win_o = win[:, 8:24].reshape(256, 256)
    vol_e = dot(cur, win_e, NT)
    vol_o = dot(cur, win_o, NT)
    pre = dot(cot, wk)
    cot_rev = cot.astype(F32)
    cot_rev = jnp.concatenate([flip8(cot_rev[8 * i : 8 * i + 8]) for i in range(16)], axis=0)
    acts, grads = [], []
    for i in range(16):
        y, odd = divmod(i, 2)
        rows = slice(8 * i, 8 * i + 8)
        act, slope = activation((vol_o if odd else vol_e)[rows])
        grads.append(skew(pre[rows], 16 * y) * slope)
        acts.append(skew(flip8(act), 249 - 16 * y))
    act = jnp.concatenate(acts, axis=0).astype(BF)
    acc_ref[...] += dot(cot_rev.astype(BF), act, TN).reshape(8, 16, 256)
    out_e = dot(jnp.concatenate(grads[0::2], axis=0).astype(BF), win_e)
    out_o = dot(jnp.concatenate(grads[1::2], axis=0).astype(BF), win_o)
    outs = []
    for y in range(8):
        outs += [out_e[8 * y : 8 * y + 8], out_o[8 * y : 8 * y + 8]]
    out_ref[p, :, pl.ds(at, 16), :] = (
        jnp.concatenate(outs, axis=0).astype(BF).reshape(8, 16, 256)
    )


def position_part(p, bb, dy, win_ref, pre_ref, prev_ref, spread, masks, out_ref):
    at = pl.multiple_of(bb * 16, 16)
    prev = prev_ref[p, :, pl.ds(at, 16), :].reshape(128, 256)
    wins, pres = [], []
    for j in range(16):
        row = jnp.where(j < 4 + dy, j, jnp.where(j < 12 + dy, 20 + j - dy, 8 + j))
        wins.append(win_ref[row, pl.ds(at, 32), :][:24])
        pres.append(pre_ref[row, pl.ds(at, 32), :][:24])
    win = jnp.concatenate(wins, axis=0)
    vol = dot(win, prev, NT)
    pre = dot(jnp.concatenate(pres, axis=0), spread)
    grads = []
    for j in range(16):
        for g in range(3):
            rows = slice(24 * j + 8 * g, 24 * j + 8 * g + 8)
            piece = pre[rows]
            if g != 1:
                piece = piece * masks[g // 2]
            piece = skew(piece, 16 * (j - 8) + 8 * (g - 1))[:, :128]
            grads.append(piece * activation(vol[rows])[1])
    grad = jnp.concatenate(grads, axis=0).astype(BF)
    out_ref[p, :, pl.ds(at, 16), :] = dot(grad, win, TN).astype(BF).reshape(8, 16, 256)


def kernel(
    shift_ref, prev_ref, cur_ref, cot_ref, w_ref, e_ref,
    gc_ref, gp_ref, gw_ref,
    edge_s, edge_r, edge_cot_s, edge_cot_r, own, own_cot, own_pre, msg, tri_s, tri_r,
    win0, win1, pre0, pre1, acc, ar1, ar2, ar3,
    side_ss, side_rs, row_ss, row_rs, s1, r1, s2, r2, s3, r3,
):
    row, col = lax.axis_index("row"), lax.axis_index("col")
    last = lax.axis_size("row") - 1
    left = col == 0
    wins, pres = (win0, win1), (pre0, pre1)
    g1, g2 = (row % 4) * 2 + col, row // 4

    def member(a, b):
        return (b * 4 + a // 2, a % 2)

    barrier = pltpu.get_barrier_semaphore()

    def greet(target):
        pl.semaphore_signal(barrier, inc=1, device_id=target, device_id_type=MESH)

    for d in range(1, 8):
        greet(member((g1 + d) % 8, g2))
    for d in range(1, 16):
        greet(member(g1, (g2 + d) % 16))
    greet(((row + 1) % (last + 1), col))
    greet(((row + last) % (last + 1), col))
    pl.semaphore_wait(barrier, 24)

    def side(p, k):
        s, r = ((edge_s, edge_r), (edge_cot_s, edge_cot_r))[k]
        return pltpu.make_async_remote_copy(
            src_ref=s.at[p], dst_ref=r.at[p], send_sem=side_ss.at[p, k],
            recv_sem=side_rs.at[p, k], device_id=(row, 1 - col), device_id_type=MESH,
        )

    def along(p, way, k):
        if k == 0:
            src, dst = msg.at[p, way], wins[p].at[pl.ds(0 if way else 16, 8)]
        else:
            src, dst = tri_s.at[p, way], tri_r.at[p, way]
        target = jnp.where(row == last, row, row + 1) if way else jnp.where(row == 0, row, row - 1)
        return pltpu.make_async_remote_copy(
            src_ref=src, dst_ref=dst, send_sem=row_ss.at[p, way, k],
            recv_sem=row_rs.at[p, way, k], device_id=(target, col), device_id_type=MESH,
        )

    start = jnp.where(left, 112, 0)
    for p in range(2):
        for y in range(8):
            pick = []
            for ref in (prev_ref, cur_ref):
                tile = ref[p, y, pl.ds(pl.multiple_of(start, 16), 16), :].astype(F32)
                pick.append(jnp.where(left, tile[8:], tile[:8]))
            edge_s[p, y] = jnp.concatenate(pick, axis=0).astype(BF)
        for y in range(0, 8, 2):
            pick = []
            for yy in (y, y + 1):
                tile = cot_ref[p, yy, pl.ds(pl.multiple_of(start, 16), 16), :].astype(F32)
                pick.append(jnp.where(left, tile[8:], tile[:8]))
            edge_cot_s[p, y // 2] = jnp.concatenate(pick, axis=0).astype(BF)
        side(p, 0).start()
        side(p, 1).start()

    w9 = w_ref[...]
    e = e_ref[...]
    wk = dot(w9, e).astype(BF)
    spread = jnp.concatenate([wk, e], axis=0)
    sub, lane = iota((8, 256), 0), iota((8, 256), 1) % 16
    masks = (jnp.where(lane >= 8 - sub, 1.0, 0.0), jnp.where(lane < 8 - sub, 1.0, 0.0))
    out_at, in_at = iota((WIDE, WIDE), 0), iota((WIDE, WIDE), 1)
    far = jnp.where(left, 136, 0)
    tri_lane = iota((WIDE, 128), 1)

    def aligner(offset, slots):
        at = jnp.where(in_at < 128, in_at + 8, in_at - 128 - slots + far)
        ok = (in_at < 128) | ((in_at >= 128 + slots) & (in_at < 136 + slots))
        return jnp.where(ok & (at == out_at + offset), 1.0, 0.0).astype(BF)

    for p in range(2):
        dy, dx = shift_ref[p, 0], shift_ref[p, 1]
        win, pre = wins[p], pres[p]
        align_p, align_c0, align_c1 = aligner(4 + dx, 0), aligner(4 - dx, 0), aligner(4 - dx, 8)
        for k in range(2):
            side(p, k).wait()
        for y in range(8):
            edge = edge_r[p, y]
            aligned = dot(align_p, jnp.concatenate([prev_ref[p, y], edge], axis=0)).astype(BF)
            own[y] = aligned
            win[8 + y] = aligned
            aligned = dot(align_c1, jnp.concatenate([cur_ref[p, y], edge], axis=0)).astype(BF)
            own[8 + y] = aligned
            win[24 + y] = aligned
            align = align_c1 if y % 2 else align_c0
            both = jnp.concatenate([cot_ref[p, y], edge_cot_r[p, y // 2]], axis=0)
            aligned = dot(align, both).astype(BF)
            pre[24 + y] = jnp.concatenate([aligned, jnp.zeros_like(aligned)], axis=1)
            own_pre[y] = dot(aligned, w9)

        def pack(s, carry):
            msg[p, 0, s] = own[jnp.where(s < 4 + dy, s, 4 + s - dy)]
            msg[p, 1, s] = own[jnp.where(s < 4 + dy, 12 + s - dy, s)]
            return carry

        lax.fori_loop(0, 8, pack, 0)

        def cell_row(t):
            return own_pre[jnp.where(t < 4 + dy, t + 4 - dy, t - 4 - dy)]

        for s in range(4):
            near, away = cell_row(s), cell_row(7 - s)
            tri_s[p, 1, s] = jnp.where(
                tri_lane >= 9 * (8 - s), near, pltpu.roll(away, 128 - 9 * (s + 1), 1)
            ).astype(BF)
            tri_s[p, 0, s] = jnp.where(
                tri_lane < 9 * (8 - s), near, pltpu.roll(away, 9 * (8 - s), 1)
            ).astype(BF)

        @pl.when(row > 0)
        def _():
            for k in range(2):
                along(p, 0, k).start()

        @pl.when(row < last)
        def _():
            for k in range(2):
                along(p, 1, k).start()

    acc[...] = jnp.zeros_like(acc)

    def arrive(p):
        win, pre = wins[p], pres[p]

        @pl.when(row > 0)
        def _():
            for k in range(2):
                along(p, 1, k).wait_recv()

        @pl.when(row == 0)
        def _():
            win[0:8] = jnp.zeros((8, WIDE, 256), BF)
            tri_r[p, 1] = jnp.zeros((4, WIDE, 128), BF)

        @pl.when(row < last)
        def _():
            for k in range(2):
                along(p, 0, k).wait_recv()

        @pl.when(row == last)
        def _():
            win[16:24] = jnp.zeros((8, WIDE, 256), BF)
            tri_r[p, 0] = jnp.zeros((4, WIDE, 128), BF)

        zero = jnp.zeros((WIDE, 128), BF)
        for s in range(4):
            got = tri_r[p, 1, s]
            pre[s] = jnp.concatenate([zero, got], axis=1)
            got = pltpu.roll(got.astype(F32), 9 * (s + 1), 1).astype(BF)
            pre[7 - s] = jnp.concatenate([zero, got], axis=1)
            got = tri_r[p, 0, s]
            pre[16 + s] = jnp.concatenate([zero, got], axis=1)
            got = pltpu.roll(got.astype(F32), 128 - 9 * (8 - s), 1).astype(BF)
            pre[23 - s] = jnp.concatenate([zero, got], axis=1)

    def run_cells(p):
        def body(bb, carry):
            cell_part(p, bb, shift_ref[p, 0], wins[p], cur_ref, cot_ref, wk, gc_ref, acc)
            return carry

        lax.fori_loop(0, 8, body, 0)

    def run_positions(p, lo, hi):
        def body(bb, carry):
            position_part(
                p, bb, shift_ref[p, 0], wins[p], pres[p], prev_ref, spread, masks, gp_ref
            )
            return carry

        lax.fori_loop(lo, hi, body, 0)

    arrive(0)
    run_cells(0)
    run_positions(0, 0, 8)
    arrive(1)
    run_cells(1)

    def first(d):
        peer = (g1 + d) % 8
        return pltpu.make_async_remote_copy(
            src_ref=acc.at[peer], dst_ref=ar1.at[g1], send_sem=s1.at[peer],
            recv_sem=r1.at[g1], device_id=member(peer, g2), device_id_type=MESH,
        )

    def second(d):
        peer = (g2 + d) % 16
        return pltpu.make_async_remote_copy(
            src_ref=ar2.at[g2], dst_ref=ar2.at[g2], send_sem=s2.at[peer],
            recv_sem=r2.at[g2], device_id=member(g1, peer), device_id_type=MESH,
        )

    def third(d):
        peer = (g1 + d) % 8
        return pltpu.make_async_remote_copy(
            src_ref=ar3.at[g1], dst_ref=ar3.at[g1], send_sem=s3.at[peer],
            recv_sem=r3.at[g1], device_id=member(peer, g2), device_id_type=MESH,
        )

    def got(buffer, sends, receives, source):
        pltpu.make_async_remote_copy(
            src_ref=buffer.at[source], dst_ref=buffer.at[source], send_sem=sends.at[source],
            recv_sem=receives.at[source], device_id=(row, 1 - col), device_id_type=MESH,
        ).wait_recv()

    for d in range(1, 8):
        first(d).start()
    run_positions(1, 0, 3)
    ar1[g1] = acc[g1]
    for d in range(1, 8):
        first(d).wait_send()
        got(ar1, s1, r1, (g1 + d) % 8)
    ar2[g2] = jnp.sum(ar1[...], axis=0)
    for d in range(1, 16):
        second(d).start()
    run_positions(1, 3, 6)
    for d in range(1, 16):
        second(d).wait_send()
        got(ar2, s2, r2, (g2 + d) % 16)
    ar3[g1] = jnp.sum(ar2[...], axis=0)
    for d in range(1, 8):
        third(d).start()
    run_positions(1, 6, 8)
    for d in range(1, 8):
        third(d).wait_send()
        got(ar3, s3, r3, (g1 + d) % 8)
    gw_ref[...] = ar3[...]

    for p in range(2):
        for k in range(2):

            @pl.when(row > 0)
            def _():
                along(p, 0, k).wait_send()

            @pl.when(row < last)
            def _():
                along(p, 1, k).wait_send()


def spread_matrix():
    e = np.zeros((128, 256), np.float32)
    for u in range(9):
        for v in range(9):
            e[9 * u + v, 16 * u + v] = 1.0 / 32.0
    return e


def local(current, previous, shift, weight, cotangent):
    pairs, channels, rows, cols = current.shape
    prev = previous.transpose(0, 2, 3, 1)
    cur = current.transpose(0, 2, 3, 1)
    cot = cotangent.transpose(0, 2, 3, 1)
    w9 = jnp.pad(weight, ((0, 0), (0, 128 - 81)))
    e = jnp.asarray(spread_matrix(), BF)
    vmem = pl.BlockSpec(memory_space=pltpu.VMEM)
    dma = pltpu.SemaphoreType.DMA
    gc, gp, gw = pl.pallas_call(
        kernel,
        in_specs=[pl.BlockSpec(memory_space=pltpu.SMEM)] + [vmem] * 5,
        out_specs=[vmem] * 3,
        out_shape=[
            jax.ShapeDtypeStruct((2, 8, 128, 256), BF),
            jax.ShapeDtypeStruct((2, 8, 128, 256), BF),
            jax.ShapeDtypeStruct((8, 16, 256), F32),
        ],
        scratch_shapes=[
            pltpu.VMEM((2, 8, 16, 256), BF),
            pltpu.VMEM((2, 8, 16, 256), BF),
            pltpu.VMEM((2, 4, 16, 128), BF),
            pltpu.VMEM((2, 4, 16, 128), BF),
            pltpu.VMEM((16, WIDE, 256), BF),
            pltpu.VMEM((8, WIDE, 128), BF),
            pltpu.VMEM((8, WIDE, 128), F32),
            pltpu.VMEM((2, 2, 8, WIDE, 256), BF),
            pltpu.VMEM((2, 2, 4, WIDE, 128), BF),
            pltpu.VMEM((2, 2, 4, WIDE, 128), BF),
            pltpu.VMEM((32, WIDE, 256), BF),
            pltpu.VMEM((32, WIDE, 256), BF),
            pltpu.VMEM((32, WIDE, 256), BF),
            pltpu.VMEM((32, WIDE, 256), BF),
            pltpu.VMEM((8, 16, 256), F32),
            pltpu.VMEM((8, 16, 256), F32),
            pltpu.VMEM((16, 16, 256), F32),
            pltpu.VMEM((8, 16, 256), F32),
            dma((2, 2)), dma((2, 2)), dma((2, 2, 2)), dma((2, 2, 2)),
            dma((8,)), dma((8,)), dma((16,)), dma((16,)), dma((8,)), dma((8,)),
        ],
        compiler_params=pltpu.CompilerParams(
            collective_id=0, has_side_effects=True, vmem_limit_bytes=56 << 20
        ),
        cost_estimate=pl.CostEstimate(
            flops=3_000_000_000, bytes_accessed=8 << 20, transcendentals=1_500_000
        ),
    )(shift, prev, cur, cot, w9, e)
    gw = gw.reshape(128, 16, 16)[:, :9, :9].reshape(128, 81)
    total = pairs * rows * lax.axis_size("row") * cols * lax.axis_size("col")
    return (
        gc.transpose(0, 3, 1, 2),
        gp.transpose(0, 3, 1, 2),
        gw * (1.0 / math.sqrt(total)),
    )


def solution(mesh):
    grid = P(None, None, "row", "col")
    return jax.shard_map(
        local,
        mesh=mesh,
        in_specs=(grid, grid, P(), P(), grid),
        out_specs=(grid, grid, P()),
        check_vma=False,
    )
```

time: 511 us -> 81.4 us (0.16); the launches traced: 501 us -> 81.2 us
  other arithmetic: 197 us -> 0.01 us
  local copies, waits for them, and re-layouts: 165 us -> 11.8 us
  blocking collectives: 76.4 us -> 0 us
  Pallas kernels: 0 us -> 68.7 us
  starting transfers between devices: 40 us -> 0 us
  between operations: 12.4 us -> 0.67 us
  waiting for transfers between devices: 6.87 us -> 0 us
    unnamed x24 -> x0, other arithmetic: 82.2 us -> none
    psum x1 -> x0, blocking collectives: 76.4 us -> none  [local(): weight_acc = weight_acc + lax.psum(weight_term, ('row', 'col'))]
    pallas_call x0 -> x1, Pallas kernels: none -> 68.7 us  [local(): pl.pallas_call(kernel, in_specs=[pl.BlockSpec(memory_space=pltpu.SMEM)] +...]
    dot_general x2 -> x0, other arithmetic: 64.5 us -> none  [spread_terms(): jnp.einsum('vyx,vcyx->cyx', grad_part, cur_stack[:, :, 8 - first:8 - firs...]
    unnamed x157 -> x15, local copies, waits for them, and re-layouts: 65 us -> 10.2 us
    dot_general x36 -> x0, local copies, waits for them, and re-layouts: 48.1 us -> none  [the longest x18 46 us: local(): jnp.einsum('vyx,vcyx->cyx', grad_volume[9 * first:9 * first + 9], prev_st...]
    ppermute x12 -> x0, starting transfers between devices: 40 us -> none  [the longest x6 28.6 us: with_halo(): before = lax.ppermute(last, axis, up)]
    slice x11 -> x0, local copies, waits for them, and re-layouts: 22.8 us -> none  [the longest x4 13.4 us: with_halo(): last = lax.slice_in_dim(x, length - width, length, axis=dim)]
  transfers between devices with their start and end apart: 12 -> 0, of which waited for: 2 -> 0; matrix products, arithmetic and copies ran while one was open for 44% -> 0% of each run, Pallas kernels for 0% -> 0%
where the time goes in v1:
time: 81.4 us; the launch traced here: 81.2 us
  Pallas kernels  68.7 us (84%)
  local copies, waits for them, and re-layouts  11.8 us (14%)
    pallas_call x1, Pallas kernels, local(): pl.pallas_call(kernel, in_specs=[pl.BlockSpec(memory_space=pltpu.SMEM)] +...  68.7 us
    unnamed x15, local copies, waits for them, and re-layouts  10.2 us

profile of v1, /device:TPU:1, one launch (start us, length us, event | category | flops | bytes accessed | tf_op | source)
XLA Modules:
  0.0 81.2 jit_solution(7244718464528168464)
XLA Ops:
  0.6 0.0 copy-start
  0.6 0.9 %copy.33 = bf16[128,81]{1,0:T(8,128)(2,1)S(1)} copy(bf16[128,81]{0,1:T(8,128)(2,1)} %param.9) | data formatting | bytes 41472 | tf_op args[3]
  1.6 0.6 pad.4.w_ref
  2.2 2.1 %copy.32 = bf16[2,128,8,128]{1,3,2,0:T(8,128)(2,1)} copy(bf16[2,128,8,128]{3,2,1,0:T(8,128)(2,1)} %param.10) | data formatting | bytes 1048576 | tf_op args[4]
  4.3 0.0 copy-done
  4.3 0.0 copy-start.1
  4.3 1.4 %copy.31 = bf16[2,256,8,128]{1,3,2,0:T(8,128)(2,1)} copy(bf16[2,256,8,128]{3,2,1,0:T(8,128)(2,1)S(1)} %copy-done) | data formatting | bytes 2097152 | tf_op args[0]
  5.8 0.0 copy-done.1
  5.8 1.4 %copy.30 = bf16[2,256,8,128]{1,3,2,0:T(8,128)(2,1)} copy(bf16[2,256,8,128]{3,2,1,0:T(8,128)(2,1)S(1)} %copy-done.1) | data formatting | bytes 2097152 | tf_op args[1]
  7.2 68.7 %shard_map.85 = (bf16[2,8,128,256]{3,2,1,0:T(8,128)(2,1)}, bf16[2,8,128,256]{3,2,1,0:T(8,128)(2,1)}, f32[8,16,256]{2,1,0:T(8,128)}) custom-call(s32[2,2]{1,0:T(2,128)} %shift_ref.1, bf16[2,8,128,256]{3,2,1,0:T(8,128)(2,1)} %bitcast.12, bf16[2,8,128,256]{3,2,1,0:T(8,128)(2,1)} %bitcast.11, bf16[2,8,128,128]{3,2,1,0:T(8,128)(2,1)} %bitcast.13, ...), custom_call_target="tpu_custom_call" | custom-call | flops 3000000000 | bytes 8388608 | tf_op jit(solution)/shard_map/pallas_call | solution.py:367
  76.0 0.0 copy-start.2
  76.0 2.5 %copy.35 = bf16[2,256,8,128]{3,2,1,0:T(8,128)(2,1)} copy(bf16[2,256,8,128]{1,3,2,0:T(8,128)(2,1)} %bitcast.10) | data formatting | bytes 2097152
  78.5 0.0 copy-done.2
  78.5 0.0 copy-start.3
  78.5 1.5 %copy.36 = bf16[2,256,8,128]{3,2,1,0:T(8,128)(2,1)} copy(bf16[2,256,8,128]{1,3,2,0:T(8,128)(2,1)S(1)} %bitcast.9) | data formatting | bytes 2097152
  80.0 0.0 copy-done.3
  80.0 0.3 reshape.12
  80.3 0.3 copy.37
  80.6 0.6 mul.11
  (1 shorter events, 0.0 us)
Async XLA Ops:
  0.6 3.7 %copy-start = (bf16[2,256,8,128]{3,2,1,0:T(8,128)(2,1)S(1)}, bf16[2,256,8,128]{3,2,1,0:T(8,128)(2,1)}, u32[]{:S(2)}) copy-start(bf16[2,256,8,128]{3,2,1,0:T(8,128)(2,1)} %param.6) | copy-start | bytes 3145732
  4.3 1.5 %copy-start.1 = (bf16[2,256,8,128]{3,2,1,0:T(8,128)(2,1)S(1)}, bf16[2,256,8,128]{3,2,1,0:T(8,128)(2,1)}, u32[]{:S(2)}) copy-start(bf16[2,256,8,128]{3,2,1,0:T(8,128)(2,1)} %param.7) | copy-start | bytes 3145732
  76.0 2.5 %copy-start.2 = (bf16[2,8,128,256]{3,2,1,0:T(8,128)(2,1)S(1)}, bf16[2,8,128,256]{3,2,1,0:T(8,128)(2,1)}, u32[]{:S(2)}) copy-start(bf16[2,8,128,256]{3,2,1,0:T(8,128)(2,1)} %get-tuple-element.7) | copy-start | bytes 3145732
  78.5 1.5 %copy-start.3 = (f32[8,16,256]{2,1,0:T(8,128)S(1)}, f32[8,16,256]{2,1,0:T(8,128)}, u32[]{:S(2)}) copy-start(f32[8,16,256]{2,1,0:T(8,128)} %get-tuple-element.8) | copy-start | bytes 393220

commit v2 on v1

v2 whole, which is shorter than its diff:
```python
import functools
import math

import jax
import jax.numpy as jnp
import numpy as np
from jax import lax
from jax.experimental import pallas as pl
from jax.experimental.pallas import tpu as pltpu
from jax.sharding import PartitionSpec as P

BF = jnp.bfloat16
F32 = jnp.float32
MESH = pl.DeviceIdType.MESH
NT = (((1,), (1,)), ((), ()))
TN = (((0,), (0,)), ((), ()))
NN = (((1,), (0,)), ((), ()))
WIDE = 144


def dot(a, b, dims=NN):
    return lax.dot_general(a, b, dims, preferred_element_type=F32)


def iota(shape, axis):
    return lax.broadcasted_iota(jnp.int32, shape, axis)


def skew(x, shift):
    return pltpu.roll(x, shift % 256, 1, stride=1, stride_axis=0)


def flip8(x):
    idx = 7 - iota((8, 128), 0)
    parts = [
        jnp.take_along_axis(x[:, at : at + 128], idx, axis=0) for at in range(0, x.shape[1], 128)
    ]
    return parts[0] if len(parts) == 1 else jnp.concatenate(parts, axis=1)


def activation(vol_dot):
    half = vol_dot * (1.0 / 32.0)
    q = 1.0 + jnp.tanh(half)
    act = half * q
    return act, q + act * (2.0 - q)


def cell_block(p, bb, rows_of, cur_ref):
    at = pl.multiple_of(bb * 16, 16)
    cur = cur_ref[p, :, pl.ds(at, 16), :].reshape(128, 256)
    rows = [rows_of(i, at) for i in range(8)]
    win = jnp.concatenate([r[0:16] for r in rows] + [r[8:24] for r in rows], axis=0)
    return win, dot(cur, win, NT)


def split_product(grads, win):
    zero = jnp.zeros((8, 128), F32)
    full = [
        jnp.concatenate([zero, g] if i % 2 else [g, zero], axis=1) for i, g in enumerate(grads)
    ]
    return dot(jnp.concatenate(full, axis=0).astype(BF), win)


def cells_early(p, bb, dy, own, cur_ref, cot_ref, wk, sum_c, act_c, pre_c):
    win, vol = cell_block(p, bb, lambda i, at: own[i, pl.ds(at, 32), :], cur_ref)
    at = pl.multiple_of(bb * 16, 16)
    pre = dot(cot_ref[p, :, pl.ds(at, 16), :].reshape(128, 128), wk)
    grads, acts, rest = [], [], []
    for i in range(16):
        y, odd = divmod(i, 2)
        rows = slice(8 * i, 8 * i + 8)
        act, slope = activation(vol[rows, 128 * odd : 128 * odd + 128])
        piece = skew(pre[rows], 16 * y)
        grads.append(piece[:, :128] * slope)
        rest.append(piece[:, 128:])
        acts.append(flip8(act))
    act_c[p, bb] = jnp.concatenate(acts, axis=0)
    pre_c[p, bb] = jnp.concatenate(rest, axis=0)
    sum_c[p, bb] = split_product(grads, win)


def cells_late(p, bb, dy, halo, cur_ref, cot_ref, sum_c, act_c, pre_c, out_ref, acc_ref):
    def rows_of(i, at):
        return halo[jnp.where(i < 4 + dy, 8 + i, i), pl.ds(at, 32), :]

    win, vol = cell_block(p, bb, rows_of, cur_ref)
    at = pl.multiple_of(bb * 16, 16)
    cot = cot_ref[p, :, pl.ds(at, 16), :].reshape(128, 128).astype(F32)
    cot_rev = jnp.concatenate([flip8(cot[8 * i : 8 * i + 8]) for i in range(16)], axis=0)
    act_own, pre = act_c[p, bb], pre_c[p, bb]
    grads, acts = [], []
    for i in range(16):
        y, odd = divmod(i, 2)
        rows = slice(8 * i, 8 * i + 8)
        act, slope = activation(vol[rows, 128 * odd : 128 * odd + 128])
        grads.append(pre[rows] * slope)
        act = jnp.concatenate([act_own[rows], flip8(act)], axis=1)
        acts.append(skew(act, 249 - 16 * y))
    act = jnp.concatenate(acts, axis=0).astype(BF)
    acc_ref[p] += dot(cot_rev.astype(BF), act, TN)
    out = sum_c[p, bb] + split_product(grads, win)
    out_ref[p, :, pl.ds(at, 16), :] = out.astype(BF).reshape(8, 16, 256)


def position_block(p, bb, rows_of, pres_of, half_of, prev_ref, spread, masks):
    at = pl.multiple_of(bb * 16, 16)
    prev = prev_ref[p, :, pl.ds(at, 16), :].reshape(128, 256)
    win = jnp.concatenate([rows_of(i, at)[:24] for i in range(8)], axis=0)
    vol = dot(win, prev, NT)
    pre = dot(jnp.concatenate([pres_of(i, at)[:24] for i in range(8)], axis=0), spread)
    grads = []
    for i in range(8):
        for g in range(3):
            rows = slice(24 * i + 8 * g, 24 * i + 8 * g + 8)
            piece = pre[rows]
            if g != 1:
                piece = piece * masks[g // 2]
            piece = skew(piece, 16 * i + 8 * (g - 1))
            grads.append(half_of(i, piece) * activation(vol[rows])[1])
    return dot(jnp.concatenate(grads, axis=0).astype(BF), win, TN)


def positions_early(p, bb, dy, own, own_cot, prev_ref, wk, masks, sum_p):
    sum_p[p, bb] = position_block(
        p, bb, lambda i, at: own[8 + i, pl.ds(at, 32), :],
        lambda i, at: own_cot[i, pl.ds(at, 32), :], lambda i, x: x[:, :128],
        prev_ref, wk, masks,
    )


def positions_late(p, bb, dy, halo, pre_halo, prev_ref, e, masks, sum_p, out_ref):
    out = sum_p[p, bb] + position_block(
        p, bb, lambda i, at: halo[jnp.where(i < 4 + dy, i, 8 + i), pl.ds(at, 32), :],
        lambda i, at: pre_halo[i, pl.ds(at, 32), :],
        lambda i, x: jnp.where(i < 4 + dy, x[:, 128:], x[:, :128]),
        prev_ref, e, masks,
    )
    at = pl.multiple_of(bb * 16, 16)
    out_ref[p, :, pl.ds(at, 16), :] = out.astype(BF).reshape(8, 16, 256)


def kernel(
    norm, shift_ref, prev_ref, cur_ref, cot_ref, w_ref, e_ref, eye_ref,
    gc_ref, gp_ref, gw_ref,
    edge_s, edge_r, edge_cot_s, edge_cot_r, own0, own1, own_cot0, own_cot1, own_pre,
    msg, tri_s, tri_r, halo0, halo1, pre_halo0, pre_halo1,
    sum_c, act_c, pre_c, sum_p, acc, ar0, ar1, ar2, ar3,
    side_ss, side_rs, row_ss, row_rs, s1, r1, s2, r2, s3, r3,
):
    row, col = lax.axis_index("row"), lax.axis_index("col")
    last = lax.axis_size("row") - 1
    left = col == 0
    owns, own_cots = (own0, own1), (own_cot0, own_cot1)
    halos, pre_halos = (halo0, halo1), (pre_halo0, pre_halo1)
    g1, g2 = (row % 4) * 2 + col, row // 4

    def member(a, b):
        return (b * 4 + a // 2, a % 2)

    barrier = pltpu.get_barrier_semaphore()

    def greet(target):
        pl.semaphore_signal(barrier, inc=1, device_id=target, device_id_type=MESH)

    for d in range(1, 8):
        greet(member((g1 + d) % 8, g2))
    for d in range(1, 16):
        greet(member(g1, (g2 + d) % 16))
    greet(((row + 1) % (last + 1), col))
    greet(((row + last) % (last + 1), col))

    def side(p, k):
        s, r = ((edge_s, edge_r), (edge_cot_s, edge_cot_r))[k]
        return pltpu.make_async_remote_copy(
            src_ref=s.at[p], dst_ref=r.at[p], send_sem=side_ss.at[p, k],
            recv_sem=side_rs.at[p, k], device_id=(row, 1 - col), device_id_type=MESH,
        )

    def along(p, way, k):
        if k == 0:
            src, dst = msg.at[p, way], halos[p].at[pl.ds(0 if way else 8, 8)]
        else:
            src, dst = tri_s.at[p, way], tri_r.at[p, way]
        target = jnp.where(row == last, row, row + 1) if way else jnp.where(row == 0, row, row - 1)
        return pltpu.make_async_remote_copy(
            src_ref=src, dst_ref=dst, send_sem=row_ss.at[p, way, k],
            recv_sem=row_rs.at[p, way, k], device_id=(target, col), device_id_type=MESH,
        )

    start = jnp.where(left, 112, 0)
    for p in range(2):
        for y in range(8):
            pick = []
            for ref in (prev_ref, cur_ref):
                tile = ref[p, y, pl.ds(pl.multiple_of(start, 16), 16), :].astype(F32)
                pick.append(jnp.where(left, tile[8:], tile[:8]))
            edge_s[p, y] = jnp.concatenate(pick, axis=0).astype(BF)
        for y in range(0, 8, 2):
            pick = []
            for yy in (y, y + 1):
                tile = cot_ref[p, yy, pl.ds(pl.multiple_of(start, 16), 16), :].astype(F32)
                pick.append(jnp.where(left, tile[8:], tile[:8]))
            edge_cot_s[p, y // 2] = jnp.concatenate(pick, axis=0).astype(BF)
    pl.semaphore_wait(barrier, 24)
    for p in range(2):
        for k in range(2):
            side(p, k).start()

    w81 = w_ref[...]
    e = e_ref[...]
    w9 = dot(w81, eye_ref[...], TN).astype(BF)
    wk = dot(w9, e)
    turns = [(16 * (shift_ref[p, 0] + 12)) % 256 for p in range(2)]
    back = [(16 * (4 - shift_ref[p, 0])) % 256 for p in range(2)]
    wks = [pltpu.roll(wk, turns[p], 1).astype(BF) for p in range(2)]
    sub, lane = iota((8, 256), 0), iota((8, 256), 1) % 16
    masks = (jnp.where(lane >= 8 - sub, 1.0, 0.0), jnp.where(lane < 8 - sub, 1.0, 0.0))
    out_at, in_at = iota((WIDE, WIDE), 0), iota((WIDE, WIDE), 1)
    far = jnp.where(left, 136, 0)
    tri_lane = iota((WIDE, 128), 1)
    acc[...] = jnp.zeros_like(acc)

    def aligner(offset, slots):
        at = jnp.where(in_at < 128, in_at + 8, in_at - 128 - slots + far)
        ok = (in_at < 128) | ((in_at >= 128 + slots) & (in_at < 136 + slots))
        return jnp.where(ok & (at == out_at + offset), 1.0, 0.0).astype(BF)

    for p in range(2):
        dy, dx = shift_ref[p, 0], shift_ref[p, 1]
        own, own_cot = owns[p], own_cots[p]
        align_p, align_c0, align_c1 = aligner(4 + dx, 0), aligner(4 - dx, 0), aligner(4 - dx, 8)
        for k in range(2):
            side(p, k).wait()
        for y in range(8):
            edge = edge_r[p, y]
            own[y] = dot(align_p, jnp.concatenate([prev_ref[p, y], edge], axis=0)).astype(BF)
            own[8 + y] = dot(align_c1, jnp.concatenate([cur_ref[p, y], edge], axis=0)).astype(BF)
            align = align_c1 if y % 2 else align_c0
            both = jnp.concatenate([cot_ref[p, y], edge_cot_r[p, y // 2]], axis=0)
            aligned = dot(align, both).astype(BF)
            own_cot[y] = aligned
            own_pre[y] = dot(aligned, w9)

        def pack(s, carry):
            msg[p, 0, s] = own[jnp.where(s < 4 + dy, s, 4 + s - dy)]
            msg[p, 1, s] = own[jnp.where(s < 4 + dy, 12 + s - dy, s)]
            return carry

        lax.fori_loop(0, 8, pack, 0)

        def cell_row(t):
            return own_pre[jnp.where(t < 4 + dy, t + 4 - dy, t - 4 - dy)]

        for s in range(4):
            near, away = cell_row(s), cell_row(7 - s)
            tri_s[p, 1, s] = jnp.where(
                tri_lane >= 9 * (8 - s), near, pltpu.roll(away, 128 - 9 * (s + 1), 1)
            ).astype(BF)
            tri_s[p, 0, s] = jnp.where(
                tri_lane < 9 * (8 - s), near, pltpu.roll(away, 9 * (8 - s), 1)
            ).astype(BF)

        @pl.when(row > 0)
        def _():
            for k in range(2):
                along(p, 0, k).start()

        @pl.when(row < last)
        def _():
            for k in range(2):
                along(p, 1, k).start()

    def arrive(p):
        dy = shift_ref[p, 0]
        halo = halos[p]

        @pl.when(row > 0)
        def _():
            for k in range(2):
                along(p, 1, k).wait_recv()

        @pl.when(row == 0)
        def _():
            halo[0:8] = jnp.zeros((8, WIDE, 256), BF)
            tri_r[p, 1] = jnp.zeros((4, WIDE, 128), BF)

        @pl.when(row < last)
        def _():
            for k in range(2):
                along(p, 0, k).wait_recv()

        @pl.when(row == last)
        def _():
            halo[8:16] = jnp.zeros((8, WIDE, 256), BF)
            tri_r[p, 0] = jnp.zeros((4, WIDE, 128), BF)

        for s in range(4):
            up, down = tri_r[p, 0, s].astype(F32), tri_r[p, 1, s].astype(F32)
            pre_halos[p][s] = jnp.where(s < 4 + dy, down, up).astype(BF)
            down = pltpu.roll(down, 9 * (s + 1), 1)
            up = pltpu.roll(up, 128 - 9 * (8 - s), 1)
            pre_halos[p][7 - s] = jnp.where(7 - s < 4 + dy, down, up).astype(BF)

    def loop(lo, hi, work):
        def body(bb, carry):
            work(bb)
            return carry

        lax.fori_loop(lo, hi, body, 0)

    def early(p):
        dy = shift_ref[p, 0]
        loop(0, 8, lambda bb: cells_early(
            p, bb, dy, owns[p], cur_ref, cot_ref, wks[p], sum_c, act_c, pre_c))
        loop(0, 8, lambda bb: positions_early(
            p, bb, dy, owns[p], own_cots[p], prev_ref, wks[p], masks, sum_p))

    def late_cells(p):
        dy = shift_ref[p, 0]
        loop(0, 8, lambda bb: cells_late(
            p, bb, dy, halos[p], cur_ref, cot_ref, sum_c, act_c, pre_c, gc_ref, acc))

    def late_positions(p, lo, hi):
        dy = shift_ref[p, 0]
        loop(lo, hi, lambda bb: positions_late(
            p, bb, dy, halos[p], pre_halos[p], prev_ref, e, masks, sum_p, gp_ref))

    early(0)
    early(1)
    arrive(0)
    late_cells(0)
    late_positions(0, 0, 8)
    arrive(1)
    late_cells(1)

    turned = (pltpu.roll(acc[0], back[0], 1) + pltpu.roll(acc[1], back[1], 1)).T
    for u in range(9):
        ar0[9 * u : 9 * u + 9] = turned[16 * u : 16 * u + 9]
    ar0[81:128] = jnp.zeros((47, 128), F32)

    def share(ref, i):
        return ref.at[pl.ds(pl.multiple_of(i * 16, 16), 16)]

    def first(d):
        peer = (g1 + d) % 8
        return pltpu.make_async_remote_copy(
            src_ref=share(ar0, peer), dst_ref=ar1.at[g1], send_sem=s1.at[peer],
            recv_sem=r1.at[g1], device_id=member(peer, g2), device_id_type=MESH,
        )

    def second(d):
        peer = (g2 + d) % 16
        return pltpu.make_async_remote_copy(
            src_ref=ar2.at[g2], dst_ref=ar2.at[g2], send_sem=s2.at[peer],
            recv_sem=r2.at[g2], device_id=member(g1, peer), device_id_type=MESH,
        )

    def third(d):
        peer = (g1 + d) % 8
        return pltpu.make_async_remote_copy(
            src_ref=ar3.at[g1], dst_ref=ar3.at[g1], send_sem=s3.at[peer],
            recv_sem=r3.at[g1], device_id=member(peer, g2), device_id_type=MESH,
        )

    def got(buffer, sends, receives, source):
        pltpu.make_async_remote_copy(
            src_ref=buffer.at[source], dst_ref=buffer.at[source], send_sem=sends.at[source],
            recv_sem=receives.at[source], device_id=(row, 1 - col), device_id_type=MESH,
        ).wait_recv()

    for d in range(1, 8):
        first(d).start()
    late_positions(1, 0, 3)
    ar1[g1] = ar0[pl.ds(pl.multiple_of(g1 * 16, 16), 16)]
    for d in range(1, 8):
        first(d).wait_send()
        got(ar1, s1, r1, (g1 + d) % 8)
    ar2[g2] = jnp.sum(ar1[...], axis=0)
    for d in range(1, 16):
        second(d).start()
    late_positions(1, 3, 6)
    for d in range(1, 16):
        second(d).wait_send()
        got(ar2, s2, r2, (g2 + d) % 16)
    ar3[g1] = jnp.sum(ar2[...], axis=0)
    for d in range(1, 8):
        third(d).start()
    late_positions(1, 6, 8)
    for d in range(1, 8):
        third(d).wait_send()
        got(ar3, s3, r3, (g1 + d) % 8)
    gw_ref[...] = ar3[...].reshape(128, 128)[:81] * norm

    for p in range(2):
        for k in range(2):

            @pl.when(row > 0)
            def _():
                along(p, 0, k).wait_send()

            @pl.when(row < last)
            def _():
                along(p, 1, k).wait_send()


def spread_matrix():
    e = np.zeros((128, 256), np.float32)
    for u in range(9):
        for v in range(9):
            e[9 * u + v, 16 * u + v] = 1.0 / 32.0
    return e


def local(current, previous, shift, weight, cotangent):
    pairs, channels, rows, cols = current.shape
    prev = previous.transpose(0, 2, 3, 1)
    cur = current.transpose(0, 2, 3, 1)
    cot = cotangent.transpose(0, 2, 3, 1)
    e = jnp.asarray(spread_matrix(), BF)
    eye = jnp.asarray(np.eye(81, 128), BF)
    total = pairs * rows * lax.axis_size("row") * cols * lax.axis_size("col")
    vmem = pl.BlockSpec(memory_space=pltpu.VMEM)
    dma = pltpu.SemaphoreType.DMA
    v = pltpu.VMEM
    gc, gp, gw = pl.pallas_call(
        functools.partial(kernel, 1.0 / math.sqrt(total)),
        in_specs=[pl.BlockSpec(memory_space=pltpu.SMEM)] + [vmem] * 6,
        out_specs=[vmem] * 3,
        out_shape=[
            jax.ShapeDtypeStruct((2, 8, 128, 256), BF),
            jax.ShapeDtypeStruct((2, 8, 128, 256), BF),
            jax.ShapeDtypeStruct((81, 128), F32),
        ],
        scratch_shapes=[
            v((2, 8, 16, 256), BF), v((2, 8, 16, 256), BF),
            v((2, 4, 16, 128), BF), v((2, 4, 16, 128), BF),
            v((16, WIDE, 256), BF), v((16, WIDE, 256), BF),
            v((8, WIDE, 128), BF), v((8, WIDE, 128), BF),
            v((8, WIDE, 128), F32),
            v((2, 2, 8, WIDE, 256), BF),
            v((2, 2, 4, WIDE, 128), BF), v((2, 2, 4, WIDE, 128), BF),
            v((16, WIDE, 256), BF), v((16, WIDE, 256), BF),
            v((8, WIDE, 128), BF), v((8, WIDE, 128), BF),
            v((2, 8, 128, 256), F32),
            v((2, 8, 128, 128), F32), v((2, 8, 128, 128), F32),
            v((2, 8, 128, 256), F32),
            v((2, 128, 256), F32),
            v((128, 128), F32), v((8, 16, 128), F32), v((16, 16, 128), F32), v((8, 16, 128), F32),
            dma((2, 2)), dma((2, 2)), dma((2, 2, 2)), dma((2, 2, 2)),
            dma((8,)), dma((8,)), dma((16,)), dma((16,)), dma((8,)), dma((8,)),
        ],
        compiler_params=pltpu.CompilerParams(
            collective_id=0, has_side_effects=True, vmem_limit_bytes=56 << 20
        ),
        cost_estimate=pl.CostEstimate(
            flops=3_000_000_000, bytes_accessed=8 << 20, transcendentals=1_500_000
        ),
    )(shift, prev, cur, cot, weight.T, e, eye)
    return gc.transpose(0, 3, 1, 2), gp.transpose(0, 3, 1, 2), gw.T


def solution(mesh):
    grid = P(None, None, "row", "col")
    return jax.shard_map(
        local,
        mesh=mesh,
        in_specs=(grid, grid, P(), P(), grid),
        out_specs=(grid, grid, P()),
        check_vma=False,
    )
```

time: 81.4 us -> 78.5 us (0.964)
  local copies, waits for them, and re-layouts: 11.8 us -> 9.71 us
    unnamed x15 -> x14, local copies, waits for them, and re-layouts: 10.2 us -> 9.71 us
where the time goes in v2:
time: 78.5 us; the launch traced here: 78.3 us
  Pallas kernels  68 us (87%)
  local copies, waits for them, and re-layouts  9.71 us (12%)
    pallas_call x1, Pallas kernels, local(): pl.pallas_call(functools.partial(kernel, 1.0 / math.sqrt(total)), in_spec...  68 us
    unnamed x14, local copies, waits for them, and re-layouts  9.71 us

profile of v2, /device:TPU:1, one launch (start us, length us, event | category | flops | bytes accessed | tf_op | source)
XLA Modules:
  0.0 78.3 jit_solution(14695883317032488079)
XLA Ops:
  0.6 0.0 copy-start
  0.6 2.2 %copy.12 = bf16[2,128,8,128]{1,3,2,0:T(8,128)(2,1)} copy(bf16[2,128,8,128]{3,2,1,0:T(8,128)(2,1)} %param.11) | data formatting | bytes 1048576 | tf_op args[4]
  2.8 0.0 copy-done
  2.8 0.0 copy-start.1
  2.8 1.4 %copy.11 = bf16[2,256,8,128]{1,3,2,0:T(8,128)(2,1)} copy(bf16[2,256,8,128]{3,2,1,0:T(8,128)(2,1)S(1)} %copy-done) | data formatting | bytes 2097152 | tf_op args[0]
  4.3 0.0 copy-done.1
  4.3 1.4 %copy.10 = bf16[2,256,8,128]{1,3,2,0:T(8,128)(2,1)} copy(bf16[2,256,8,128]{3,2,1,0:T(8,128)(2,1)S(1)} %copy-done.1) | data formatting | bytes 2097152 | tf_op args[1]
  5.7 68.0 %shard_map.94 = (bf16[2,8,128,256]{3,2,1,0:T(8,128)(2,1)}, bf16[2,8,128,256]{3,2,1,0:T(8,128)(2,1)}, f32[81,128]{1,0:T(8,128)}) custom-call(s32[2,2]{1,0:T(2,128)} %shift_ref.1, bf16[2,8,128,256]{3,2,1,0:T(8,128)(2,1)} %bitcast.10, bf16[2,8,128,256]{3,2,1,0:T(8,128)(2,1)} %bitcast.9, bf16[2,8,128,128]{3,2,1,0:T(8,128)(2,1)} %bitcast.11, ...), custom_call_target="tpu_custom_call" | custom-call | flops 3000000000 | bytes 8388608 | tf_op jit(solution)/shard_map/pallas_call | solution.py:425
  73.7 0.0 copy-start.2
  73.7 2.5 %copy.13 = bf16[2,256,8,128]{3,2,1,0:T(8,128)(2,1)} copy(bf16[2,256,8,128]{1,3,2,0:T(8,128)(2,1)} %bitcast.8) | data formatting | bytes 2097152
  76.3 0.0 copy-done.2
  76.3 0.0 copy-start.3
  76.3 1.5 %copy.14 = bf16[2,256,8,128]{3,2,1,0:T(8,128)(2,1)} copy(bf16[2,256,8,128]{1,3,2,0:T(8,128)(2,1)S(1)} %bitcast.7) | data formatting | bytes 2097152
  77.7 0.0 copy-done.3
  77.7 0.6 copy.16
Async XLA Ops:
  0.6 2.2 %copy-start = (bf16[2,256,8,128]{3,2,1,0:T(8,128)(2,1)S(1)}, bf16[2,256,8,128]{3,2,1,0:T(8,128)(2,1)}, u32[]{:S(2)}) copy-start(bf16[2,256,8,128]{3,2,1,0:T(8,128)(2,1)} %param.7) | copy-start | bytes 3145732
  2.8 1.5 %copy-start.1 = (bf16[2,256,8,128]{3,2,1,0:T(8,128)(2,1)S(1)}, bf16[2,256,8,128]{3,2,1,0:T(8,128)(2,1)}, u32[]{:S(2)}) copy-start(bf16[2,256,8,128]{3,2,1,0:T(8,128)(2,1)} %param.8) | copy-start | bytes 3145732
  73.7 2.5 %copy-start.2 = (bf16[2,8,128,256]{3,2,1,0:T(8,128)(2,1)S(1)}, bf16[2,8,128,256]{3,2,1,0:T(8,128)(2,1)}, u32[]{:S(2)}) copy-start(bf16[2,8,128,256]{3,2,1,0:T(8,128)(2,1)} %get-tuple-element.7) | copy-start | bytes 3145732
  76.3 1.5 %copy-start.3 = (f32[81,128]{1,0:T(8,128)S(1)}, f32[81,128]{1,0:T(8,128)}, u32[]{:S(2)}) copy-start(f32[81,128]{1,0:T(8,128)} %get-tuple-element.8) | copy-start | bytes 124420

commit v3 on v2

--- a/solution.py
+++ b/solution.py
@@ -310,28 +310,35 @@
 
     def early(p):
         dy = shift_ref[p, 0]
-        loop(0, 8, lambda bb: cells_early(
-            p, bb, dy, owns[p], cur_ref, cot_ref, wks[p], sum_c, act_c, pre_c))
-        loop(0, 8, lambda bb: positions_early(
-            p, bb, dy, owns[p], own_cots[p], prev_ref, wks[p], masks, sum_p))
-
-    def late_cells(p):
-        dy = shift_ref[p, 0]
-        loop(0, 8, lambda bb: cells_late(
-            p, bb, dy, halos[p], cur_ref, cot_ref, sum_c, act_c, pre_c, gc_ref, acc))
-
-    def late_positions(p, lo, hi):
-        dy = shift_ref[p, 0]
-        loop(lo, hi, lambda bb: positions_late(
-            p, bb, dy, halos[p], pre_halos[p], prev_ref, e, masks, sum_p, gp_ref))
+
+        def work(i):
+            for bb in (2 * i, 2 * i + 1):
+                cells_early(
+                    p, bb, dy, owns[p], cur_ref, cot_ref, wks[p], sum_c, act_c, pre_c)
+                positions_early(
+                    p, bb, dy, owns[p], own_cots[p], prev_ref, wks[p], masks, sum_p)
+
+        loop(0, 4, work)
+
+    def late_cells(p, bb):
+        cells_late(
+            p, bb, shift_ref[p, 0], halos[p], cur_ref, cot_ref, sum_c, act_c, pre_c, gc_ref, acc)
+
+    def late_positions(p, bb):
+        positions_late(
+            p, bb, shift_ref[p, 0], halos[p], pre_halos[p], prev_ref, e, masks, sum_p, gp_ref)
+
+    def late(i):
+        for bb in (2 * i, 2 * i + 1):
+            late_cells(0, bb)
+            late_positions(0, bb)
 
     early(0)
     early(1)
     arrive(0)
-    late_cells(0)
-    late_positions(0, 0, 8)
+    loop(0, 4, late)
     arrive(1)
-    late_cells(1)
+    loop(0, 2, lambda i: [late_cells(1, 4 * i + k) for k in range(4)])
 
     turned = (pltpu.roll(acc[0], back[0], 1) + pltpu.roll(acc[1], back[1], 1)).T
     for u in range(9):
@@ -370,7 +377,7 @@
 
     for d in range(1, 8):
         first(d).start()
-    late_positions(1, 0, 3)
+    loop(0, 1, lambda i: [late_positions(1, k) for k in range(3)])
     ar1[g1] = ar0[pl.ds(pl.multiple_of(g1 * 16, 16), 16)]
     for d in range(1, 8):
         first(d).wait_send()
@@ -378,14 +385,14 @@
     ar2[g2] = jnp.sum(ar1[...], axis=0)
     for d in range(1, 16):
         second(d).start()
-    late_positions(1, 3, 6)
+    loop(0, 1, lambda i: [late_positions(1, 3 + k) for k in range(3)])
     for d in range(1, 16):
         second(d).wait_send()
         got(ar2, s2, r2, (g2 + d) % 16)
     ar3[g1] = jnp.sum(ar2[...], axis=0)
     for d in range(1, 8):
         third(d).start()
-    late_positions(1, 6, 8)
+    loop(0, 1, lambda i: [late_positions(1, 6 + k) for k in range(2)])
     for d in range(1, 8):
         third(d).wait_send()
         got(ar3, s3, r3, (g1 + d) % 8)

time: 78.5 us -> 77 us (0.981)
  Pallas kernels: 68 us -> 66.4 us
    pallas_call x1, Pallas kernels: 68 us -> 66.4 us  [local(): pl.pallas_call(functools.partial(kernel, 1.0 / math.sqrt(total)), in_spec...]
where the time goes in v3:
time: 77 us; the launch traced here: 76.8 us
  Pallas kernels  66.4 us (86%)
  local copies, waits for them, and re-layouts  9.71 us (13%)
    pallas_call x1, Pallas kernels, local(): pl.pallas_call(functools.partial(kernel, 1.0 / math.sqrt(total)), in_spec...  66.4 us
    unnamed x14, local copies, waits for them, and re-layouts  9.71 us

profile of v3, /device:TPU:1, one launch (start us, length us, event | category | flops | bytes accessed | tf_op | source)
XLA Modules:
  0.0 76.8 jit_solution(18121215565036641068)
XLA Ops:
  0.6 0.0 copy-start
  0.6 2.2 %copy.12 = bf16[2,128,8,128]{1,3,2,0:T(8,128)(2,1)} copy(bf16[2,128,8,128]{3,2,1,0:T(8,128)(2,1)} %param.11) | data formatting | bytes 1048576 | tf_op args[4]
  2.8 0.0 copy-done
  2.8 0.0 copy-start.1
  2.8 1.4 %copy.11 = bf16[2,256,8,128]{1,3,2,0:T(8,128)(2,1)} copy(bf16[2,256,8,128]{3,2,1,0:T(8,128)(2,1)S(1)} %copy-done) | data formatting | bytes 2097152 | tf_op args[0]
  4.3 0.0 copy-done.1
  4.3 1.4 %copy.10 = bf16[2,256,8,128]{1,3,2,0:T(8,128)(2,1)} copy(bf16[2,256,8,128]{3,2,1,0:T(8,128)(2,1)S(1)} %copy-done.1) | data formatting | bytes 2097152 | tf_op args[1]
  5.7 66.4 %shard_map.94 = (bf16[2,8,128,256]{3,2,1,0:T(8,128)(2,1)}, bf16[2,8,128,256]{3,2,1,0:T(8,128)(2,1)}, f32[81,128]{1,0:T(8,128)}) custom-call(s32[2,2]{1,0:T(2,128)} %shift_ref.1, bf16[2,8,128,256]{3,2,1,0:T(8,128)(2,1)} %bitcast.10, bf16[2,8,128,256]{3,2,1,0:T(8,128)(2,1)} %bitcast.9, bf16[2,8,128,128]{3,2,1,0:T(8,128)(2,1)} %bitcast.11, ...), custom_call_target="tpu_custom_call" | custom-call | flops 3000000000 | bytes 8388608 | tf_op jit(solution)/shard_map/pallas_call | solution.py:432
  72.2 0.0 copy-start.2
  72.2 2.5 %copy.13 = bf16[2,256,8,128]{3,2,1,0:T(8,128)(2,1)} copy(bf16[2,256,8,128]{1,3,2,0:T(8,128)(2,1)} %bitcast.8) | data formatting | bytes 2097152
  74.7 0.0 copy-done.2
  74.7 0.0 copy-start.3
  74.7 1.5 %copy.14 = bf16[2,256,8,128]{3,2,1,0:T(8,128)(2,1)} copy(bf16[2,256,8,128]{1,3,2,0:T(8,128)(2,1)S(1)} %bitcast.7) | data formatting | bytes 2097152
  76.2 0.0 copy-done.3
  76.2 0.6 copy.16
Async XLA Ops:
  0.6 2.2 %copy-start = (bf16[2,256,8,128]{3,2,1,0:T(8,128)(2,1)S(1)}, bf16[2,256,8,128]{3,2,1,0:T(8,128)(2,1)}, u32[]{:S(2)}) copy-start(bf16[2,256,8,128]{3,2,1,0:T(8,128)(2,1)} %param.7) | copy-start | bytes 3145732
  2.8 1.5 %copy-start.1 = (bf16[2,256,8,128]{3,2,1,0:T(8,128)(2,1)S(1)}, bf16[2,256,8,128]{3,2,1,0:T(8,128)(2,1)}, u32[]{:S(2)}) copy-start(bf16[2,256,8,128]{3,2,1,0:T(8,128)(2,1)} %param.8) | copy-start | bytes 3145732
  72.2 2.5 %copy-start.2 = (bf16[2,8,128,256]{3,2,1,0:T(8,128)(2,1)S(1)}, bf16[2,8,128,256]{3,2,1,0:T(8,128)(2,1)}, u32[]{:S(2)}) copy-start(bf16[2,8,128,256]{3,2,1,0:T(8,128)(2,1)} %get-tuple-element.7) | copy-start | bytes 3145732
  74.7 1.5 %copy-start.3 = (f32[81,128]{1,0:T(8,128)S(1)}, f32[81,128]{1,0:T(8,128)}, u32[]{:S(2)}) copy-start(f32[81,128]{1,0:T(8,128)} %get-tuple-element.8) | copy-start | bytes 124420

commit v4 on v3

--- a/solution.py
+++ b/solution.py
@@ -81,7 +81,7 @@
 
 def cells_late(p, bb, dy, halo, cur_ref, cot_ref, sum_c, act_c, pre_c, out_ref, acc_ref):
     def rows_of(i, at):
-        return halo[jnp.where(i < 4 + dy, 8 + i, i), pl.ds(at, 32), :]
+        return halo[i, pl.ds(at, 32), :]
 
     win, vol = cell_block(p, bb, rows_of, cur_ref)
     at = pl.multiple_of(bb * 16, 16)
@@ -130,7 +130,7 @@
 
 def positions_late(p, bb, dy, halo, pre_halo, prev_ref, e, masks, sum_p, out_ref):
     out = sum_p[p, bb] + position_block(
-        p, bb, lambda i, at: halo[jnp.where(i < 4 + dy, i, 8 + i), pl.ds(at, 32), :],
+        p, bb, lambda i, at: halo[8 + i, pl.ds(at, 32), :],
         lambda i, at: pre_halo[i, pl.ds(at, 32), :],
         lambda i, x: jnp.where(i < 4 + dy, x[:, 128:], x[:, :128]),
         prev_ref, e, masks,
@@ -140,9 +140,10 @@
 
 
 def kernel(
-    norm, shift_ref, prev_ref, cur_ref, cot_ref, w_ref, e_ref, eye_ref,
+    norm, shift_ref, prev_in, cur_in, cot_in, w_ref, e_ref, eye_ref,
     gc_ref, gp_ref, gw_ref,
-    edge_s, edge_r, edge_cot_s, edge_cot_r, own0, own1, own_cot0, own_cot1, own_pre,
+    prev_ref, cur_ref, cot_ref, flat0, flat1, msg_r, rim_s, rim_r,
+    edge_s, edge_r0, edge_r1, edge_cot_s, edge_cot_r, own0, own1, own_cot0, own_cot1, own_pre,
     msg, tri_s, tri_r, halo0, halo1, pre_halo0, pre_halo1,
     sum_c, act_c, pre_c, sum_p, acc, ar0, ar1, ar2, ar3,
     side_ss, side_rs, row_ss, row_rs, s1, r1, s2, r2, s3, r3,
@@ -170,25 +171,66 @@
     greet(((row + last) % (last + 1), col))
 
     def side(p, k):
-        s, r = ((edge_s, edge_r), (edge_cot_s, edge_cot_r))[k]
+        src, dst = (
+            (edge_s.at[p], (edge_r0, edge_r1)[p]), (edge_cot_s.at[p], edge_cot_r.at[p])
+        )[k]
         return pltpu.make_async_remote_copy(
-            src_ref=s.at[p], dst_ref=r.at[p], send_sem=side_ss.at[p, k],
+            src_ref=src, dst_ref=dst, send_sem=side_ss.at[p, k],
             recv_sem=side_rs.at[p, k], device_id=(row, 1 - col), device_id_type=MESH,
         )
 
     def along(p, way, k):
-        if k == 0:
-            src, dst = msg.at[p, way], halos[p].at[pl.ds(0 if way else 8, 8)]
-        else:
-            src, dst = tri_s.at[p, way], tri_r.at[p, way]
+        s, r = ((msg, msg_r), (rim_s, rim_r), (tri_s, tri_r))[k]
+        src, dst = s.at[p, way], r.at[p, way]
         target = jnp.where(row == last, row, row + 1) if way else jnp.where(row == 0, row, row - 1)
         return pltpu.make_async_remote_copy(
             src_ref=src, dst_ref=dst, send_sem=row_ss.at[p, way, k],
             recv_sem=row_rs.at[p, way, k], device_id=(target, col), device_id_type=MESH,
         )
 
+    def pack(p):
+        dy = shift_ref[p, 0]
+
+        def chunk(i, carry):
+            at = pl.ds(pl.multiple_of(i * 16, 16), 16)
+            pos = prev_in[p, at].astype(F32)
+            cell = pltpu.roll(cur_in[p, at].astype(F32), (4 + dy) % 8, 1)
+            low = iota((16, 8, 128), 1) < 4 + dy
+            msg[p, 0, at] = jnp.where(low, pos, cell).astype(BF)
+            msg[p, 1, at] = jnp.where(low, cell, pos).astype(BF)
+            return carry
+
+        lax.fori_loop(0, 16, chunk, 0)
+
+    def send(p, k):
+        @pl.when(row > 0)
+        def _():
+            along(p, 0, k).start()
+
+        @pl.when(row < last)
+        def _():
+            along(p, 1, k).start()
+
+    ident = jnp.where(iota((128, 128), 0) == iota((128, 128), 1), 1.0, 0.0).astype(BF)
+
+    def spread_rows(flat, x):
+        flat[0 : x.shape[0] * 8] = x.reshape(x.shape[0] * 8, 128)
+
+    def picked(flat, y, channels):
+        return flat[pl.ds(y, channels, stride=8), :].astype(BF)
+
+    def turn(p):
+        for source, target, flat in (
+            (prev_in, prev_ref, flat0), (cur_in, cur_ref, flat1), (cot_in, cot_ref, flat0)
+        ):
+            channels = source.shape[1]
+            spread_rows(flat, source[p].astype(F32))
+            for y in range(8):
+                target[p, y] = dot(ident, picked(flat, y, channels), NT).astype(BF)
+
     start = jnp.where(left, 112, 0)
-    for p in range(2):
+
+    def edges(p):
         for y in range(8):
             pick = []
             for ref in (prev_ref, cur_ref):
@@ -201,10 +243,17 @@
                 tile = cot_ref[p, yy, pl.ds(pl.multiple_of(start, 16), 16), :].astype(F32)
                 pick.append(jnp.where(left, tile[8:], tile[:8]))
             edge_cot_s[p, y // 2] = jnp.concatenate(pick, axis=0).astype(BF)
-    pl.semaphore_wait(barrier, 24)
-    for p in range(2):
         for k in range(2):
             side(p, k).start()
+
+    pack(0)
+    pl.semaphore_wait(barrier, 24)
+    send(0, 0)
+    turn(0)
+    edges(0)
+    pack(1)
+    turn(1)
+    edges(1)
 
     w81 = w_ref[...]
     e = e_ref[...]
@@ -215,38 +264,45 @@
     wks = [pltpu.roll(wk, turns[p], 1).astype(BF) for p in range(2)]
     sub, lane = iota((8, 256), 0), iota((8, 256), 1) % 16
     masks = (jnp.where(lane >= 8 - sub, 1.0, 0.0), jnp.where(lane < 8 - sub, 1.0, 0.0))
-    out_at, in_at = iota((WIDE, WIDE), 0), iota((WIDE, WIDE), 1)
     far = jnp.where(left, 136, 0)
     tri_lane = iota((WIDE, 128), 1)
     acc[...] = jnp.zeros_like(acc)
 
-    def aligner(offset, slots):
-        at = jnp.where(in_at < 128, in_at + 8, in_at - 128 - slots + far)
-        ok = (in_at < 128) | ((in_at >= 128 + slots) & (in_at < 136 + slots))
-        return jnp.where(ok & (at == out_at + offset), 1.0, 0.0).astype(BF)
-
-    for p in range(2):
+    def aligner(offset):
+        take = iota((WIDE, 128), 1) + 8 == iota((WIDE, 128), 0) + offset
+        out = [jnp.where(take, 1.0, 0.0).astype(BF)]
+        at, in_at = iota((WIDE, 16), 0) + offset, iota((WIDE, 16), 1)
+        for slots in (0, 8):
+            ok = (in_at >= slots) & (in_at < slots + 8) & (in_at - slots + far == at)
+            out.append(jnp.where(ok, 1.0, 0.0).astype(BF))
+        return out
+
+    def join(p):
         dy, dx = shift_ref[p, 0], shift_ref[p, 1]
-        own, own_cot = owns[p], own_cots[p]
-        align_p, align_c0, align_c1 = aligner(4 + dx, 0), aligner(4 - dx, 0), aligner(4 - dx, 8)
+        own, own_cot, edge_r = owns[p], own_cots[p], (edge_r0, edge_r1)[p]
+        take_p, rim_p, _ = aligner(4 + dx)
+        take_c, rim_c0, rim_c1 = aligner(4 - dx)
         for k in range(2):
             side(p, k).wait()
         for y in range(8):
-            edge = edge_r[p, y]
-            own[y] = dot(align_p, jnp.concatenate([prev_ref[p, y], edge], axis=0)).astype(BF)
-            own[8 + y] = dot(align_c1, jnp.concatenate([cur_ref[p, y], edge], axis=0)).astype(BF)
-            align = align_c1 if y % 2 else align_c0
-            both = jnp.concatenate([cot_ref[p, y], edge_cot_r[p, y // 2]], axis=0)
-            aligned = dot(align, both).astype(BF)
+            edge = edge_r[y]
+            own[y] = (dot(take_p, prev_ref[p, y]) + dot(rim_p, edge)).astype(BF)
+            own[8 + y] = (dot(take_c, cur_ref[p, y]) + dot(rim_c1, edge)).astype(BF)
+            rim = dot(rim_c1 if y % 2 else rim_c0, edge_cot_r[p, y // 2])
+            aligned = (dot(take_c, cot_ref[p, y]) + rim).astype(BF)
             own_cot[y] = aligned
             own_pre[y] = dot(aligned, w9)
 
-        def pack(s, carry):
-            msg[p, 0, s] = own[jnp.where(s < 4 + dy, s, 4 + s - dy)]
-            msg[p, 1, s] = own[jnp.where(s < 4 + dy, 12 + s - dy, s)]
-            return carry
-
-        lax.fori_loop(0, 8, pack, 0)
+        def tile(s, up):
+            is_prev = (s < 4 + dy) if up else (s >= 4 + dy)
+            at = jnp.where(is_prev, s, jnp.where(s < 4 + dy, s + 4 - dy, s - 4 - dy))
+            both = edge_r[at].astype(F32)
+            return jnp.where(is_prev, both[:8], both[8:])
+
+        for k in range(4):
+            for way in range(2):
+                pair = [tile(2 * k, way == 0), tile(2 * k + 1, way == 0)]
+                rim_s[p, way, k] = jnp.concatenate(pair, axis=0).astype(BF)
 
         def cell_row(t):
             return own_pre[jnp.where(t < 4 + dy, t + 4 - dy, t - 4 - dy)]
@@ -259,41 +315,62 @@
             tri_s[p, 0, s] = jnp.where(
                 tri_lane < 9 * (8 - s), near, pltpu.roll(away, 9 * (8 - s), 1)
             ).astype(BF)
+        send(p, 1)
+        send(p, 2)
+
+    join(0)
+    send(1, 0)
+    join(1)
+
+    def arrive(p):
+        dy, dx = shift_ref[p, 0], shift_ref[p, 1]
+        halo = halos[p]
+        take_p, *rim_p = aligner(4 + dx)
+        take_c, *rim_c = aligner(4 - dx)
 
         @pl.when(row > 0)
         def _():
-            for k in range(2):
-                along(p, 0, k).start()
+            for k in range(3):
+                along(p, 1, k).wait_recv()
+
+        @pl.when(row == 0)
+        def _():
+            msg_r[p, 1] = jnp.zeros((256, 8, 128), BF)
+            rim_r[p, 1] = jnp.zeros((4, 16, 256), BF)
+            tri_r[p, 1] = jnp.zeros((4, WIDE, 128), BF)
 
         @pl.when(row < last)
         def _():
-            for k in range(2):
-                along(p, 1, k).start()
-
-    def arrive(p):
-        dy = shift_ref[p, 0]
-        halo = halos[p]
-
-        @pl.when(row > 0)
-        def _():
-            for k in range(2):
-                along(p, 1, k).wait_recv()
-
-        @pl.when(row == 0)
-        def _():
-            halo[0:8] = jnp.zeros((8, WIDE, 256), BF)
-            tri_r[p, 1] = jnp.zeros((4, WIDE, 128), BF)
-
-        @pl.when(row < last)
-        def _():
-            for k in range(2):
+            for k in range(3):
                 along(p, 0, k).wait_recv()
 
         @pl.when(row == last)
         def _():
-            halo[8:16] = jnp.zeros((8, WIDE, 256), BF)
+            msg_r[p, 0] = jnp.zeros((256, 8, 128), BF)
+            rim_r[p, 0] = jnp.zeros((4, 16, 256), BF)
             tri_r[p, 0] = jnp.zeros((4, WIDE, 128), BF)
 
+        def sort(i, carry):
+            at = pl.ds(pl.multiple_of(i * 16, 16), 16)
+            to = pl.ds(pl.multiple_of(i * 128, 128), 128)
+            up, down = msg_r[p, 0, at].astype(F32), msg_r[p, 1, at].astype(F32)
+            low = iota((16, 8, 128), 1) < 4 + dy
+            flat0[to] = jnp.where(low, up, down).reshape(128, 128)
+            flat1[to] = jnp.where(low, down, up).reshape(128, 128)
+            return carry
+
+        lax.fori_loop(0, 16, sort, 0)
+        for k in range(4):
+            up, down = rim_r[p, 0, k].astype(F32), rim_r[p, 1, k].astype(F32)
+            low = 2 * k + iota((16, 256), 0) // 8 < 4 + dy
+            edge_p = jnp.where(low, up, down).astype(BF)
+            edge_c = jnp.where(low, down, up).astype(BF)
+            for h in range(2):
+                s = 2 * k + h
+                x = dot(take_p, picked(flat0, s, 256), NT) + dot(rim_p[h], edge_p)
+                halo[s] = x.astype(BF)
+                x = dot(take_c, picked(flat1, s, 256), NT) + dot(rim_c[h], edge_c)
+                halo[8 + s] = x.astype(BF)
         for s in range(4):
             up, down = tri_r[p, 0, s].astype(F32), tri_r[p, 1, s].astype(F32)
             pre_halos[p][s] = jnp.where(s < 4 + dy, down, up).astype(BF)
@@ -399,7 +476,7 @@
     gw_ref[...] = ar3[...].reshape(128, 128)[:81] * norm
 
     for p in range(2):
-        for k in range(2):
+        for k in range(3):
 
             @pl.when(row > 0)
             def _():
@@ -420,9 +497,6 @@
 
 def local(current, previous, shift, weight, cotangent):
     pairs, channels, rows, cols = current.shape
-    prev = previous.transpose(0, 2, 3, 1)
-    cur = current.transpose(0, 2, 3, 1)
-    cot = cotangent.transpose(0, 2, 3, 1)
     e = jnp.asarray(spread_matrix(), BF)
     eye = jnp.asarray(np.eye(81, 128), BF)
     total = pairs * rows * lax.axis_size("row") * cols * lax.axis_size("col")
@@ -439,12 +513,15 @@
             jax.ShapeDtypeStruct((81, 128), F32),
         ],
         scratch_shapes=[
-            v((2, 8, 16, 256), BF), v((2, 8, 16, 256), BF),
+            v((2, 8, 128, 256), BF), v((2, 8, 128, 256), BF), v((2, 8, 128, 128), BF),
+            v((2048, 128), F32), v((2048, 128), F32),
+            v((2, 2, 256, 8, 128), BF), v((2, 2, 4, 16, 256), BF), v((2, 2, 4, 16, 256), BF),
+            v((2, 8, 16, 256), BF), v((8, 16, 256), BF), v((8, 16, 256), BF),
             v((2, 4, 16, 128), BF), v((2, 4, 16, 128), BF),
             v((16, WIDE, 256), BF), v((16, WIDE, 256), BF),
             v((8, WIDE, 128), BF), v((8, WIDE, 128), BF),
             v((8, WIDE, 128), F32),
-            v((2, 2, 8, WIDE, 256), BF),
+            v((2, 2, 256, 8, 128), BF),
             v((2, 2, 4, WIDE, 128), BF), v((2, 2, 4, WIDE, 128), BF),
             v((16, WIDE, 256), BF), v((16, WIDE, 256), BF),
             v((8, WIDE, 128), BF), v((8, WIDE, 128), BF),
@@ -453,7 +530,7 @@
             v((2, 8, 128, 256), F32),
             v((2, 128, 256), F32),
             v((128, 128), F32), v((8, 16, 128), F32), v((16, 16, 128), F32), v((8, 16, 128), F32),
-            dma((2, 2)), dma((2, 2)), dma((2, 2, 2)), dma((2, 2, 2)),
+            dma((2, 2)), dma((2, 2)), dma((2, 2, 3)), dma((2, 2, 3)),
             dma((8,)), dma((8,)), dma((16,)), dma((16,)), dma((8,)), dma((8,)),
         ],
         compiler_params=pltpu.CompilerParams(
@@ -462,7 +539,7 @@
         cost_estimate=pl.CostEstimate(
             flops=3_000_000_000, bytes_accessed=8 << 20, transcendentals=1_500_000
         ),
-    )(shift, prev, cur, cot, weight.T, e, eye)
+    )(shift, previous, current, cotangent, weight.T, e, eye)
     return gc.transpose(0, 3, 1, 2), gp.transpose(0, 3, 1, 2), gw.T
 
 

time: 77 us -> 72.8 us (0.945)
  local copies, waits for them, and re-layouts: 9.71 us -> 4.6 us
  Pallas kernels: 66.4 us -> 67.4 us
    unnamed x14 -> x7, local copies, waits for them, and re-layouts: 9.71 us -> 4.6 us
    pallas_call x1, Pallas kernels: 66.4 us -> 67.4 us  [local(): pl.pallas_call(functools.partial(kernel, 1.0 / math.sqrt(total)), in_spec...]
where the time goes in v4:
time: 72.8 us; the launch traced here: 72.7 us
  Pallas kernels  67.4 us (93%)
  local copies, waits for them, and re-layouts  4.6 us (6%)
    pallas_call x1, Pallas kernels, local(): pl.pallas_call(functools.partial(kernel, 1.0 / math.sqrt(total)), in_spec...  67.4 us
    unnamed x7, local copies, waits for them, and re-layouts  4.6 us

profile of v4, /device:TPU:1, one launch (start us, length us, event | category | flops | bytes accessed | tf_op | source)
XLA Modules:
  0.0 72.7 jit_solution(13708276978888416348)
XLA Ops:
  0.6 67.4 %shard_map.94 = (bf16[2,8,128,256]{3,2,1,0:T(8,128)(2,1)}, bf16[2,8,128,256]{3,2,1,0:T(8,128)(2,1)}, f32[81,128]{1,0:T(8,128)}) custom-call(s32[2,2]{1,0:T(2,128)} %shift_ref.1, bf16[2,256,8,128]{3,2,1,0:T(8,128)(2,1)} %prev_in.1, bf16[2,256,8,128]{3,2,1,0:T(8,128)(2,1)} %cur_in.1, bf16[2,128,8,128]{3,2,1,0:T(8,128)(2,1)} %cot_in.1, ...), custom_call_target="tpu_custom_call" | custom-call | flops 3000000000 | bytes 8388608 | tf_op jit(solution)/shard_map/pallas_call | solution.py:506
  68.0 0.0 copy-start
  68.1 2.5 %copy.10 = bf16[2,256,8,128]{3,2,1,0:T(8,128)(2,1)} copy(bf16[2,256,8,128]{1,3,2,0:T(8,128)(2,1)} %bitcast.5) | data formatting | bytes 2097152
  70.6 0.0 copy-done
  70.6 0.0 copy-start.1
  70.6 1.5 %copy.11 = bf16[2,256,8,128]{3,2,1,0:T(8,128)(2,1)} copy(bf16[2,256,8,128]{1,3,2,0:T(8,128)(2,1)S(1)} %bitcast.4) | data formatting | bytes 2097152
  72.0 0.0 copy-done.1
  72.0 0.6 copy.13
Async XLA Ops:
  68.0 2.5 %copy-start = (bf16[2,8,128,256]{3,2,1,0:T(8,128)(2,1)S(1)}, bf16[2,8,128,256]{3,2,1,0:T(8,128)(2,1)}, u32[]{:S(2)}) copy-start(bf16[2,8,128,256]{3,2,1,0:T(8,128)(2,1)} %get-tuple-element.7) | copy-start | bytes 3145732
  70.6 1.5 %copy-start.1 = (f32[81,128]{1,0:T(8,128)S(1)}, f32[81,128]{1,0:T(8,128)}, u32[]{:S(2)}) copy-start(f32[81,128]{1,0:T(8,128)} %get-tuple-element.8) | copy-start | bytes 124420

commit v5 on v4

--- a/solution.py
+++ b/solution.py
@@ -53,15 +53,15 @@
     return win, dot(cur, win, NT)
 
 
-def split_product(grads, win):
+def split_grads(grads):
     zero = jnp.zeros((8, 128), F32)
     full = [
         jnp.concatenate([zero, g] if i % 2 else [g, zero], axis=1) for i, g in enumerate(grads)
     ]
-    return dot(jnp.concatenate(full, axis=0).astype(BF), win)
-
-
-def cells_early(p, bb, dy, own, cur_ref, cot_ref, wk, sum_c, act_c, pre_c):
+    return jnp.concatenate(full, axis=0).astype(BF)
+
+
+def cells_early(p, bb, own, cur_ref, cot_ref, wk, sum_c, act_c, pre_c, sum_q):
     win, vol = cell_block(p, bb, lambda i, at: own[i, pl.ds(at, 32), :], cur_ref)
     at = pl.multiple_of(bb * 16, 16)
     pre = dot(cot_ref[p, :, pl.ds(at, 16), :].reshape(128, 128), wk)
@@ -76,7 +76,15 @@
         acts.append(flip8(act))
     act_c[p, bb] = jnp.concatenate(acts, axis=0)
     pre_c[p, bb] = jnp.concatenate(rest, axis=0)
-    sum_c[p, bb] = split_product(grads, win)
+    grad = split_grads(grads)
+    sum_c[p, bb] = dot(grad, win)
+    cur = cur_ref[p, :, pl.ds(at, 16), :].reshape(128, 256)
+    back = dot(grad, cur, TN)
+    for i in range(8):
+        even, odd = back[16 * i : 16 * i + 16], back[128 + 16 * i : 128 + 16 * i + 16]
+        sum_q[p, i, pl.ds(at, 8), :] += even[:8]
+        sum_q[p, i, pl.ds(at + 8, 8), :] = even[8:] + odd[:8]
+        sum_q[p, i, pl.ds(at + 16, 8), :] = odd[8:]
 
 
 def cells_late(p, bb, dy, halo, cur_ref, cot_ref, sum_c, act_c, pre_c, out_ref, acc_ref):
@@ -98,16 +106,36 @@
         acts.append(skew(act, 249 - 16 * y))
     act = jnp.concatenate(acts, axis=0).astype(BF)
     acc_ref[p] += dot(cot_rev.astype(BF), act, TN)
-    out = sum_c[p, bb] + split_product(grads, win)
+    out = sum_c[p, bb] + dot(split_grads(grads), win)
     out_ref[p, :, pl.ds(at, 16), :] = out.astype(BF).reshape(8, 16, 256)
 
 
-def position_block(p, bb, rows_of, pres_of, half_of, prev_ref, spread, masks):
+def rim_positions(p, left, rim_cur, rim_cot, prev_ref, wk, masks, rim_sum):
+    at = pl.multiple_of(jnp.where(left, 112, 0), 16)
+    prev = prev_ref[p, :, pl.ds(at, 16), :].reshape(128, 256)
+    win = rim_cur[p].reshape(64, 256).astype(BF)
+    vol = dot(win, prev, NT)
+    pre = dot(rim_cot[p].reshape(64, 128).astype(BF), wk)
+    mask = jnp.where(left, masks[1], masks[0])
+    grads = []
+    for i in range(8):
+        rows = slice(8 * i, 8 * i + 8)
+        piece = pre[rows] * mask
+        piece = jnp.where(left, skew(piece, 16 * i + 8), skew(piece, 16 * i - 8))[:, :128]
+        grads.append(piece * activation(vol[rows])[1])
+    rim_sum[p] = dot(jnp.concatenate(grads, axis=0).astype(BF), win, TN)
+
+
+def positions_late(
+    p, bb, dy, dx, left, halo, pre_halo, prev_ref, e, masks, sum_q, rim_sum, out_ref
+):
     at = pl.multiple_of(bb * 16, 16)
     prev = prev_ref[p, :, pl.ds(at, 16), :].reshape(128, 256)
-    win = jnp.concatenate([rows_of(i, at)[:24] for i in range(8)], axis=0)
+    win = jnp.concatenate([halo[8 + i, pl.ds(at, 32), :][:24] for i in range(8)], axis=0)
     vol = dot(win, prev, NT)
-    pre = dot(jnp.concatenate([pres_of(i, at)[:24] for i in range(8)], axis=0), spread)
+    pre = dot(
+        jnp.concatenate([pre_halo[i, pl.ds(at, 32), :][:24] for i in range(8)], axis=0), e
+    )
     grads = []
     for i in range(8):
         for g in range(3):
@@ -116,42 +144,27 @@
             if g != 1:
                 piece = piece * masks[g // 2]
             piece = skew(piece, 16 * i + 8 * (g - 1))
-            grads.append(half_of(i, piece) * activation(vol[rows])[1])
-    return dot(jnp.concatenate(grads, axis=0).astype(BF), win, TN)
-
-
-def positions_early(p, bb, dy, own, own_cot, prev_ref, wk, masks, sum_p):
-    sum_p[p, bb] = position_block(
-        p, bb, lambda i, at: own[8 + i, pl.ds(at, 32), :],
-        lambda i, at: own_cot[i, pl.ds(at, 32), :], lambda i, x: x[:, :128],
-        prev_ref, wk, masks,
-    )
-
-
-def positions_late(p, bb, dy, halo, pre_halo, prev_ref, e, masks, sum_p, out_ref):
-    out = sum_p[p, bb] + position_block(
-        p, bb, lambda i, at: halo[8 + i, pl.ds(at, 32), :],
-        lambda i, at: pre_halo[i, pl.ds(at, 32), :],
-        lambda i, x: jnp.where(i < 4 + dy, x[:, 128:], x[:, :128]),
-        prev_ref, e, masks,
-    )
-    at = pl.multiple_of(bb * 16, 16)
-    out_ref[p, :, pl.ds(at, 16), :] = out.astype(BF).reshape(8, 16, 256)
+            piece = jnp.where(i < 4 + dy, piece[:, 128:], piece[:, :128])
+            grads.append(piece * activation(vol[rows])[1])
+    out = dot(jnp.concatenate(grads, axis=0).astype(BF), win, TN)
+    own = pltpu.roll(sum_q[p, :, pl.ds(at, 24), :], (20 + dx) % 24, 1)[:, :16].reshape(128, 256)
+    rim = jnp.where(bb == jnp.where(left, 7, 0), 1.0, 0.0) * rim_sum[p]
+    out_ref[p, :, pl.ds(at, 16), :] = (out + own + rim).astype(BF).reshape(8, 16, 256)
 
 
 def kernel(
     norm, shift_ref, prev_in, cur_in, cot_in, w_ref, e_ref, eye_ref,
     gc_ref, gp_ref, gw_ref,
     prev_ref, cur_ref, cot_ref, flat0, flat1, msg_r, rim_s, rim_r,
-    edge_s, edge_r0, edge_r1, edge_cot_s, edge_cot_r, own0, own1, own_cot0, own_cot1, own_pre,
+    edge_s, edge_r0, edge_r1, edge_cot_s, edge_cot_r, own0, own1, cot_x, own_pre, rim_cur, rim_cot,
     msg, tri_s, tri_r, halo0, halo1, pre_halo0, pre_halo1,
-    sum_c, act_c, pre_c, sum_p, acc, ar0, ar1, ar2, ar3,
+    sum_c, act_c, pre_c, sum_q, rim_sum, acc, ar0, ar1, ar2, ar3,
     side_ss, side_rs, row_ss, row_rs, s1, r1, s2, r2, s3, r3,
 ):
     row, col = lax.axis_index("row"), lax.axis_index("col")
     last = lax.axis_size("row") - 1
     left = col == 0
-    owns, own_cots = (own0, own1), (own_cot0, own_cot1)
+    owns = (own0, own1)
     halos, pre_halos = (halo0, halo1), (pre_halo0, pre_halo1)
     g1, g2 = (row % 4) * 2 + col, row // 4
 
@@ -219,14 +232,34 @@
     def picked(flat, y, channels):
         return flat[pl.ds(y, channels, stride=8), :].astype(BF)
 
+    def aligner(offset):
+        take = iota((WIDE, 128), 1) + 8 == iota((WIDE, 128), 0) + offset
+        return jnp.where(take, 1.0, 0.0).astype(BF)
+
+    def rim_aligner(rows, first, offset, slots):
+        far = jnp.where(left, 136, 0)
+        at, in_at = iota((rows, 16), 0) + offset, iota((rows, 16), 1)
+        at = at + (first if rows == 8 else jnp.where(iota((rows, 16), 0) < 16, 0, 112))
+        ok = (in_at >= slots) & (in_at < slots + 8) & (in_at - slots + far == at)
+        return jnp.where(ok, 1.0, 0.0).astype(BF)
+
     def turn(p):
-        for source, target, flat in (
-            (prev_in, prev_ref, flat0), (cur_in, cur_ref, flat1), (cot_in, cot_ref, flat0)
-        ):
-            channels = source.shape[1]
-            spread_rows(flat, source[p].astype(F32))
-            for y in range(8):
-                target[p, y] = dot(ident, picked(flat, y, channels), NT).astype(BF)
+        dx = shift_ref[p, 1]
+        both_p = jnp.concatenate([ident, aligner(4 + dx)], axis=0)
+        both_c = jnp.concatenate([ident, aligner(4 - dx)], axis=0)
+        spread_rows(flat0, prev_in[p].astype(F32))
+        for y in range(8):
+            x = dot(both_p, picked(flat0, y, 256), NT).astype(BF)
+            prev_ref[p, y] = x[:128]
+            owns[p][y] = x[128:]
+        spread_rows(flat1, cur_in[p].astype(F32))
+        for y in range(8):
+            cur_ref[p, y] = dot(ident, picked(flat1, y, 256), NT).astype(BF)
+        spread_rows(flat0, cot_in[p].astype(F32))
+        for y in range(8):
+            x = dot(both_c, picked(flat0, y, 128), NT)
+            cot_ref[p, y] = x[:128].astype(BF)
+            cot_x[p, y] = x[128:]
 
     start = jnp.where(left, 112, 0)
 
@@ -264,34 +297,30 @@
     wks = [pltpu.roll(wk, turns[p], 1).astype(BF) for p in range(2)]
     sub, lane = iota((8, 256), 0), iota((8, 256), 1) % 16
     masks = (jnp.where(lane >= 8 - sub, 1.0, 0.0), jnp.where(lane < 8 - sub, 1.0, 0.0))
-    far = jnp.where(left, 136, 0)
     tri_lane = iota((WIDE, 128), 1)
     acc[...] = jnp.zeros_like(acc)
-
-    def aligner(offset):
-        take = iota((WIDE, 128), 1) + 8 == iota((WIDE, 128), 0) + offset
-        out = [jnp.where(take, 1.0, 0.0).astype(BF)]
-        at, in_at = iota((WIDE, 16), 0) + offset, iota((WIDE, 16), 1)
-        for slots in (0, 8):
-            ok = (in_at >= slots) & (in_at < slots + 8) & (in_at - slots + far == at)
-            out.append(jnp.where(ok, 1.0, 0.0).astype(BF))
-        return out
+    sum_q[:, :, 0:8] = jnp.zeros((2, 8, 8, 256), F32)
 
     def join(p):
         dy, dx = shift_ref[p, 0], shift_ref[p, 1]
-        own, own_cot, edge_r = owns[p], own_cots[p], (edge_r0, edge_r1)[p]
-        take_p, rim_p, _ = aligner(4 + dx)
-        take_c, rim_c0, rim_c1 = aligner(4 - dx)
+        own, edge_r = owns[p], (edge_r0, edge_r1)[p]
+        first = jnp.where(left, 128, 0)
+        rim_p = rim_aligner(32, 0, 4 + dx, 0)
+        rim_c = [rim_aligner(32, 0, 4 - dx, slots) for slots in (0, 8)]
+        rim_8 = [rim_aligner(8, first, 4 - dx, slots) for slots in (0, 8)]
         for k in range(2):
             side(p, k).wait()
         for y in range(8):
-            edge = edge_r[y]
-            own[y] = (dot(take_p, prev_ref[p, y]) + dot(rim_p, edge)).astype(BF)
-            own[8 + y] = (dot(take_c, cur_ref[p, y]) + dot(rim_c1, edge)).astype(BF)
-            rim = dot(rim_c1 if y % 2 else rim_c0, edge_cot_r[p, y // 2])
-            aligned = (dot(take_c, cot_ref[p, y]) + rim).astype(BF)
-            own_cot[y] = aligned
-            own_pre[y] = dot(aligned, w9)
+            edge, edge_cot = edge_r[y], edge_cot_r[p, y // 2]
+            rim = dot(rim_p, edge)
+            own[y, 0:16] = (own[y, 0:16].astype(F32) + rim[:16]).astype(BF)
+            own[y, 128:144] = (own[y, 128:144].astype(F32) + rim[16:]).astype(BF)
+            rim_cur[p, y] = dot(rim_8[1], edge)
+            rim_cot[p, y] = dot(rim_8[y % 2], edge_cot)
+            rim = dot(rim_c[y % 2], edge_cot)
+            x = cot_x[p, y]
+            x = jnp.concatenate([x[:16] + rim[:16], x[16:128], x[128:] + rim[16:]], axis=0)
+            own_pre[y] = dot(x.astype(BF), w9)
 
         def tile(s, up):
             is_prev = (s < 4 + dy) if up else (s >= 4 + dy)
@@ -325,8 +354,9 @@
     def arrive(p):
         dy, dx = shift_ref[p, 0], shift_ref[p, 1]
         halo = halos[p]
-        take_p, *rim_p = aligner(4 + dx)
-        take_c, *rim_c = aligner(4 - dx)
+        take_p, take_c = aligner(4 + dx), aligner(4 - dx)
+        rim_p = [rim_aligner(32, 0, 4 + dx, slots) for slots in (0, 8)]
+        rim_c = [rim_aligner(32, 0, 4 - dx, slots) for slots in (0, 8)]
 
         @pl.when(row > 0)
         def _():
@@ -367,10 +397,13 @@
             edge_c = jnp.where(low, down, up).astype(BF)
             for h in range(2):
                 s = 2 * k + h
-                x = dot(take_p, picked(flat0, s, 256), NT) + dot(rim_p[h], edge_p)
-                halo[s] = x.astype(BF)
-                x = dot(take_c, picked(flat1, s, 256), NT) + dot(rim_c[h], edge_c)
-                halo[8 + s] = x.astype(BF)
+                for to, take, flat, rims, edge in (
+                    (s, take_p, flat0, rim_p, edge_p), (8 + s, take_c, flat1, rim_c, edge_c)
+                ):
+                    x, rim = dot(take, picked(flat, s, 256), NT), dot(rims[h], edge)
+                    halo[to, 0:16] = (x[:16] + rim[:16]).astype(BF)
+                    halo[to, 16:128] = x[16:128].astype(BF)
+                    halo[to, 128:144] = (x[128:] + rim[16:]).astype(BF)
         for s in range(4):
             up, down = tri_r[p, 0, s].astype(F32), tri_r[p, 1, s].astype(F32)
             pre_halos[p][s] = jnp.where(s < 4 + dy, down, up).astype(BF)
@@ -386,16 +419,13 @@
         lax.fori_loop(lo, hi, body, 0)
 
     def early(p):
-        dy = shift_ref[p, 0]
-
         def work(i):
             for bb in (2 * i, 2 * i + 1):
                 cells_early(
-                    p, bb, dy, owns[p], cur_ref, cot_ref, wks[p], sum_c, act_c, pre_c)
-                positions_early(
-                    p, bb, dy, owns[p], own_cots[p], prev_ref, wks[p], masks, sum_p)
+                    p, bb, owns[p], cur_ref, cot_ref, wks[p], sum_c, act_c, pre_c, sum_q)
 
         loop(0, 4, work)
+        rim_positions(p, left, rim_cur, rim_cot, prev_ref, wks[p], masks, rim_sum)
 
     def late_cells(p, bb):
         cells_late(
@@ -403,7 +433,8 @@
 
     def late_positions(p, bb):
         positions_late(
-            p, bb, shift_ref[p, 0], halos[p], pre_halos[p], prev_ref, e, masks, sum_p, gp_ref)
+            p, bb, shift_ref[p, 0], shift_ref[p, 1], left, halos[p], pre_halos[p], prev_ref, e,
+            masks, sum_q, rim_sum, gp_ref)
 
     def late(i):
         for bb in (2 * i, 2 * i + 1):
@@ -518,16 +549,16 @@
             v((2, 2, 256, 8, 128), BF), v((2, 2, 4, 16, 256), BF), v((2, 2, 4, 16, 256), BF),
             v((2, 8, 16, 256), BF), v((8, 16, 256), BF), v((8, 16, 256), BF),
             v((2, 4, 16, 128), BF), v((2, 4, 16, 128), BF),
-            v((16, WIDE, 256), BF), v((16, WIDE, 256), BF),
-            v((8, WIDE, 128), BF), v((8, WIDE, 128), BF),
-            v((8, WIDE, 128), F32),
+            v((8, WIDE, 256), BF), v((8, WIDE, 256), BF),
+            v((2, 8, WIDE, 128), F32), v((8, WIDE, 128), F32),
+            v((2, 8, 8, 256), F32), v((2, 8, 8, 128), F32),
             v((2, 2, 256, 8, 128), BF),
             v((2, 2, 4, WIDE, 128), BF), v((2, 2, 4, WIDE, 128), BF),
             v((16, WIDE, 256), BF), v((16, WIDE, 256), BF),
             v((8, WIDE, 128), BF), v((8, WIDE, 128), BF),
             v((2, 8, 128, 256), F32),
             v((2, 8, 128, 128), F32), v((2, 8, 128, 128), F32),
-            v((2, 8, 128, 256), F32),
+            v((2, 8, WIDE, 256), F32), v((2, 128, 256), F32),
             v((2, 128, 256), F32),
             v((128, 128), F32), v((8, 16, 128), F32), v((16, 16, 128), F32), v((8, 16, 128), F32),
             dma((2, 2)), dma((2, 2)), dma((2, 2, 3)), dma((2, 2, 3)),

time: 72.8 us -> 71.5 us (0.982)
  Pallas kernels: 67.4 us -> 66.1 us
    pallas_call x1, Pallas kernels: 67.4 us -> 66.1 us  [local(): pl.pallas_call(functools.partial(kernel, 1.0 / math.sqrt(total)), in_spec...]
where the time goes in v5:
time: 71.5 us; the launch traced here: 71.3 us
  Pallas kernels  66.1 us (92%)
  local copies, waits for them, and re-layouts  4.6 us (6%)
    pallas_call x1, Pallas kernels, local(): pl.pallas_call(functools.partial(kernel, 1.0 / math.sqrt(total)), in_spec...  66.1 us
    unnamed x7, local copies, waits for them, and re-layouts  4.6 us

profile of v5, /device:TPU:1, one launch (start us, length us, event | category | flops | bytes accessed | tf_op | source)
XLA Modules:
  0.0 71.3 jit_solution(16546365395527199861)
XLA Ops:
  0.6 66.1 %shard_map.94 = (bf16[2,8,128,256]{3,2,1,0:T(8,128)(2,1)}, bf16[2,8,128,256]{3,2,1,0:T(8,128)(2,1)}, f32[81,128]{1,0:T(8,128)}) custom-call(s32[2,2]{1,0:T(2,128)} %shift_ref.1, bf16[2,256,8,128]{3,2,1,0:T(8,128)(2,1)} %prev_in.1, bf16[2,256,8,128]{3,2,1,0:T(8,128)(2,1)} %cur_in.1, bf16[2,128,8,128]{3,2,1,0:T(8,128)(2,1)} %cot_in.1, ...), custom_call_target="tpu_custom_call" | custom-call | flops 3000000000 | bytes 8388608 | tf_op jit(solution)/shard_map/pallas_call | solution.py:537
  66.7 0.0 copy-start
  66.7 2.5 %copy.10 = bf16[2,256,8,128]{3,2,1,0:T(8,128)(2,1)} copy(bf16[2,256,8,128]{1,3,2,0:T(8,128)(2,1)} %bitcast.5) | data formatting | bytes 2097152
  69.2 0.0 copy-done
  69.2 0.0 copy-start.1
  69.2 1.5 %copy.11 = bf16[2,256,8,128]{3,2,1,0:T(8,128)(2,1)} copy(bf16[2,256,8,128]{1,3,2,0:T(8,128)(2,1)S(1)} %bitcast.4) | data formatting | bytes 2097152
  70.7 0.0 copy-done.1
  70.7 0.6 copy.13
Async XLA Ops:
  66.7 2.5 %copy-start = (bf16[2,8,128,256]{3,2,1,0:T(8,128)(2,1)S(1)}, bf16[2,8,128,256]{3,2,1,0:T(8,128)(2,1)}, u32[]{:S(2)}) copy-start(bf16[2,8,128,256]{3,2,1,0:T(8,128)(2,1)} %get-tuple-element.7) | copy-start | bytes 3145732
  69.2 1.5 %copy-start.1 = (f32[81,128]{1,0:T(8,128)S(1)}, f32[81,128]{1,0:T(8,128)}, u32[]{:S(2)}) copy-start(f32[81,128]{1,0:T(8,128)} %get-tuple-element.8) | copy-start | bytes 124420

commit v6 on v5

--- a/solution.py
+++ b/solution.py
@@ -127,14 +127,14 @@
 
 
 def positions_late(
-    p, bb, dy, dx, left, halo, pre_halo, prev_ref, e, masks, sum_q, rim_sum, out_ref
+    p, bb, dx, left, halo, pre_halo, prev_ref, e_fold, masks, sum_q, rim_sum, out_ref
 ):
     at = pl.multiple_of(bb * 16, 16)
     prev = prev_ref[p, :, pl.ds(at, 16), :].reshape(128, 256)
     win = jnp.concatenate([halo[8 + i, pl.ds(at, 32), :][:24] for i in range(8)], axis=0)
     vol = dot(win, prev, NT)
     pre = dot(
-        jnp.concatenate([pre_halo[i, pl.ds(at, 32), :][:24] for i in range(8)], axis=0), e
+        jnp.concatenate([pre_halo[i, pl.ds(at, 32), :][:24] for i in range(8)], axis=0), e_fold
     )
     grads = []
     for i in range(8):
@@ -142,9 +142,9 @@
             rows = slice(24 * i + 8 * g, 24 * i + 8 * g + 8)
             piece = pre[rows]
             if g != 1:
-                piece = piece * masks[g // 2]
-            piece = skew(piece, 16 * i + 8 * (g - 1))
-            piece = jnp.where(i < 4 + dy, piece[:, 128:], piece[:, :128])
+                piece = piece * masks[g // 2][:, :128]
+            shift = (16 * i + 8 * (g - 1)) % 128
+            piece = pltpu.roll(piece, shift, 1, stride=1, stride_axis=0)
             grads.append(piece * activation(vol[rows])[1])
     out = dot(jnp.concatenate(grads, axis=0).astype(BF), win, TN)
     own = pltpu.roll(sum_q[p, :, pl.ds(at, 24), :], (20 + dx) % 24, 1)[:, :16].reshape(128, 256)
@@ -153,23 +153,35 @@
 
 
 def kernel(
-    norm, shift_ref, prev_in, cur_in, cot_in, w_ref, e_ref, eye_ref,
-    gc_ref, gp_ref, gw_ref,
+    norm, shift_ref, prev_hbm, cur_hbm, cot_hbm, w_ref, e_ref, eye_ref,
+    gc_hbm, gp_hbm, gw_ref,
+    prev_in, cur_in, cot_in, gc_ref, gp_ref,
     prev_ref, cur_ref, cot_ref, flat0, flat1, msg_r, rim_s, rim_r,
     edge_s, edge_r0, edge_r1, edge_cot_s, edge_cot_r, own0, own1, cot_x, own_pre, rim_cur, rim_cot,
     msg, tri_s, tri_r, halo0, halo1, pre_halo0, pre_halo1,
-    sum_c, act_c, pre_c, sum_q, rim_sum, acc, ar0, ar1, ar2, ar3,
-    side_ss, side_rs, row_ss, row_rs, s1, r1, s2, r2, s3, r3,
+    sum_c, act_c, pre_c, sum_q, rim_sum, acc, ar0, ar1, ar2, ar3, ar4,
+    side_ss, side_rs, row_ss, row_rs, s1, r1, s2, r2, s3, r3, s4, r4, load_sem, store_sem,
 ):
     row, col = lax.axis_index("row"), lax.axis_index("col")
     last = lax.axis_size("row") - 1
     left = col == 0
     owns = (own0, own1)
     halos, pre_halos = (halo0, halo1), (pre_halo0, pre_halo1)
-    g1, g2 = (row % 4) * 2 + col, row // 4
-
-    def member(a, b):
-        return (b * 4 + a // 2, a % 2)
+    g1, g2, g3 = (row % 4) * 2 + col, (row // 4) % 4, row // 16
+
+    def member(a, b, c):
+        return ((c * 4 + b) * 4 + a // 2, a % 2)
+
+    loads, stores = [], []
+    for p in range(2):
+        for source, target in ((prev_hbm, prev_in), (cur_hbm, cur_in), (cot_hbm, cot_in)):
+            at = load_sem.at[len(loads)]
+            loads.append(pltpu.make_async_copy(source.at[p], target.at[p], at))
+        for source, target in ((gc_ref, gc_hbm), (gp_ref, gp_hbm)):
+            at = store_sem.at[len(stores)]
+            stores.append(pltpu.make_async_copy(source.at[p], target.at[p], at))
+    for copy in loads:
+        copy.start()
 
     barrier = pltpu.get_barrier_semaphore()
 
@@ -177,9 +189,10 @@
         pl.semaphore_signal(barrier, inc=1, device_id=target, device_id_type=MESH)
 
     for d in range(1, 8):
-        greet(member((g1 + d) % 8, g2))
-    for d in range(1, 16):
-        greet(member(g1, (g2 + d) % 16))
+        greet(member((g1 + d) % 8, g2, g3))
+    for d in range(1, 4):
+        greet(member(g1, (g2 + d) % 4, g3))
+        greet(member(g1, g2, (g3 + d) % 4))
     greet(((row + 1) % (last + 1), col))
     greet(((row + last) % (last + 1), col))
 
@@ -236,28 +249,33 @@
         take = iota((WIDE, 128), 1) + 8 == iota((WIDE, 128), 0) + offset
         return jnp.where(take, 1.0, 0.0).astype(BF)
 
-    def rim_aligner(rows, first, offset, slots):
-        far = jnp.where(left, 136, 0)
-        at, in_at = iota((rows, 16), 0) + offset, iota((rows, 16), 1)
-        at = at + (first if rows == 8 else jnp.where(iota((rows, 16), 0) < 16, 0, 112))
-        ok = (in_at >= slots) & (in_at < slots + 8) & (in_at - slots + far == at)
-        return jnp.where(ok, 1.0, 0.0).astype(BF)
-
-    def turn(p):
-        dx = shift_ref[p, 1]
-        both_p = jnp.concatenate([ident, aligner(4 + dx)], axis=0)
-        both_c = jnp.concatenate([ident, aligner(4 - dx)], axis=0)
+    def rim_place(tile, offset):
+        tile = pltpu.roll(tile, offset % 8, tile.ndim - 2)
+        at = iota(tile.shape, tile.ndim - 2)
+        keep = jnp.where(left, at, -1 - at) >= jnp.where(left, offset, -offset)
+        return jnp.where(keep, tile, 0.0)
+
+    def rim_add(x, rim):
+        zero = jnp.zeros_like(rim)
+        low, high = jnp.where(left, zero, rim), jnp.where(left, rim, zero)
+        return jnp.concatenate([x[:8] + low, x[8:128], x[128:136] + high, x[136:]], axis=0)
+
+    def turn_prev(p):
+        both = jnp.concatenate([ident, aligner(4 + shift_ref[p, 1])], axis=0)
         spread_rows(flat0, prev_in[p].astype(F32))
         for y in range(8):
-            x = dot(both_p, picked(flat0, y, 256), NT).astype(BF)
+            x = dot(both, picked(flat0, y, 256), NT).astype(BF)
             prev_ref[p, y] = x[:128]
             owns[p][y] = x[128:]
+
+    def turn_cells(p):
+        both = jnp.concatenate([ident, aligner(4 - shift_ref[p, 1])], axis=0)
         spread_rows(flat1, cur_in[p].astype(F32))
         for y in range(8):
             cur_ref[p, y] = dot(ident, picked(flat1, y, 256), NT).astype(BF)
         spread_rows(flat0, cot_in[p].astype(F32))
         for y in range(8):
-            x = dot(both_c, picked(flat0, y, 128), NT)
+            x = dot(both, picked(flat0, y, 128), NT)
             cot_ref[p, y] = x[:128].astype(BF)
             cot_x[p, y] = x[128:]
 
@@ -279,19 +297,26 @@
         for k in range(2):
             side(p, k).start()
 
+    for copy in loads[:2]:
+        copy.wait()
     pack(0)
-    pl.semaphore_wait(barrier, 24)
+    pl.semaphore_wait(barrier, 15)
     send(0, 0)
-    turn(0)
+    for copy in loads[2:]:
+        copy.wait()
+    turn_prev(0)
+    turn_cells(0)
     edges(0)
     pack(1)
-    turn(1)
+    turn_prev(1)
+    turn_cells(1)
     edges(1)
 
     w81 = w_ref[...]
     e = e_ref[...]
     w9 = dot(w81, eye_ref[...], TN).astype(BF)
     wk = dot(w9, e)
+    e_fold = (e[:, :128].astype(F32) + e[:, 128:].astype(F32)).astype(BF)
     turns = [(16 * (shift_ref[p, 0] + 12)) % 256 for p in range(2)]
     back = [(16 * (4 - shift_ref[p, 0])) % 256 for p in range(2)]
     wks = [pltpu.roll(wk, turns[p], 1).astype(BF) for p in range(2)]
@@ -304,23 +329,20 @@
     def join(p):
         dy, dx = shift_ref[p, 0], shift_ref[p, 1]
         own, edge_r = owns[p], (edge_r0, edge_r1)[p]
-        first = jnp.where(left, 128, 0)
-        rim_p = rim_aligner(32, 0, 4 + dx, 0)
-        rim_c = [rim_aligner(32, 0, 4 - dx, slots) for slots in (0, 8)]
-        rim_8 = [rim_aligner(8, first, 4 - dx, slots) for slots in (0, 8)]
         for k in range(2):
             side(p, k).wait()
         for y in range(8):
-            edge, edge_cot = edge_r[y], edge_cot_r[p, y // 2]
-            rim = dot(rim_p, edge)
-            own[y, 0:16] = (own[y, 0:16].astype(F32) + rim[:16]).astype(BF)
-            own[y, 128:144] = (own[y, 128:144].astype(F32) + rim[16:]).astype(BF)
-            rim_cur[p, y] = dot(rim_8[1], edge)
-            rim_cot[p, y] = dot(rim_8[y % 2], edge_cot)
-            rim = dot(rim_c[y % 2], edge_cot)
-            x = cot_x[p, y]
-            x = jnp.concatenate([x[:16] + rim[:16], x[16:128], x[128:] + rim[16:]], axis=0)
-            own_pre[y] = dot(x.astype(BF), w9)
+            edge = edge_r[y].astype(F32)
+            rim = rim_place(edge[:8], 4 - dx)
+            zero = jnp.zeros_like(rim)
+            for at, piece in ((0, jnp.where(left, zero, rim)), (128, jnp.where(left, rim, zero))):
+                tile = own[y, at : at + 16].astype(F32) + jnp.concatenate([piece, zero], axis=0)
+                own[y, at : at + 16] = tile.astype(BF)
+            rim_cur[p, y] = rim_place(edge[8:], 4 + dx)
+            at = 8 * (y % 2)
+            rim = rim_place(edge_cot_r[p, y // 2].astype(F32)[at : at + 8], 4 + dx)
+            rim_cot[p, y] = rim
+            own_pre[y] = dot(rim_add(cot_x[p, y], rim).astype(BF), w9)
 
         def tile(s, up):
             is_prev = (s < 4 + dy) if up else (s >= 4 + dy)
@@ -355,30 +377,21 @@
         dy, dx = shift_ref[p, 0], shift_ref[p, 1]
         halo = halos[p]
         take_p, take_c = aligner(4 + dx), aligner(4 - dx)
-        rim_p = [rim_aligner(32, 0, 4 + dx, slots) for slots in (0, 8)]
-        rim_c = [rim_aligner(32, 0, 4 - dx, slots) for slots in (0, 8)]
-
-        @pl.when(row > 0)
-        def _():
-            for k in range(3):
-                along(p, 1, k).wait_recv()
-
-        @pl.when(row == 0)
-        def _():
-            msg_r[p, 1] = jnp.zeros((256, 8, 128), BF)
-            rim_r[p, 1] = jnp.zeros((4, 16, 256), BF)
-            tri_r[p, 1] = jnp.zeros((4, WIDE, 128), BF)
-
-        @pl.when(row < last)
-        def _():
-            for k in range(3):
-                along(p, 0, k).wait_recv()
-
-        @pl.when(row == last)
-        def _():
-            msg_r[p, 0] = jnp.zeros((256, 8, 128), BF)
-            rim_r[p, 0] = jnp.zeros((4, 16, 256), BF)
-            tri_r[p, 0] = jnp.zeros((4, WIDE, 128), BF)
+
+        def receive(k, buffer):
+            for way, edge_row in ((1, 0), (0, last)):
+
+                @pl.when(row != edge_row)
+                def _():
+                    along(p, way, k).wait_recv()
+
+                @pl.when(row == edge_row)
+                def _():
+                    part = buffer.at[p, way]
+                    part[...] = jnp.zeros(part.shape, BF)
+
+        for k, buffer in enumerate((msg_r, rim_r, tri_r)):
+            receive(k, buffer)
 
         def sort(i, carry):
             at = pl.ds(pl.multiple_of(i * 16, 16), 16)
@@ -390,26 +403,27 @@
             return carry
 
         lax.fori_loop(0, 16, sort, 0)
-        for k in range(4):
-            up, down = rim_r[p, 0, k].astype(F32), rim_r[p, 1, k].astype(F32)
-            low = 2 * k + iota((16, 256), 0) // 8 < 4 + dy
-            edge_p = jnp.where(low, up, down).astype(BF)
-            edge_c = jnp.where(low, down, up).astype(BF)
-            for h in range(2):
-                s = 2 * k + h
-                for to, take, flat, rims, edge in (
-                    (s, take_p, flat0, rim_p, edge_p), (8 + s, take_c, flat1, rim_c, edge_c)
-                ):
-                    x, rim = dot(take, picked(flat, s, 256), NT), dot(rims[h], edge)
-                    halo[to, 0:16] = (x[:16] + rim[:16]).astype(BF)
-                    halo[to, 16:128] = x[16:128].astype(BF)
-                    halo[to, 128:144] = (x[128:] + rim[16:]).astype(BF)
+        for s in range(8):
+            at = 8 * (s % 2)
+            up = rim_r[p, 0, s // 2].astype(F32)[at : at + 8]
+            down = rim_r[p, 1, s // 2].astype(F32)[at : at + 8]
+            low = s < 4 + dy
+            x = dot(take_p, picked(flat0, s, 256), NT)
+            rim = rim_place(jnp.where(low, up, down), 4 - dx)
+            halo[s] = rim_add(x, rim).astype(BF)
+            x = dot(take_c, picked(flat1, s, 256), NT)
+            rim = rim_place(jnp.where(low, down, up), 4 + dx)
+            halo[8 + s] = rim_add(x, rim).astype(BF)
         for s in range(4):
             up, down = tri_r[p, 0, s].astype(F32), tri_r[p, 1, s].astype(F32)
-            pre_halos[p][s] = jnp.where(s < 4 + dy, down, up).astype(BF)
+            near = tri_lane >= 9 * (8 - s)
+            x = jnp.where(near == (s < 4 + dy), jnp.where(s < 4 + dy, down, up), 0.0)
+            pre_halos[p][s] = x.astype(BF)
             down = pltpu.roll(down, 9 * (s + 1), 1)
             up = pltpu.roll(up, 128 - 9 * (8 - s), 1)
-            pre_halos[p][7 - s] = jnp.where(7 - s < 4 + dy, down, up).astype(BF)
+            near = tri_lane >= 9 * (s + 1)
+            x = jnp.where(near == (7 - s < 4 + dy), jnp.where(7 - s < 4 + dy, down, up), 0.0)
+            pre_halos[p][7 - s] = jnp.where(tri_lane < 81, x, 0.0).astype(BF)
 
     def loop(lo, hi, work):
         def body(bb, carry):
@@ -433,8 +447,8 @@
 
     def late_positions(p, bb):
         positions_late(
-            p, bb, shift_ref[p, 0], shift_ref[p, 1], left, halos[p], pre_halos[p], prev_ref, e,
-            masks, sum_q, rim_sum, gp_ref)
+            p, bb, shift_ref[p, 1], left, halos[p], pre_halos[p], prev_ref, e_fold, masks,
+            sum_q, rim_sum, gp_ref)
 
     def late(i):
         for bb in (2 * i, 2 * i + 1):
@@ -445,8 +459,12 @@
     early(1)
     arrive(0)
     loop(0, 4, late)
+    stores[0].start()
+    stores[1].start()
     arrive(1)
     loop(0, 2, lambda i: [late_cells(1, 4 * i + k) for k in range(4)])
+
+    stores[2].start()
 
     turned = (pltpu.roll(acc[0], back[0], 1) + pltpu.roll(acc[1], back[1], 1)).T
     for u in range(9):
@@ -460,21 +478,28 @@
         peer = (g1 + d) % 8
         return pltpu.make_async_remote_copy(
             src_ref=share(ar0, peer), dst_ref=ar1.at[g1], send_sem=s1.at[peer],
-            recv_sem=r1.at[g1], device_id=member(peer, g2), device_id_type=MESH,
+            recv_sem=r1.at[g1], device_id=member(peer, g2, g3), device_id_type=MESH,
         )
 
     def second(d):
-        peer = (g2 + d) % 16
+        peer = (g2 + d) % 4
         return pltpu.make_async_remote_copy(
             src_ref=ar2.at[g2], dst_ref=ar2.at[g2], send_sem=s2.at[peer],
-            recv_sem=r2.at[g2], device_id=member(g1, peer), device_id_type=MESH,
+            recv_sem=r2.at[g2], device_id=member(g1, peer, g3), device_id_type=MESH,
         )
 
     def third(d):
+        peer = (g3 + d) % 4
+        return pltpu.make_async_remote_copy(
+            src_ref=ar3.at[g3], dst_ref=ar3.at[g3], send_sem=s3.at[peer],
+            recv_sem=r3.at[g3], device_id=member(g1, g2, peer), device_id_type=MESH,
+        )
+
+    def fourth(d):
         peer = (g1 + d) % 8
         return pltpu.make_async_remote_copy(
-            src_ref=ar3.at[g1], dst_ref=ar3.at[g1], send_sem=s3.at[peer],
-            recv_sem=r3.at[g1], device_id=member(peer, g2), device_id_type=MESH,
+            src_ref=ar4.at[g1], dst_ref=ar4.at[g1], send_sem=s4.at[peer],
+            recv_sem=r4.at[g1], device_id=member(peer, g2, g3), device_id_type=MESH,
         )
 
     def got(buffer, sends, receives, source):
@@ -483,28 +508,41 @@
             recv_sem=receives.at[source], device_id=(row, 1 - col), device_id_type=MESH,
         ).wait_recv()
 
+    def some_positions(lo, hi):
+        loop(0, 1, lambda i: [late_positions(1, k) for k in range(lo, hi)])
+
     for d in range(1, 8):
         first(d).start()
-    loop(0, 1, lambda i: [late_positions(1, k) for k in range(3)])
+    some_positions(0, 2)
     ar1[g1] = ar0[pl.ds(pl.multiple_of(g1 * 16, 16), 16)]
     for d in range(1, 8):
         first(d).wait_send()
         got(ar1, s1, r1, (g1 + d) % 8)
     ar2[g2] = jnp.sum(ar1[...], axis=0)
-    for d in range(1, 16):
+    for d in range(1, 4):
         second(d).start()
-    loop(0, 1, lambda i: [late_positions(1, 3 + k) for k in range(3)])
-    for d in range(1, 16):
+    some_positions(2, 4)
+    for d in range(1, 4):
         second(d).wait_send()
-        got(ar2, s2, r2, (g2 + d) % 16)
-    ar3[g1] = jnp.sum(ar2[...], axis=0)
+        got(ar2, s2, r2, (g2 + d) % 4)
+    ar3[g3] = jnp.sum(ar2[...], axis=0)
+    for d in range(1, 4):
+        third(d).start()
+    some_positions(4, 6)
+    for d in range(1, 4):
+        third(d).wait_send()
+        got(ar3, s3, r3, (g3 + d) % 4)
+    ar4[g1] = jnp.sum(ar3[...], axis=0)
     for d in range(1, 8):
-        third(d).start()
-    loop(0, 1, lambda i: [late_positions(1, 6 + k) for k in range(2)])
+        fourth(d).start()
+    some_positions(6, 8)
+    stores[3].start()
     for d in range(1, 8):
-        third(d).wait_send()
-        got(ar3, s3, r3, (g1 + d) % 8)
-    gw_ref[...] = ar3[...].reshape(128, 128)[:81] * norm
+        fourth(d).wait_send()
+        got(ar4, s4, r4, (g1 + d) % 8)
+    gw_ref[...] = ar4[...].reshape(128, 128)[:81] * norm
+    for copy in stores:
+        copy.wait()
 
     for p in range(2):
         for k in range(3):
@@ -532,18 +570,21 @@
     eye = jnp.asarray(np.eye(81, 128), BF)
     total = pairs * rows * lax.axis_size("row") * cols * lax.axis_size("col")
     vmem = pl.BlockSpec(memory_space=pltpu.VMEM)
+    hbm = pl.BlockSpec(memory_space=pl.ANY)
     dma = pltpu.SemaphoreType.DMA
     v = pltpu.VMEM
     gc, gp, gw = pl.pallas_call(
         functools.partial(kernel, 1.0 / math.sqrt(total)),
-        in_specs=[pl.BlockSpec(memory_space=pltpu.SMEM)] + [vmem] * 6,
-        out_specs=[vmem] * 3,
+        in_specs=[pl.BlockSpec(memory_space=pltpu.SMEM)] + [hbm] * 3 + [vmem] * 3,
+        out_specs=[hbm, hbm, vmem],
         out_shape=[
             jax.ShapeDtypeStruct((2, 8, 128, 256), BF),
             jax.ShapeDtypeStruct((2, 8, 128, 256), BF),
             jax.ShapeDtypeStruct((81, 128), F32),
         ],
         scratch_shapes=[
+            v((2, 256, 8, 128), BF), v((2, 256, 8, 128), BF), v((2, 128, 8, 128), BF),
+            v((2, 8, 128, 256), BF), v((2, 8, 128, 256), BF),
             v((2, 8, 128, 256), BF), v((2, 8, 128, 256), BF), v((2, 8, 128, 128), BF),
             v((2048, 128), F32), v((2048, 128), F32),
             v((2, 2, 256, 8, 128), BF), v((2, 2, 4, 16, 256), BF), v((2, 2, 4, 16, 256), BF),
@@ -560,9 +601,11 @@
             v((2, 8, 128, 128), F32), v((2, 8, 128, 128), F32),
             v((2, 8, WIDE, 256), F32), v((2, 128, 256), F32),
             v((2, 128, 256), F32),
-            v((128, 128), F32), v((8, 16, 128), F32), v((16, 16, 128), F32), v((8, 16, 128), F32),
+            v((128, 128), F32), v((8, 16, 128), F32), v((4, 16, 128), F32), v((4, 16, 128), F32),
+            v((8, 16, 128), F32),
             dma((2, 2)), dma((2, 2)), dma((2, 2, 3)), dma((2, 2, 3)),
-            dma((8,)), dma((8,)), dma((16,)), dma((16,)), dma((8,)), dma((8,)),
+            dma((8,)), dma((8,)), dma((4,)), dma((4,)), dma((4,)), dma((4,)), dma((8,)), dma((8,)),
+            dma((6,)), dma((4,)),
         ],
         compiler_params=pltpu.CompilerParams(
             collective_id=0, has_side_effects=True, vmem_limit_bytes=56 << 20

time: 71.5 us -> 71.1 us (level)
  no operation moved by 1% of the time
where the time goes in v6:
time: 71.1 us; the launch traced here: 70.9 us
  Pallas kernels  65.6 us (92%)
  local copies, waits for them, and re-layouts  4.6 us (6%)
    pallas_call x1, Pallas kernels, local(): pl.pallas_call(functools.partial(kernel, 1.0 / math.sqrt(total)), in_spec...  65.6 us
    unnamed x7, local copies, waits for them, and re-layouts  4.6 us

profile of v6, /device:TPU:1, one launch (start us, length us, event | category | flops | bytes accessed | tf_op | source)
XLA Modules:
  0.0 70.9 jit_solution(2842820624644652384)
XLA Ops:
  0.6 65.6 %shard_map.94 = (bf16[2,8,128,256]{3,2,1,0:T(8,128)(2,1)}, bf16[2,8,128,256]{3,2,1,0:T(8,128)(2,1)}, f32[81,128]{1,0:T(8,128)}) custom-call(s32[2,2]{1,0:T(2,128)} %shift_ref.1, bf16[2,256,8,128]{3,2,1,0:T(8,128)(2,1)} %prev_hbm.1, bf16[2,256,8,128]{3,2,1,0:T(8,128)(2,1)} %cur_hbm.1, bf16[2,128,8,128]{3,2,1,0:T(8,128)(2,1)} %cot_hbm.1, ...), custom_call_target="tpu_custom_call" | custom-call | flops 3000000000 | bytes 8388608 | tf_op jit(solution)/shard_map/pallas_call | solution.py:576
  66.2 0.0 copy-start
  66.2 2.5 %copy.10 = bf16[2,256,8,128]{3,2,1,0:T(8,128)(2,1)} copy(bf16[2,256,8,128]{1,3,2,0:T(8,128)(2,1)} %bitcast.5) | data formatting | bytes 2097152
  68.8 0.0 copy-done
  68.8 0.0 copy-start.1
  68.8 1.5 %copy.11 = bf16[2,256,8,128]{3,2,1,0:T(8,128)(2,1)} copy(bf16[2,256,8,128]{1,3,2,0:T(8,128)(2,1)S(1)} %bitcast.4) | data formatting | bytes 2097152
  70.2 0.0 copy-done.1
  70.2 0.6 copy.13
Async XLA Ops:
  66.2 2.5 %copy-start = (bf16[2,8,128,256]{3,2,1,0:T(8,128)(2,1)S(1)}, bf16[2,8,128,256]{3,2,1,0:T(8,128)(2,1)}, u32[]{:S(2)}) copy-start(bf16[2,8,128,256]{3,2,1,0:T(8,128)(2,1)} %get-tuple-element.7) | copy-start | bytes 3145732
  68.8 1.5 %copy-start.1 = (f32[81,128]{1,0:T(8,128)S(1)}, f32[81,128]{1,0:T(8,128)}, u32[]{:S(2)}) copy-start(f32[81,128]{1,0:T(8,128)} %get-tuple-element.8) | copy-start | bytes 124420

commit v7 on v6

--- a/solution.py
+++ b/solution.py
@@ -159,18 +159,18 @@
     prev_ref, cur_ref, cot_ref, flat0, flat1, msg_r, rim_s, rim_r,
     edge_s, edge_r0, edge_r1, edge_cot_s, edge_cot_r, own0, own1, cot_x, own_pre, rim_cur, rim_cot,
     msg, tri_s, tri_r, halo0, halo1, pre_halo0, pre_halo1,
-    sum_c, act_c, pre_c, sum_q, rim_sum, acc, ar0, ar1, ar2, ar3, ar4,
-    side_ss, side_rs, row_ss, row_rs, s1, r1, s2, r2, s3, r3, s4, r4, load_sem, store_sem,
+    sum_c, act_c, pre_c, sum_q, rim_sum, acc, ar0, ar1, ar2, ar3,
+    side_ss, side_rs, row_ss, row_rs, s1, r1, s2, r2, s3, r3, load_sem, store_sem,
 ):
     row, col = lax.axis_index("row"), lax.axis_index("col")
     last = lax.axis_size("row") - 1
     left = col == 0
     owns = (own0, own1)
     halos, pre_halos = (halo0, halo1), (pre_halo0, pre_halo1)
-    g1, g2, g3 = (row % 4) * 2 + col, (row // 4) % 4, row // 16
-
-    def member(a, b, c):
-        return ((c * 4 + b) * 4 + a // 2, a % 2)
+    g1, g2 = (row % 4) * 2 + col, row // 4
+
+    def member(a, b):
+        return (b * 4 + a // 2, a % 2)
 
     loads, stores = [], []
     for p in range(2):
@@ -189,10 +189,9 @@
         pl.semaphore_signal(barrier, inc=1, device_id=target, device_id_type=MESH)
 
     for d in range(1, 8):
-        greet(member((g1 + d) % 8, g2, g3))
-    for d in range(1, 4):
-        greet(member(g1, (g2 + d) % 4, g3))
-        greet(member(g1, g2, (g3 + d) % 4))
+        greet(member((g1 + d) % 8, g2))
+    for d in range(1, 16):
+        greet(member(g1, (g2 + d) % 16))
     greet(((row + 1) % (last + 1), col))
     greet(((row + last) % (last + 1), col))
 
@@ -300,7 +299,7 @@
     for copy in loads[:2]:
         copy.wait()
     pack(0)
-    pl.semaphore_wait(barrier, 15)
+    pl.semaphore_wait(barrier, 24)
     send(0, 0)
     for copy in loads[2:]:
         copy.wait()
@@ -309,8 +308,6 @@
     edges(0)
     pack(1)
     turn_prev(1)
-    turn_cells(1)
-    edges(1)
 
     w81 = w_ref[...]
     e = e_ref[...]
@@ -371,7 +368,8 @@
 
     join(0)
     send(1, 0)
-    join(1)
+    turn_cells(1)
+    edges(1)
 
     def arrive(p):
         dy, dx = shift_ref[p, 0], shift_ref[p, 1]
@@ -450,17 +448,12 @@
             p, bb, shift_ref[p, 1], left, halos[p], pre_halos[p], prev_ref, e_fold, masks,
             sum_q, rim_sum, gp_ref)
 
-    def late(i):
-        for bb in (2 * i, 2 * i + 1):
-            late_cells(0, bb)
-            late_positions(0, bb)
-
     early(0)
+    join(1)
     early(1)
     arrive(0)
-    loop(0, 4, late)
+    loop(0, 2, lambda i: [late_cells(0, 4 * i + k) for k in range(4)])
     stores[0].start()
-    stores[1].start()
     arrive(1)
     loop(0, 2, lambda i: [late_cells(1, 4 * i + k) for k in range(4)])
 
@@ -478,28 +471,21 @@
         peer = (g1 + d) % 8
         return pltpu.make_async_remote_copy(
             src_ref=share(ar0, peer), dst_ref=ar1.at[g1], send_sem=s1.at[peer],
-            recv_sem=r1.at[g1], device_id=member(peer, g2, g3), device_id_type=MESH,
+            recv_sem=r1.at[g1], device_id=member(peer, g2), device_id_type=MESH,
         )
 
     def second(d):
-        peer = (g2 + d) % 4
+        peer = (g2 + d) % 16
         return pltpu.make_async_remote_copy(
             src_ref=ar2.at[g2], dst_ref=ar2.at[g2], send_sem=s2.at[peer],
-            recv_sem=r2.at[g2], device_id=member(g1, peer, g3), device_id_type=MESH,
+            recv_sem=r2.at[g2], device_id=member(g1, peer), device_id_type=MESH,
         )
 
     def third(d):
-        peer = (g3 + d) % 4
-        return pltpu.make_async_remote_copy(
-            src_ref=ar3.at[g3], dst_ref=ar3.at[g3], send_sem=s3.at[peer],
-            recv_sem=r3.at[g3], device_id=member(g1, g2, peer), device_id_type=MESH,
-        )
-
-    def fourth(d):
         peer = (g1 + d) % 8
         return pltpu.make_async_remote_copy(
-            src_ref=ar4.at[g1], dst_ref=ar4.at[g1], send_sem=s4.at[peer],
-            recv_sem=r4.at[g1], device_id=member(peer, g2, g3), device_id_type=MESH,
+            src_ref=ar3.at[g1], dst_ref=ar3.at[g1], send_sem=s3.at[peer],
+            recv_sem=r3.at[g1], device_id=member(peer, g2), device_id_type=MESH,
         )
 
     def got(buffer, sends, receives, source):
@@ -508,39 +494,35 @@
             recv_sem=receives.at[source], device_id=(row, 1 - col), device_id_type=MESH,
         ).wait_recv()
 
-    def some_positions(lo, hi):
-        loop(0, 1, lambda i: [late_positions(1, k) for k in range(lo, hi)])
+    def some_positions(p, lo, hi):
+        loop(lo // 2, hi // 2, lambda i: [late_positions(p, 2 * i + k) for k in range(2)])
 
     for d in range(1, 8):
         first(d).start()
-    some_positions(0, 2)
+    some_positions(0, 0, 8)
+    stores[1].start()
     ar1[g1] = ar0[pl.ds(pl.multiple_of(g1 * 16, 16), 16)]
     for d in range(1, 8):
-        first(d).wait_send()
         got(ar1, s1, r1, (g1 + d) % 8)
     ar2[g2] = jnp.sum(ar1[...], axis=0)
-    for d in range(1, 4):
+    for d in range(1, 16):
         second(d).start()
-    some_positions(2, 4)
-    for d in range(1, 4):
-        second(d).wait_send()
-        got(ar2, s2, r2, (g2 + d) % 4)
-    ar3[g3] = jnp.sum(ar2[...], axis=0)
-    for d in range(1, 4):
+    some_positions(1, 0, 4)
+    for d in range(1, 16):
+        got(ar2, s2, r2, (g2 + d) % 16)
+    ar3[g1] = jnp.sum(ar2[...], axis=0)
+    for d in range(1, 8):
         third(d).start()
-    some_positions(4, 6)
-    for d in range(1, 4):
-        third(d).wait_send()
-        got(ar3, s3, r3, (g3 + d) % 4)
-    ar4[g1] = jnp.sum(ar3[...], axis=0)
-    for d in range(1, 8):
-        fourth(d).start()
-    some_positions(6, 8)
+    some_positions(1, 4, 8)
     stores[3].start()
     for d in range(1, 8):
-        fourth(d).wait_send()
-        got(ar4, s4, r4, (g1 + d) % 8)
-    gw_ref[...] = ar4[...].reshape(128, 128)[:81] * norm
+        got(ar3, s3, r3, (g1 + d) % 8)
+    gw_ref[...] = ar3[...].reshape(128, 128)[:81] * norm
+    for d in range(1, 8):
+        first(d).wait_send()
+        third(d).wait_send()
+    for d in range(1, 16):
+        second(d).wait_send()
     for copy in stores:
         copy.wait()
 
@@ -601,10 +583,9 @@
             v((2, 8, 128, 128), F32), v((2, 8, 128, 128), F32),
             v((2, 8, WIDE, 256), F32), v((2, 128, 256), F32),
             v((2, 128, 256), F32),
-            v((128, 128), F32), v((8, 16, 128), F32), v((4, 16, 128), F32), v((4, 16, 128), F32),
-            v((8, 16, 128), F32),
+            v((128, 128), F32), v((8, 16, 128), F32), v((16, 16, 128), F32), v((8, 16, 128), F32),
             dma((2, 2)), dma((2, 2)), dma((2, 2, 3)), dma((2, 2, 3)),
-            dma((8,)), dma((8,)), dma((4,)), dma((4,)), dma((4,)), dma((4,)), dma((8,)), dma((8,)),
+            dma((8,)), dma((8,)), dma((16,)), dma((16,)), dma((8,)), dma((8,)),
             dma((6,)), dma((4,)),
         ],
         compiler_params=pltpu.CompilerParams(

time: 71.1 us -> 73.3 us (1.031)
  Pallas kernels: 65.6 us -> 67.8 us
    pallas_call x1, Pallas kernels: 65.6 us -> 67.8 us  [local(): pl.pallas_call(functools.partial(kernel, 1.0 / math.sqrt(total)), in_spec...]
where the time goes in v7:
time: 73.3 us; the launch traced here: 73.1 us
  Pallas kernels  67.8 us (92%)
  local copies, waits for them, and re-layouts  4.6 us (6%)
    pallas_call x1, Pallas kernels, local(): pl.pallas_call(functools.partial(kernel, 1.0 / math.sqrt(total)), in_spec...  67.8 us
    unnamed x7, local copies, waits for them, and re-layouts  4.6 us

profile of v7, /device:TPU:1, one launch (start us, length us, event | category | flops | bytes accessed | tf_op | source)
XLA Modules:
  0.0 73.1 jit_solution(918619414397150064)
XLA Ops:
  0.6 67.8 %shard_map.94 = (bf16[2,8,128,256]{3,2,1,0:T(8,128)(2,1)}, bf16[2,8,128,256]{3,2,1,0:T(8,128)(2,1)}, f32[81,128]{1,0:T(8,128)}) custom-call(s32[2,2]{1,0:T(2,128)} %shift_ref.1, bf16[2,256,8,128]{3,2,1,0:T(8,128)(2,1)} %prev_hbm.1, bf16[2,256,8,128]{3,2,1,0:T(8,128)(2,1)} %cur_hbm.1, bf16[2,128,8,128]{3,2,1,0:T(8,128)(2,1)} %cot_hbm.1, ...), custom_call_target="tpu_custom_call" | custom-call | flops 3000000000 | bytes 8388608 | tf_op jit(solution)/shard_map/pallas_call | solution.py:558
  68.4 0.0 copy-start
  68.4 2.5 %copy.10 = bf16[2,256,8,128]{3,2,1,0:T(8,128)(2,1)} copy(bf16[2,256,8,128]{1,3,2,0:T(8,128)(2,1)} %bitcast.5) | data formatting | bytes 2097152
  71.0 0.0 copy-done
  71.0 0.0 copy-start.1
  71.0 1.5 %copy.11 = bf16[2,256,8,128]{3,2,1,0:T(8,128)(2,1)} copy(bf16[2,256,8,128]{1,3,2,0:T(8,128)(2,1)S(1)} %bitcast.4) | data formatting | bytes 2097152
  72.4 0.0 copy-done.1
  72.4 0.6 copy.13
Async XLA Ops:
  68.4 2.5 %copy-start = (bf16[2,8,128,256]{3,2,1,0:T(8,128)(2,1)S(1)}, bf16[2,8,128,256]{3,2,1,0:T(8,128)(2,1)}, u32[]{:S(2)}) copy-start(bf16[2,8,128,256]{3,2,1,0:T(8,128)(2,1)} %get-tuple-element.7) | copy-start | bytes 3145732
  71.0 1.5 %copy-start.1 = (f32[81,128]{1,0:T(8,128)S(1)}, f32[81,128]{1,0:T(8,128)}, u32[]{:S(2)}) copy-start(f32[81,128]{1,0:T(8,128)} %get-tuple-element.8) | copy-start | bytes 124420

commit v8 on v6

--- a/solution.py
+++ b/solution.py
@@ -45,9 +45,9 @@
     return act, q + act * (2.0 - q)
 
 
-def cell_block(p, bb, rows_of, cur_ref):
+def cell_block(p, bb, rows_of, both):
     at = pl.multiple_of(bb * 16, 16)
-    cur = cur_ref[p, :, pl.ds(at, 16), :].reshape(128, 256)
+    cur = both[p, 8:16, pl.ds(at, 16), :].reshape(128, 256)
     rows = [rows_of(i, at) for i in range(8)]
     win = jnp.concatenate([r[0:16] for r in rows] + [r[8:24] for r in rows], axis=0)
     return win, dot(cur, win, NT)
@@ -61,8 +61,8 @@
     return jnp.concatenate(full, axis=0).astype(BF)
 
 
-def cells_early(p, bb, own, cur_ref, cot_ref, wk, sum_c, act_c, pre_c, sum_q):
-    win, vol = cell_block(p, bb, lambda i, at: own[i, pl.ds(at, 32), :], cur_ref)
+def cells_early(p, bb, own, both, cot_ref, wk, sum_c, act_c, pre_c, sum_q):
+    win, vol = cell_block(p, bb, lambda i, at: own[i, pl.ds(at, 32), :], both)
     at = pl.multiple_of(bb * 16, 16)
     pre = dot(cot_ref[p, :, pl.ds(at, 16), :].reshape(128, 128), wk)
     grads, acts, rest = [], [], []
@@ -78,7 +78,7 @@
     pre_c[p, bb] = jnp.concatenate(rest, axis=0)
     grad = split_grads(grads)
     sum_c[p, bb] = dot(grad, win)
-    cur = cur_ref[p, :, pl.ds(at, 16), :].reshape(128, 256)
+    cur = both[p, 8:16, pl.ds(at, 16), :].reshape(128, 256)
     back = dot(grad, cur, TN)
     for i in range(8):
         even, odd = back[16 * i : 16 * i + 16], back[128 + 16 * i : 128 + 16 * i + 16]
@@ -87,11 +87,11 @@
         sum_q[p, i, pl.ds(at + 16, 8), :] = odd[8:]
 
 
-def cells_late(p, bb, dy, halo, cur_ref, cot_ref, sum_c, act_c, pre_c, out_ref, acc_ref):
+def cells_late(p, bb, dy, halo, both, cot_ref, sum_c, act_c, pre_c, out_ref, acc_ref):
     def rows_of(i, at):
         return halo[i, pl.ds(at, 32), :]
 
-    win, vol = cell_block(p, bb, rows_of, cur_ref)
+    win, vol = cell_block(p, bb, rows_of, both)
     at = pl.multiple_of(bb * 16, 16)
     cot = cot_ref[p, :, pl.ds(at, 16), :].reshape(128, 128).astype(F32)
     cot_rev = jnp.concatenate([flip8(cot[8 * i : 8 * i + 8]) for i in range(16)], axis=0)
@@ -110,9 +110,9 @@
     out_ref[p, :, pl.ds(at, 16), :] = out.astype(BF).reshape(8, 16, 256)
 
 
-def rim_positions(p, left, rim_cur, rim_cot, prev_ref, wk, masks, rim_sum):
+def rim_positions(p, left, rim_cur, rim_cot, both, wk, masks, rim_sum):
     at = pl.multiple_of(jnp.where(left, 112, 0), 16)
-    prev = prev_ref[p, :, pl.ds(at, 16), :].reshape(128, 256)
+    prev = both[p, 0:8, pl.ds(at, 16), :].reshape(128, 256)
     win = rim_cur[p].reshape(64, 256).astype(BF)
     vol = dot(win, prev, NT)
     pre = dot(rim_cot[p].reshape(64, 128).astype(BF), wk)
@@ -127,10 +127,10 @@
 
 
 def positions_late(
-    p, bb, dx, left, halo, pre_halo, prev_ref, e_fold, masks, sum_q, rim_sum, out_ref
+    p, bb, dx, left, halo, pre_halo, both, e_fold, masks, sum_q, rim_sum, out_ref
 ):
     at = pl.multiple_of(bb * 16, 16)
-    prev = prev_ref[p, :, pl.ds(at, 16), :].reshape(128, 256)
+    prev = both[p, 0:8, pl.ds(at, 16), :].reshape(128, 256)
     win = jnp.concatenate([halo[8 + i, pl.ds(at, 32), :][:24] for i in range(8)], axis=0)
     vol = dot(win, prev, NT)
     pre = dot(
@@ -155,9 +155,8 @@
 def kernel(
     norm, shift_ref, prev_hbm, cur_hbm, cot_hbm, w_ref, e_ref, eye_ref,
     gc_hbm, gp_hbm, gw_ref,
-    prev_in, cur_in, cot_in, gc_ref, gp_ref,
-    prev_ref, cur_ref, cot_ref, flat0, flat1, msg_r, rim_s, rim_r,
-    edge_s, edge_r0, edge_r1, edge_cot_s, edge_cot_r, own0, own1, cot_x, own_pre, rim_cur, rim_cot,
+    both, cot_ref, gc_ref, gp_ref, msg_r0, msg_r1, rim_s, rim_r,
+    edge_s, edge_r0, edge_r1, edge_cot_s, edge_cot_r, own0, own1, own_pre, rim_cur, rim_cot,
     msg, tri_s, tri_r, halo0, halo1, pre_halo0, pre_halo1,
     sum_c, act_c, pre_c, sum_q, rim_sum, acc, ar0, ar1, ar2, ar3, ar4,
     side_ss, side_rs, row_ss, row_rs, s1, r1, s2, r2, s3, r3, s4, r4, load_sem, store_sem,
@@ -174,9 +173,11 @@
 
     loads, stores = [], []
     for p in range(2):
-        for source, target in ((prev_hbm, prev_in), (cur_hbm, cur_in), (cot_hbm, cot_in)):
+        for source, target in (
+            (prev_hbm, both.at[p, 0:8]), (cur_hbm, both.at[p, 8:16]), (cot_hbm, cot_ref.at[p])
+        ):
             at = load_sem.at[len(loads)]
-            loads.append(pltpu.make_async_copy(source.at[p], target.at[p], at))
+            loads.append(pltpu.make_async_copy(source.at[p], target, at))
         for source, target in ((gc_ref, gc_hbm), (gp_ref, gp_hbm)):
             at = store_sem.at[len(stores)]
             stores.append(pltpu.make_async_copy(source.at[p], target.at[p], at))
@@ -206,8 +207,10 @@
         )
 
     def along(p, way, k):
-        s, r = ((msg, msg_r), (rim_s, rim_r), (tri_s, tri_r))[k]
-        src, dst = s.at[p, way], r.at[p, way]
+        src, dst = (
+            (msg.at[p, way], (msg_r0, msg_r1)[p].at[way]), (rim_s.at[p, way], rim_r.at[p, way]),
+            (tri_s.at[p, way], tri_r.at[p, way]),
+        )[k]
         target = jnp.where(row == last, row, row + 1) if way else jnp.where(row == 0, row, row - 1)
         return pltpu.make_async_remote_copy(
             src_ref=src, dst_ref=dst, send_sem=row_ss.at[p, way, k],
@@ -217,16 +220,12 @@
     def pack(p):
         dy = shift_ref[p, 0]
 
-        def chunk(i, carry):
-            at = pl.ds(pl.multiple_of(i * 16, 16), 16)
-            pos = prev_in[p, at].astype(F32)
-            cell = pltpu.roll(cur_in[p, at].astype(F32), (4 + dy) % 8, 1)
-            low = iota((16, 8, 128), 1) < 4 + dy
-            msg[p, 0, at] = jnp.where(low, pos, cell).astype(BF)
-            msg[p, 1, at] = jnp.where(low, cell, pos).astype(BF)
+        def copy(s, carry):
+            msg[p, 0, s] = both[p, jnp.where(s < 4 + dy, s, 4 + s - dy)]
+            msg[p, 1, s] = both[p, jnp.where(s < 4 + dy, 12 + s - dy, s)]
             return carry
 
-        lax.fori_loop(0, 16, chunk, 0)
+        lax.fori_loop(0, 8, copy, 0)
 
     def send(p, k):
         @pl.when(row > 0)
@@ -236,14 +235,6 @@
         @pl.when(row < last)
         def _():
             along(p, 1, k).start()
-
-    ident = jnp.where(iota((128, 128), 0) == iota((128, 128), 1), 1.0, 0.0).astype(BF)
-
-    def spread_rows(flat, x):
-        flat[0 : x.shape[0] * 8] = x.reshape(x.shape[0] * 8, 128)
-
-    def picked(flat, y, channels):
-        return flat[pl.ds(y, channels, stride=8), :].astype(BF)
 
     def aligner(offset):
         take = iota((WIDE, 128), 1) + 8 == iota((WIDE, 128), 0) + offset
@@ -260,32 +251,13 @@
         low, high = jnp.where(left, zero, rim), jnp.where(left, rim, zero)
         return jnp.concatenate([x[:8] + low, x[8:128], x[128:136] + high, x[136:]], axis=0)
 
-    def turn_prev(p):
-        both = jnp.concatenate([ident, aligner(4 + shift_ref[p, 1])], axis=0)
-        spread_rows(flat0, prev_in[p].astype(F32))
-        for y in range(8):
-            x = dot(both, picked(flat0, y, 256), NT).astype(BF)
-            prev_ref[p, y] = x[:128]
-            owns[p][y] = x[128:]
-
-    def turn_cells(p):
-        both = jnp.concatenate([ident, aligner(4 - shift_ref[p, 1])], axis=0)
-        spread_rows(flat1, cur_in[p].astype(F32))
-        for y in range(8):
-            cur_ref[p, y] = dot(ident, picked(flat1, y, 256), NT).astype(BF)
-        spread_rows(flat0, cot_in[p].astype(F32))
-        for y in range(8):
-            x = dot(both, picked(flat0, y, 128), NT)
-            cot_ref[p, y] = x[:128].astype(BF)
-            cot_x[p, y] = x[128:]
-
     start = jnp.where(left, 112, 0)
 
     def edges(p):
         for y in range(8):
             pick = []
-            for ref in (prev_ref, cur_ref):
-                tile = ref[p, y, pl.ds(pl.multiple_of(start, 16), 16), :].astype(F32)
+            for ref_row in (y, 8 + y):
+                tile = both[p, ref_row, pl.ds(pl.multiple_of(start, 16), 16), :].astype(F32)
                 pick.append(jnp.where(left, tile[8:], tile[:8]))
             edge_s[p, y] = jnp.concatenate(pick, axis=0).astype(BF)
         for y in range(0, 8, 2):
@@ -294,23 +266,19 @@
                 tile = cot_ref[p, yy, pl.ds(pl.multiple_of(start, 16), 16), :].astype(F32)
                 pick.append(jnp.where(left, tile[8:], tile[:8]))
             edge_cot_s[p, y // 2] = jnp.concatenate(pick, axis=0).astype(BF)
-        for k in range(2):
-            side(p, k).start()
-
-    for copy in loads[:2]:
+
+    for copy in loads:
         copy.wait()
+    edges(0)
     pack(0)
     pl.semaphore_wait(barrier, 15)
+    for k in range(2):
+        side(0, k).start()
     send(0, 0)
-    for copy in loads[2:]:
-        copy.wait()
-    turn_prev(0)
-    turn_cells(0)
-    edges(0)
+    edges(1)
+    for k in range(2):
+        side(1, k).start()
     pack(1)
-    turn_prev(1)
-    turn_cells(1)
-    edges(1)
 
     w81 = w_ref[...]
     e = e_ref[...]
@@ -329,20 +297,17 @@
     def join(p):
         dy, dx = shift_ref[p, 0], shift_ref[p, 1]
         own, edge_r = owns[p], (edge_r0, edge_r1)[p]
+        take_p, take_c = aligner(4 + dx), aligner(4 - dx)
         for k in range(2):
             side(p, k).wait()
         for y in range(8):
             edge = edge_r[y].astype(F32)
-            rim = rim_place(edge[:8], 4 - dx)
-            zero = jnp.zeros_like(rim)
-            for at, piece in ((0, jnp.where(left, zero, rim)), (128, jnp.where(left, rim, zero))):
-                tile = own[y, at : at + 16].astype(F32) + jnp.concatenate([piece, zero], axis=0)
-                own[y, at : at + 16] = tile.astype(BF)
+            own[y] = rim_add(dot(take_p, both[p, y]), rim_place(edge[:8], 4 - dx)).astype(BF)
             rim_cur[p, y] = rim_place(edge[8:], 4 + dx)
             at = 8 * (y % 2)
             rim = rim_place(edge_cot_r[p, y // 2].astype(F32)[at : at + 8], 4 + dx)
             rim_cot[p, y] = rim
-            own_pre[y] = dot(rim_add(cot_x[p, y], rim).astype(BF), w9)
+            own_pre[y] = dot(rim_add(dot(take_c, cot_ref[p, y]), rim).astype(BF), w9)
 
         def tile(s, up):
             is_prev = (s < 4 + dy) if up else (s >= 4 + dy)
@@ -387,31 +352,22 @@
 
                 @pl.when(row == edge_row)
                 def _():
-                    part = buffer.at[p, way]
+                    part = buffer[way]
                     part[...] = jnp.zeros(part.shape, BF)
 
-        for k, buffer in enumerate((msg_r, rim_r, tri_r)):
-            receive(k, buffer)
-
-        def sort(i, carry):
-            at = pl.ds(pl.multiple_of(i * 16, 16), 16)
-            to = pl.ds(pl.multiple_of(i * 128, 128), 128)
-            up, down = msg_r[p, 0, at].astype(F32), msg_r[p, 1, at].astype(F32)
-            low = iota((16, 8, 128), 1) < 4 + dy
-            flat0[to] = jnp.where(low, up, down).reshape(128, 128)
-            flat1[to] = jnp.where(low, down, up).reshape(128, 128)
-            return carry
-
-        lax.fori_loop(0, 16, sort, 0)
+        msg_r = (msg_r0, msg_r1)[p]
+        receive(0, msg_r.at)
+        receive(1, rim_r.at[p].at)
+        receive(2, tri_r.at[p].at)
         for s in range(8):
             at = 8 * (s % 2)
             up = rim_r[p, 0, s // 2].astype(F32)[at : at + 8]
             down = rim_r[p, 1, s // 2].astype(F32)[at : at + 8]
             low = s < 4 + dy
-            x = dot(take_p, picked(flat0, s, 256), NT)
+            x = dot(take_p, msg_r[jnp.where(low, 0, 1), s])
             rim = rim_place(jnp.where(low, up, down), 4 - dx)
             halo[s] = rim_add(x, rim).astype(BF)
-            x = dot(take_c, picked(flat1, s, 256), NT)
+            x = dot(take_c, msg_r[jnp.where(low, 1, 0), s])
             rim = rim_place(jnp.where(low, down, up), 4 + dx)
             halo[8 + s] = rim_add(x, rim).astype(BF)
         for s in range(4):
@@ -436,18 +392,18 @@
         def work(i):
             for bb in (2 * i, 2 * i + 1):
                 cells_early(
-                    p, bb, owns[p], cur_ref, cot_ref, wks[p], sum_c, act_c, pre_c, sum_q)
+                    p, bb, owns[p], both, cot_ref, wks[p], sum_c, act_c, pre_c, sum_q)
 
         loop(0, 4, work)
-        rim_positions(p, left, rim_cur, rim_cot, prev_ref, wks[p], masks, rim_sum)
+        rim_positions(p, left, rim_cur, rim_cot, both, wks[p], masks, rim_sum)
 
     def late_cells(p, bb):
         cells_late(
-            p, bb, shift_ref[p, 0], halos[p], cur_ref, cot_ref, sum_c, act_c, pre_c, gc_ref, acc)
+            p, bb, shift_ref[p, 0], halos[p], both, cot_ref, sum_c, act_c, pre_c, gc_ref, acc)
 
     def late_positions(p, bb):
         positions_late(
-            p, bb, shift_ref[p, 1], left, halos[p], pre_halos[p], prev_ref, e_fold, masks,
+            p, bb, shift_ref[p, 1], left, halos[p], pre_halos[p], both, e_fold, masks,
             sum_q, rim_sum, gp_ref)
 
     def late(i):
@@ -566,6 +522,9 @@
 
 def local(current, previous, shift, weight, cotangent):
     pairs, channels, rows, cols = current.shape
+    prev = previous.transpose(0, 2, 3, 1)
+    cur = current.transpose(0, 2, 3, 1)
+    cot = cotangent.transpose(0, 2, 3, 1)
     e = jnp.asarray(spread_matrix(), BF)
     eye = jnp.asarray(np.eye(81, 128), BF)
     total = pairs * rows * lax.axis_size("row") * cols * lax.axis_size("col")
@@ -583,17 +542,16 @@
             jax.ShapeDtypeStruct((81, 128), F32),
         ],
         scratch_shapes=[
-            v((2, 256, 8, 128), BF), v((2, 256, 8, 128), BF), v((2, 128, 8, 128), BF),
+            v((2, 16, 128, 256), BF), v((2, 8, 128, 128), BF),
             v((2, 8, 128, 256), BF), v((2, 8, 128, 256), BF),
-            v((2, 8, 128, 256), BF), v((2, 8, 128, 256), BF), v((2, 8, 128, 128), BF),
-            v((2048, 128), F32), v((2048, 128), F32),
-            v((2, 2, 256, 8, 128), BF), v((2, 2, 4, 16, 256), BF), v((2, 2, 4, 16, 256), BF),
+            v((2, 8, 128, 256), BF), v((2, 8, 128, 256), BF),
+            v((2, 2, 4, 16, 256), BF), v((2, 2, 4, 16, 256), BF),
             v((2, 8, 16, 256), BF), v((8, 16, 256), BF), v((8, 16, 256), BF),
             v((2, 4, 16, 128), BF), v((2, 4, 16, 128), BF),
             v((8, WIDE, 256), BF), v((8, WIDE, 256), BF),
-            v((2, 8, WIDE, 128), F32), v((8, WIDE, 128), F32),
+            v((8, WIDE, 128), F32),
             v((2, 8, 8, 256), F32), v((2, 8, 8, 128), F32),
-            v((2, 2, 256, 8, 128), BF),
+            v((2, 2, 8, 128, 256), BF),
             v((2, 2, 4, WIDE, 128), BF), v((2, 2, 4, WIDE, 128), BF),
             v((16, WIDE, 256), BF), v((16, WIDE, 256), BF),
             v((8, WIDE, 128), BF), v((8, WIDE, 128), BF),
@@ -613,7 +571,7 @@
         cost_estimate=pl.CostEstimate(
             flops=3_000_000_000, bytes_accessed=8 << 20, transcendentals=1_500_000
         ),
-    )(shift, previous, current, cotangent, weight.T, e, eye)
+    )(shift, prev, cur, cot, weight.T, e, eye)
     return gc.transpose(0, 3, 1, 2), gp.transpose(0, 3, 1, 2), gw.T
 
 

time: 71.1 us -> 74.3 us (1.045)
  local copies, waits for them, and re-layouts: 4.6 us -> 9.71 us
  Pallas kernels: 65.6 us -> 63.7 us
    unnamed x7 -> x14, local copies, waits for them, and re-layouts: 4.6 us -> 9.71 us
    pallas_call x1, Pallas kernels: 65.6 us -> 63.7 us  [local(): pl.pallas_call(functools.partial(kernel, 1.0 / math.sqrt(total)), in_spec...]
where the time goes in v8:
time: 74.3 us; the launch traced here: 74 us
  Pallas kernels  63.7 us (86%)
  local copies, waits for them, and re-layouts  9.71 us (13%)
    pallas_call x1, Pallas kernels, local(): pl.pallas_call(functools.partial(kernel, 1.0 / math.sqrt(total)), in_spec...  63.7 us
    unnamed x14, local copies, waits for them, and re-layouts  9.71 us

profile of v8, /device:TPU:1, one launch (start us, length us, event | category | flops | bytes accessed | tf_op | source)
XLA Modules:
  0.0 74.0 jit_solution(8791729341794013223)
XLA Ops:
  0.6 0.0 copy-start
  0.6 2.2 %copy.12 = bf16[2,128,8,128]{1,3,2,0:T(8,128)(2,1)} copy(bf16[2,128,8,128]{3,2,1,0:T(8,128)(2,1)} %param.11) | data formatting | bytes 1048576 | tf_op args[4]
  2.8 0.0 copy-done
  2.8 0.0 copy-start.1
  2.8 1.4 %copy.11 = bf16[2,256,8,128]{1,3,2,0:T(8,128)(2,1)} copy(bf16[2,256,8,128]{3,2,1,0:T(8,128)(2,1)S(1)} %copy-done) | data formatting | bytes 2097152 | tf_op args[0]
  4.3 0.0 copy-done.1
  4.3 1.4 %copy.10 = bf16[2,256,8,128]{1,3,2,0:T(8,128)(2,1)} copy(bf16[2,256,8,128]{3,2,1,0:T(8,128)(2,1)S(1)} %copy-done.1) | data formatting | bytes 2097152 | tf_op args[1]
  5.7 63.7 %shard_map.94 = (bf16[2,8,128,256]{3,2,1,0:T(8,128)(2,1)}, bf16[2,8,128,256]{3,2,1,0:T(8,128)(2,1)}, f32[81,128]{1,0:T(8,128)}) custom-call(s32[2,2]{1,0:T(2,128)} %shift_ref.1, bf16[2,8,128,256]{3,2,1,0:T(8,128)(2,1)} %bitcast.10, bf16[2,8,128,256]{3,2,1,0:T(8,128)(2,1)} %bitcast.9, bf16[2,8,128,128]{3,2,1,0:T(8,128)(2,1)} %bitcast.11, ...), custom_call_target="tpu_custom_call" | custom-call | flops 3000000000 | bytes 8388608 | tf_op jit(solution)/shard_map/pallas_call | solution.py:535
  69.4 0.0 copy-start.2
  69.4 2.5 %copy.13 = bf16[2,256,8,128]{3,2,1,0:T(8,128)(2,1)} copy(bf16[2,256,8,128]{1,3,2,0:T(8,128)(2,1)} %bitcast.8) | data formatting | bytes 2097152
  72.0 0.0 copy-done.2
  72.0 0.0 copy-start.3
  72.0 1.5 %copy.14 = bf16[2,256,8,128]{3,2,1,0:T(8,128)(2,1)} copy(bf16[2,256,8,128]{1,3,2,0:T(8,128)(2,1)S(1)} %bitcast.7) | data formatting | bytes 2097152
  73.4 0.0 copy-done.3
  73.4 0.6 copy.16
Async XLA Ops:
  0.6 2.2 %copy-start = (bf16[2,256,8,128]{3,2,1,0:T(8,128)(2,1)S(1)}, bf16[2,256,8,128]{3,2,1,0:T(8,128)(2,1)}, u32[]{:S(2)}) copy-start(bf16[2,256,8,128]{3,2,1,0:T(8,128)(2,1)} %param.7) | copy-start | bytes 3145732
  2.8 1.5 %copy-start.1 = (bf16[2,256,8,128]{3,2,1,0:T(8,128)(2,1)S(1)}, bf16[2,256,8,128]{3,2,1,0:T(8,128)(2,1)}, u32[]{:S(2)}) copy-start(bf16[2,256,8,128]{3,2,1,0:T(8,128)(2,1)} %param.8) | copy-start | bytes 3145732
  69.4 2.5 %copy-start.2 = (bf16[2,8,128,256]{3,2,1,0:T(8,128)(2,1)S(1)}, bf16[2,8,128,256]{3,2,1,0:T(8,128)(2,1)}, u32[]{:S(2)}) copy-start(bf16[2,8,128,256]{3,2,1,0:T(8,128)(2,1)} %get-tuple-element.7) | copy-start | bytes 3145732
  72.0 1.5 %copy-start.3 = (f32[81,128]{1,0:T(8,128)S(1)}, f32[81,128]{1,0:T(8,128)}, u32[]{:S(2)}) copy-start(f32[81,128]{1,0:T(8,128)} %get-tuple-element.8) | copy-start | bytes 124420

commit v9 on v6

--- a/solution.py
+++ b/solution.py
@@ -30,14 +30,6 @@
     return pltpu.roll(x, shift % 256, 1, stride=1, stride_axis=0)
 
 
-def flip8(x):
-    idx = 7 - iota((8, 128), 0)
-    parts = [
-        jnp.take_along_axis(x[:, at : at + 128], idx, axis=0) for at in range(0, x.shape[1], 128)
-    ]
-    return parts[0] if len(parts) == 1 else jnp.concatenate(parts, axis=1)
-
-
 def activation(vol_dot):
     half = vol_dot * (1.0 / 32.0)
     q = 1.0 + jnp.tanh(half)
@@ -45,12 +37,13 @@
     return act, q + act * (2.0 - q)
 
 
-def cell_block(p, bb, rows_of, cur_ref):
+def cell_block(p, bb, rows_of, cur_ref, rev_ref):
     at = pl.multiple_of(bb * 16, 16)
     cur = cur_ref[p, :, pl.ds(at, 16), :].reshape(128, 256)
     rows = [rows_of(i, at) for i in range(8)]
     win = jnp.concatenate([r[0:16] for r in rows] + [r[8:24] for r in rows], axis=0)
-    return win, dot(cur, win, NT)
+    rev = rev_ref[p, :, pl.ds(at, 16), :].reshape(128, 256)
+    return win, dot(jnp.concatenate([cur, rev], axis=0), win, NT)
 
 
 def split_grads(grads):
@@ -61,19 +54,20 @@
     return jnp.concatenate(full, axis=0).astype(BF)
 
 
-def cells_early(p, bb, own, cur_ref, cot_ref, wk, sum_c, act_c, pre_c, sum_q):
-    win, vol = cell_block(p, bb, lambda i, at: own[i, pl.ds(at, 32), :], cur_ref)
+def cells_early(p, bb, own, cur_ref, rev_ref, cot_ref, wk, sum_c, act_c, pre_c, sum_q):
+    win, vol = cell_block(p, bb, lambda i, at: own[i, pl.ds(at, 32), :], cur_ref, rev_ref)
     at = pl.multiple_of(bb * 16, 16)
     pre = dot(cot_ref[p, :, pl.ds(at, 16), :].reshape(128, 128), wk)
     grads, acts, rest = [], [], []
     for i in range(16):
         y, odd = divmod(i, 2)
         rows = slice(8 * i, 8 * i + 8)
-        act, slope = activation(vol[rows, 128 * odd : 128 * odd + 128])
+        lanes = slice(128 * odd, 128 * odd + 128)
+        slope = activation(vol[rows, lanes])[1]
         piece = skew(pre[rows], 16 * y)
         grads.append(piece[:, :128] * slope)
         rest.append(piece[:, 128:])
-        acts.append(flip8(act))
+        acts.append(activation(vol[128 + 8 * i : 136 + 8 * i, lanes])[0])
     act_c[p, bb] = jnp.concatenate(acts, axis=0)
     pre_c[p, bb] = jnp.concatenate(rest, axis=0)
     grad = split_grads(grads)
@@ -87,25 +81,25 @@
         sum_q[p, i, pl.ds(at + 16, 8), :] = odd[8:]
 
 
-def cells_late(p, bb, dy, halo, cur_ref, cot_ref, sum_c, act_c, pre_c, out_ref, acc_ref):
+def cells_late(p, bb, dy, halo, cur_ref, rev_ref, cot_rev_ref, sum_c, act_c, pre_c, out_ref, acc_ref):
     def rows_of(i, at):
         return halo[i, pl.ds(at, 32), :]
 
-    win, vol = cell_block(p, bb, rows_of, cur_ref)
+    win, vol = cell_block(p, bb, rows_of, cur_ref, rev_ref)
     at = pl.multiple_of(bb * 16, 16)
-    cot = cot_ref[p, :, pl.ds(at, 16), :].reshape(128, 128).astype(F32)
-    cot_rev = jnp.concatenate([flip8(cot[8 * i : 8 * i + 8]) for i in range(16)], axis=0)
+    cot_rev = cot_rev_ref[p, :, pl.ds(at, 16), :].reshape(128, 128)
     act_own, pre = act_c[p, bb], pre_c[p, bb]
     grads, acts = [], []
     for i in range(16):
         y, odd = divmod(i, 2)
         rows = slice(8 * i, 8 * i + 8)
-        act, slope = activation(vol[rows, 128 * odd : 128 * odd + 128])
-        grads.append(pre[rows] * slope)
-        act = jnp.concatenate([act_own[rows], flip8(act)], axis=1)
+        lanes = slice(128 * odd, 128 * odd + 128)
+        grads.append(pre[rows] * activation(vol[rows, lanes])[1])
+        act = activation(vol[128 + 8 * i : 136 + 8 * i, lanes])[0]
+        act = jnp.concatenate([act_own[rows], act], axis=1)
         acts.append(skew(act, 249 - 16 * y))
     act = jnp.concatenate(acts, axis=0).astype(BF)
-    acc_ref[p] += dot(cot_rev.astype(BF), act, TN)
+    acc_ref[p] += dot(cot_rev, act, TN)
     out = sum_c[p, bb] + dot(split_grads(grads), win)
     out_ref[p, :, pl.ds(at, 16), :] = out.astype(BF).reshape(8, 16, 256)
 
@@ -156,7 +150,7 @@
     norm, shift_ref, prev_hbm, cur_hbm, cot_hbm, w_ref, e_ref, eye_ref,
     gc_hbm, gp_hbm, gw_ref,
     prev_in, cur_in, cot_in, gc_ref, gp_ref,
-    prev_ref, cur_ref, cot_ref, flat0, flat1, msg_r, rim_s, rim_r,
+    prev_ref, cur_ref, cot_ref, rev_ref, cot_rev, flat0, flat1, msg_r, rim_s, rim_r,
     edge_s, edge_r0, edge_r1, edge_cot_s, edge_cot_r, own0, own1, cot_x, own_pre, rim_cur, rim_cot,
     msg, tri_s, tri_r, halo0, halo1, pre_halo0, pre_halo1,
     sum_c, act_c, pre_c, sum_q, rim_sum, acc, ar0, ar1, ar2, ar3, ar4,
@@ -237,6 +231,8 @@
         def _():
             along(p, 1, k).start()
 
+    mirror = iota((128, 128), 0) // 8 * 8 + 7 - iota((128, 128), 0) % 8 == iota((128, 128), 1)
+    mirror = jnp.where(mirror, 1.0, 0.0).astype(BF)
     ident = jnp.where(iota((128, 128), 0) == iota((128, 128), 1), 1.0, 0.0).astype(BF)
 
     def spread_rows(flat, x):
@@ -269,15 +265,19 @@
             owns[p][y] = x[128:]
 
     def turn_cells(p):
-        both = jnp.concatenate([ident, aligner(4 - shift_ref[p, 1])], axis=0)
+        two = jnp.concatenate([ident, mirror], axis=0)
+        three = jnp.concatenate([ident, mirror, aligner(4 - shift_ref[p, 1])], axis=0)
         spread_rows(flat1, cur_in[p].astype(F32))
         for y in range(8):
-            cur_ref[p, y] = dot(ident, picked(flat1, y, 256), NT).astype(BF)
+            x = dot(two, picked(flat1, y, 256), NT).astype(BF)
+            cur_ref[p, y] = x[:128]
+            rev_ref[p, y] = x[128:]
         spread_rows(flat0, cot_in[p].astype(F32))
         for y in range(8):
-            x = dot(both, picked(flat0, y, 128), NT)
+            x = dot(three, picked(flat0, y, 128), NT)
             cot_ref[p, y] = x[:128].astype(BF)
-            cot_x[p, y] = x[128:]
+            cot_rev[p, y] = x[128:256].astype(BF)
+            cot_x[p, y] = x[256:]
 
     start = jnp.where(left, 112, 0)
 
@@ -436,14 +436,15 @@
         def work(i):
             for bb in (2 * i, 2 * i + 1):
                 cells_early(
-                    p, bb, owns[p], cur_ref, cot_ref, wks[p], sum_c, act_c, pre_c, sum_q)
+                    p, bb, owns[p], cur_ref, rev_ref, cot_ref, wks[p], sum_c, act_c, pre_c, sum_q)
 
         loop(0, 4, work)
         rim_positions(p, left, rim_cur, rim_cot, prev_ref, wks[p], masks, rim_sum)
 
     def late_cells(p, bb):
         cells_late(
-            p, bb, shift_ref[p, 0], halos[p], cur_ref, cot_ref, sum_c, act_c, pre_c, gc_ref, acc)
+            p, bb, shift_ref[p, 0], halos[p], cur_ref, rev_ref, cot_rev, sum_c, act_c, pre_c,
+            gc_ref, acc)
 
     def late_positions(p, bb):
         positions_late(
@@ -586,6 +587,7 @@
             v((2, 256, 8, 128), BF), v((2, 256, 8, 128), BF), v((2, 128, 8, 128), BF),
             v((2, 8, 128, 256), BF), v((2, 8, 128, 256), BF),
             v((2, 8, 128, 256), BF), v((2, 8, 128, 256), BF), v((2, 8, 128, 128), BF),
+            v((2, 8, 128, 256), BF), v((2, 8, 128, 128), BF),
             v((2048, 128), F32), v((2048, 128), F32),
             v((2, 2, 256, 8, 128), BF), v((2, 2, 4, 16, 256), BF), v((2, 2, 4, 16, 256), BF),
             v((2, 8, 16, 256), BF), v((8, 16, 256), BF), v((8, 16, 256), BF),

time: 71.1 us -> 71 us (level)
  no operation moved by 1% of the time
where the time goes in v9:
time: 71 us; the launch traced here: 70.8 us
  Pallas kernels  65.6 us (92%)
  local copies, waits for them, and re-layouts  4.6 us (6%)
    pallas_call x1, Pallas kernels, local(): pl.pallas_call(functools.partial(kernel, 1.0 / math.sqrt(total)), in_spec...  65.6 us
    unnamed x7, local copies, waits for them, and re-layouts  4.6 us

profile of v9, /device:TPU:1, one launch (start us, length us, event | category | flops | bytes accessed | tf_op | source)
XLA Modules:
  0.0 70.8 jit_solution(7726667699615653325)
XLA Ops:
  0.6 65.6 %shard_map.94 = (bf16[2,8,128,256]{3,2,1,0:T(8,128)(2,1)}, bf16[2,8,128,256]{3,2,1,0:T(8,128)(2,1)}, f32[81,128]{1,0:T(8,128)}) custom-call(s32[2,2]{1,0:T(2,128)} %shift_ref.1, bf16[2,256,8,128]{3,2,1,0:T(8,128)(2,1)} %prev_hbm.1, bf16[2,256,8,128]{3,2,1,0:T(8,128)(2,1)} %cur_hbm.1, bf16[2,128,8,128]{3,2,1,0:T(8,128)(2,1)} %cot_hbm.1, ...), custom_call_target="tpu_custom_call" | custom-call | flops 3000000000 | bytes 8388608 | tf_op jit(solution)/shard_map/pallas_call | solution.py:577
  66.2 0.0 copy-start
  66.2 2.5 %copy.10 = bf16[2,256,8,128]{3,2,1,0:T(8,128)(2,1)} copy(bf16[2,256,8,128]{1,3,2,0:T(8,128)(2,1)} %bitcast.5) | data formatting | bytes 2097152
  68.7 0.0 copy-done
  68.7 0.0 copy-start.1
  68.7 1.5 %copy.11 = bf16[2,256,8,128]{3,2,1,0:T(8,128)(2,1)} copy(bf16[2,256,8,128]{1,3,2,0:T(8,128)(2,1)S(1)} %bitcast.4) | data formatting | bytes 2097152
  70.2 0.0 copy-done.1
  70.2 0.6 copy.13
Async XLA Ops:
  66.2 2.5 %copy-start = (bf16[2,8,128,256]{3,2,1,0:T(8,128)(2,1)S(1)}, bf16[2,8,128,256]{3,2,1,0:T(8,128)(2,1)}, u32[]{:S(2)}) copy-start(bf16[2,8,128,256]{3,2,1,0:T(8,128)(2,1)} %get-tuple-element.7) | copy-start | bytes 3145732
  68.7 1.5 %copy-start.1 = (f32[81,128]{1,0:T(8,128)S(1)}, f32[81,128]{1,0:T(8,128)}, u32[]{:S(2)}) copy-start(f32[81,128]{1,0:T(8,128)} %get-tuple-element.8) | copy-start | bytes 124420

commit v10 on v9

--- a/solution.py
+++ b/solution.py
@@ -55,7 +55,7 @@
 
 
 def cells_early(p, bb, own, cur_ref, rev_ref, cot_ref, wk, sum_c, act_c, pre_c, sum_q):
-    win, vol = cell_block(p, bb, lambda i, at: own[i, pl.ds(at, 32), :], cur_ref, rev_ref)
+    win, vol = cell_block(p, bb, lambda i, at: own[p, i, pl.ds(at, 32), :], cur_ref, rev_ref)
     at = pl.multiple_of(bb * 16, 16)
     pre = dot(cot_ref[p, :, pl.ds(at, 16), :].reshape(128, 128), wk)
     grads, acts, rest = [], [], []
@@ -151,7 +151,7 @@
     gc_hbm, gp_hbm, gw_ref,
     prev_in, cur_in, cot_in, gc_ref, gp_ref,
     prev_ref, cur_ref, cot_ref, rev_ref, cot_rev, flat0, flat1, msg_r, rim_s, rim_r,
-    edge_s, edge_r0, edge_r1, edge_cot_s, edge_cot_r, own0, own1, cot_x, own_pre, rim_cur, rim_cot,
+    edge_s, edge_r0, edge_r1, edge_cot_s, edge_cot_r, own_all, wk_all, cot_x, own_pre, rim_cur, rim_cot,
     msg, tri_s, tri_r, halo0, halo1, pre_halo0, pre_halo1,
     sum_c, act_c, pre_c, sum_q, rim_sum, acc, ar0, ar1, ar2, ar3, ar4,
     side_ss, side_rs, row_ss, row_rs, s1, r1, s2, r2, s3, r3, s4, r4, load_sem, store_sem,
@@ -159,7 +159,7 @@
     row, col = lax.axis_index("row"), lax.axis_index("col")
     last = lax.axis_size("row") - 1
     left = col == 0
-    owns = (own0, own1)
+    owns = (own_all.at[0], own_all.at[1])
     halos, pre_halos = (halo0, halo1), (pre_halo0, pre_halo1)
     g1, g2, g3 = (row % 4) * 2 + col, (row // 4) % 4, row // 16
 
@@ -322,6 +322,8 @@
     wks = [pltpu.roll(wk, turns[p], 1).astype(BF) for p in range(2)]
     sub, lane = iota((8, 256), 0), iota((8, 256), 1) % 16
     masks = (jnp.where(lane >= 8 - sub, 1.0, 0.0), jnp.where(lane < 8 - sub, 1.0, 0.0))
+    for p in range(2):
+        wk_all[p] = wks[p]
     tri_lane = iota((WIDE, 128), 1)
     acc[...] = jnp.zeros_like(acc)
     sum_q[:, :, 0:8] = jnp.zeros((2, 8, 8, 256), F32)
@@ -432,14 +434,10 @@
 
         lax.fori_loop(lo, hi, body, 0)
 
-    def early(p):
-        def work(i):
-            for bb in (2 * i, 2 * i + 1):
-                cells_early(
-                    p, bb, owns[p], cur_ref, rev_ref, cot_ref, wks[p], sum_c, act_c, pre_c, sum_q)
-
-        loop(0, 4, work)
-        rim_positions(p, left, rim_cur, rim_cot, prev_ref, wks[p], masks, rim_sum)
+    def early(i):
+        p, bb = i // 8, i % 8
+        cells_early(
+            p, bb, own_all, cur_ref, rev_ref, cot_ref, wk_all[p], sum_c, act_c, pre_c, sum_q)
 
     def late_cells(p, bb):
         cells_late(
@@ -451,19 +449,19 @@
             p, bb, shift_ref[p, 1], left, halos[p], pre_halos[p], prev_ref, e_fold, masks,
             sum_q, rim_sum, gp_ref)
 
-    def late(i):
-        for bb in (2 * i, 2 * i + 1):
-            late_cells(0, bb)
-            late_positions(0, bb)
-
-    early(0)
-    early(1)
+    def late(bb):
+        late_cells(0, bb)
+        late_positions(0, bb)
+
+    loop(0, 16, early)
+    for p in range(2):
+        rim_positions(p, left, rim_cur, rim_cot, prev_ref, wks[p], masks, rim_sum)
     arrive(0)
-    loop(0, 4, late)
+    loop(0, 8, late)
     stores[0].start()
     stores[1].start()
     arrive(1)
-    loop(0, 2, lambda i: [late_cells(1, 4 * i + k) for k in range(4)])
+    loop(0, 8, lambda bb: late_cells(1, bb))
 
     stores[2].start()
 
@@ -510,7 +508,7 @@
         ).wait_recv()
 
     def some_positions(lo, hi):
-        loop(0, 1, lambda i: [late_positions(1, k) for k in range(lo, hi)])
+        loop(lo, hi, lambda bb: late_positions(1, bb))
 
     for d in range(1, 8):
         first(d).start()
@@ -592,7 +590,7 @@
             v((2, 2, 256, 8, 128), BF), v((2, 2, 4, 16, 256), BF), v((2, 2, 4, 16, 256), BF),
             v((2, 8, 16, 256), BF), v((8, 16, 256), BF), v((8, 16, 256), BF),
             v((2, 4, 16, 128), BF), v((2, 4, 16, 128), BF),
-            v((8, WIDE, 256), BF), v((8, WIDE, 256), BF),
+            v((2, 8, WIDE, 256), BF), v((2, 128, 256), BF),
             v((2, 8, WIDE, 128), F32), v((8, WIDE, 128), F32),
             v((2, 8, 8, 256), F32), v((2, 8, 8, 128), F32),
             v((2, 2, 256, 8, 128), BF),

time: 71 us -> 72.8 us (1.025)
  Pallas kernels: 65.6 us -> 67.4 us
    pallas_call x1, Pallas kernels: 65.6 us -> 67.4 us  [local(): pl.pallas_call(functools.partial(kernel, 1.0 / math.sqrt(total)), in_spec...]
where the time goes in v10:
time: 72.8 us; the launch traced here: 72.6 us
  Pallas kernels  67.4 us (93%)
  local copies, waits for them, and re-layouts  4.6 us (6%)
    pallas_call x1, Pallas kernels, local(): pl.pallas_call(functools.partial(kernel, 1.0 / math.sqrt(total)), in_spec...  67.4 us
    unnamed x7, local copies, waits for them, and re-layouts  4.6 us

profile of v10, /device:TPU:1, one launch (start us, length us, event | category | flops | bytes accessed | tf_op | source)
XLA Modules:
  0.0 72.6 jit_solution(8926949657119922765)
XLA Ops:
  0.6 67.4 %shard_map.94 = (bf16[2,8,128,256]{3,2,1,0:T(8,128)(2,1)}, bf16[2,8,128,256]{3,2,1,0:T(8,128)(2,1)}, f32[81,128]{1,0:T(8,128)}) custom-call(s32[2,2]{1,0:T(2,128)} %shift_ref.1, bf16[2,256,8,128]{3,2,1,0:T(8,128)(2,1)} %prev_hbm.1, bf16[2,256,8,128]{3,2,1,0:T(8,128)(2,1)} %cur_hbm.1, bf16[2,128,8,128]{3,2,1,0:T(8,128)(2,1)} %cot_hbm.1, ...), custom_call_target="tpu_custom_call" | custom-call | flops 3000000000 | bytes 8388608 | tf_op jit(solution)/shard_map/pallas_call | solution.py:575
  68.0 0.0 copy-start
  68.0 2.5 %copy.10 = bf16[2,256,8,128]{3,2,1,0:T(8,128)(2,1)} copy(bf16[2,256,8,128]{1,3,2,0:T(8,128)(2,1)} %bitcast.5) | data formatting | bytes 2097152
  70.5 0.0 copy-done
  70.6 0.0 copy-start.1
  70.6 1.5 %copy.11 = bf16[2,256,8,128]{3,2,1,0:T(8,128)(2,1)} copy(bf16[2,256,8,128]{1,3,2,0:T(8,128)(2,1)S(1)} %bitcast.4) | data formatting | bytes 2097152
  72.0 0.0 copy-done.1
  72.0 0.6 copy.13
Async XLA Ops:
  68.0 2.5 %copy-start = (bf16[2,8,128,256]{3,2,1,0:T(8,128)(2,1)S(1)}, bf16[2,8,128,256]{3,2,1,0:T(8,128)(2,1)}, u32[]{:S(2)}) copy-start(bf16[2,8,128,256]{3,2,1,0:T(8,128)(2,1)} %get-tuple-element.7) | copy-start | bytes 3145732
  70.6 1.5 %copy-start.1 = (f32[81,128]{1,0:T(8,128)S(1)}, f32[81,128]{1,0:T(8,128)}, u32[]{:S(2)}) copy-start(f32[81,128]{1,0:T(8,128)} %get-tuple-element.8) | copy-start | bytes 124420

commit v11 on v9

--- a/solution.py
+++ b/solution.py
@@ -434,11 +434,11 @@
 
     def early(p):
         def work(i):
-            for bb in (2 * i, 2 * i + 1):
+            for bb in [4 * i + k for k in range(4)]:
                 cells_early(
                     p, bb, owns[p], cur_ref, rev_ref, cot_ref, wks[p], sum_c, act_c, pre_c, sum_q)
 
-        loop(0, 4, work)
+        loop(0, 2, work)
         rim_positions(p, left, rim_cur, rim_cot, prev_ref, wks[p], masks, rim_sum)
 
     def late_cells(p, bb):
@@ -452,14 +452,14 @@
             sum_q, rim_sum, gp_ref)
 
     def late(i):
-        for bb in (2 * i, 2 * i + 1):
+        for bb in [4 * i + k for k in range(4)]:
             late_cells(0, bb)
             late_positions(0, bb)
 
     early(0)
     early(1)
     arrive(0)
-    loop(0, 4, late)
+    loop(0, 2, late)
     stores[0].start()
     stores[1].start()
     arrive(1)

time: 71 us -> 71 us (level)
  no operation moved by 1% of the time
where the time goes in v11:
time: 71 us; the launch traced here: 70.8 us
  Pallas kernels  65.6 us (92%)
  local copies, waits for them, and re-layouts  4.6 us (6%)
    pallas_call x1, Pallas kernels, local(): pl.pallas_call(functools.partial(kernel, 1.0 / math.sqrt(total)), in_spec...  65.6 us
    unnamed x7, local copies, waits for them, and re-layouts  4.6 us

profile of v11, /device:TPU:1, one launch (start us, length us, event | category | flops | bytes accessed | tf_op | source)
XLA Modules:
  0.0 70.8 jit_solution(3285602910273824882)
XLA Ops:
  0.6 65.6 %shard_map.94 = (bf16[2,8,128,256]{3,2,1,0:T(8,128)(2,1)}, bf16[2,8,128,256]{3,2,1,0:T(8,128)(2,1)}, f32[81,128]{1,0:T(8,128)}) custom-call(s32[2,2]{1,0:T(2,128)} %shift_ref.1, bf16[2,256,8,128]{3,2,1,0:T(8,128)(2,1)} %prev_hbm.1, bf16[2,256,8,128]{3,2,1,0:T(8,128)(2,1)} %cur_hbm.1, bf16[2,128,8,128]{3,2,1,0:T(8,128)(2,1)} %cot_hbm.1, ...), custom_call_target="tpu_custom_call" | custom-call | flops 3000000000 | bytes 8388608 | tf_op jit(solution)/shard_map/pallas_call | solution.py:577
  66.2 0.0 copy-start
  66.2 2.5 %copy.10 = bf16[2,256,8,128]{3,2,1,0:T(8,128)(2,1)} copy(bf16[2,256,8,128]{1,3,2,0:T(8,128)(2,1)} %bitcast.5) | data formatting | bytes 2097152
  68.7 0.0 copy-done
  68.7 0.0 copy-start.1
  68.7 1.5 %copy.11 = bf16[2,256,8,128]{3,2,1,0:T(8,128)(2,1)} copy(bf16[2,256,8,128]{1,3,2,0:T(8,128)(2,1)S(1)} %bitcast.4) | data formatting | bytes 2097152
  70.2 0.0 copy-done.1
  70.2 0.6 copy.13
Async XLA Ops:
  66.2 2.5 %copy-start = (bf16[2,8,128,256]{3,2,1,0:T(8,128)(2,1)S(1)}, bf16[2,8,128,256]{3,2,1,0:T(8,128)(2,1)}, u32[]{:S(2)}) copy-start(bf16[2,8,128,256]{3,2,1,0:T(8,128)(2,1)} %get-tuple-element.7) | copy-start | bytes 3145732
  68.7 1.5 %copy-start.1 = (f32[81,128]{1,0:T(8,128)S(1)}, f32[81,128]{1,0:T(8,128)}, u32[]{:S(2)}) copy-start(f32[81,128]{1,0:T(8,128)} %get-tuple-element.8) | copy-start | bytes 124420
